TPU v7x, 256 devices: a whole 4x4x8 slice. The times are simulated.
256 devices in a mesh: tm: 32 (over x_hi, z, core), space: 8 (over x_lo, y).
Axes of the slice: x: 4 (x_hi: 2, x_lo: 2; x = x_hi * 2 + x_lo), y: 4, z: 8, core: 2. Of those that a mesh axis runs over, the one named last changes fastest.
Arguments:
- iterate: float32 [32, 1024, 1024], P('tm', 'space'), may hold values from -6 to 6
- forcing: float32 [32, 1024, 1024], P('tm', 'space'), may hold values from -6 to 6
- initial: float32 [1024, 1024], P('space'), may hold values from -6 to 6
- levels: int32 [1024, 1024], P('space'), may hold values from 0 to 7
Outputs:
- increment: float32 [32, 1024, 1024], P('tm', 'space')
All inputs are finite; a program needn't handle non-finite values.
Results may differ from a plain program's by a relative error of at most 0.0003.
Values sent between devices are 32-bit elements; how exact they have to be, the bound alone decides.
No kernel may reach another device: no remote copies, remote signals or barrier semaphores. Data moves between devices by JAX's collectives and lax.ppermute only.
A program may use at most 64 MiB of HBM per device.

v0:
```python
import functools
import math

import jax
import jax.numpy as jnp
import ml_dtypes
import numpy as np
from jax import lax
from jax.experimental import pallas as pl
from jax.experimental.pallas import tpu as pltpu
from jax.sharding import PartitionSpec as P

TIME_STEP = 0.05
CIRCULANT_ALPHA = 0.1
MEAN_DAMPING = 5.25
DAMPING_TABLE = (0.5, 1.0, 1.5, 2.5, 4.0, 6.0, 8.0, 10.0)
GROUP = ("space", "tm")
VMEM = pl.BlockSpec(memory_space=pltpu.VMEM)
SMEM = pl.BlockSpec(memory_space=pltpu.SMEM)


def hartley_tables(length):
    positions = np.arange(length, dtype=np.int64)
    angle = (positions[:, None] * positions[None, :] % length) * (2.0 * math.pi / length)
    table = (np.cos(angle) + np.sin(angle)) / math.sqrt(length)
    high = table.astype(ml_dtypes.bfloat16)
    low = (table - high.astype(np.float64)).astype(ml_dtypes.bfloat16)
    return high, low


def pieces(block):
    high = block.astype(jnp.bfloat16)
    low = (block - high.astype(jnp.float32)).astype(jnp.bfloat16)
    return high, low


def product(a, b, dims):
    return lax.dot_general(a, b, (dims, ((), ())), preferred_element_type=jnp.float32)


def from_left(table_high, table_low, block, dims=((1,), (0,))):
    high, low = pieces(block)
    axis = 1 - dims[1][0]
    count = block.shape[axis]
    wide = product(table_high, jnp.concatenate([high, low], axis=axis), dims)
    return wide[:, :count] + wide[:, count:] + product(table_low, high, dims)


def from_right(block, table_high, table_low):
    high, low = pieces(block)
    count = block.shape[0]
    dims = ((1,), (0,))
    tall = product(jnp.concatenate([high, low], axis=0), table_high, dims)
    return tall[:count] + tall[count:] + product(high, table_low, dims)


def excess_of(levels):
    excess = jnp.full(levels.shape, -TIME_STEP * (DAMPING_TABLE[0] - MEAN_DAMPING), jnp.float32)
    for level_id in range(1, len(DAMPING_TABLE)):
        value = -TIME_STEP * (DAMPING_TABLE[level_id] - MEAN_DAMPING)
        excess = jnp.where(levels == level_id, value, excess)
    return excess


def roll(block, amount, axis):
    return pltpu.roll(block, amount % block.shape[axis], axis)


def source_kernel(steps, step_ref, x_ref, above_ref, below_ref, forcing_ref, initial_ref, levels_ref,
                  high_ref, low_ref, out_ref, source_ref):
    x = x_ref[...]
    rows, width = x.shape
    row = lax.broadcasted_iota(jnp.int32, (rows, width), 0)
    above, below = above_ref[...], below_ref[...]

    def neighbours(block, before, after):
        up = jnp.where(row == 0, before, roll(block, 1, 0))
        down = jnp.where(row == rows - 1, after, roll(block, -1, 0))
        return up, down, roll(block, 1, 1), roll(block, -1, 1)

    def sides(line):
        return roll(line, 1, 1) + roll(line, -1, 1)

    up, down, left, right = neighbours(x, above[1:2], below[0:1])
    grad_rows, grad_cols = down - up, right - left
    source_ref[...] = (
        excess_of(levels_ref[...]) * x
        + TIME_STEP * forcing_ref[...]
        - (TIME_STEP / 8.0) * (grad_rows * grad_rows + grad_cols * grad_cols)
    )

    @pl.when(step_ref[0] == 0)
    def _():
        source_ref[...] += initial_ref[...]

    @pl.when(step_ref[0] == steps - 1)
    def _():
        lap = up + down + left + right - 4.0 * x
        lap_above = above[0:1] + x[0:1] + sides(above)[1:2] - 4.0 * above[1:2]
        lap_below = x[rows - 1 : rows] + below[1:2] + sides(below)[0:1] - 4.0 * below[0:1]
        up2, down2, left2, right2 = neighbours(lap, lap_above, lap_below)
        lap_two = up2 + down2 + left2 + right2 - 4.0 * lap
        source_ref[...] -= x + TIME_STEP * (lap + lap_two + MEAN_DAMPING * x)

    out_ref[...] = from_left(high_ref[...], low_ref[...], source_ref[...], ((1,), (1,)))


def turned_kernel(steps, step_ref, x_ref, levels_ref, x_out, excess_out):
    keep = jnp.where(step_ref[0] == steps - 1, 0.0, 1.0)
    x_out[...] = (x_ref[...] * keep).T
    excess_out[...] = excess_of(levels_ref[...]).T


def solve_kernel(slabs, steps, x_ref, gain_ref, high_ref, low_ref, out_ref):
    rows = x_ref.shape[0] // slabs
    high, low = high_ref[...], low_ref[...]
    fields = jnp.concatenate([x_ref[pl.ds(s * rows, rows), :] for s in range(slabs)], axis=1)
    spectrum = from_right(fields, high, low)
    width = spectrum.shape[1]
    gain = gain_ref[...]
    comps = rows // steps
    pack = gain.shape[0]
    powers = [gain]
    while len(powers) < steps.bit_length():
        powers.append(powers[-1] * powers[-1])
    start = gain / (1.0 - CIRCULANT_ALPHA * powers[-1])
    groups = rows // pack
    u = spectrum.reshape(groups, pack, width) * start[None]
    lane_row = lax.broadcasted_iota(jnp.int32, (1, pack, width), 1)
    for j in range(steps.bit_length() - 1):
        shift = comps << j
        if shift < pack:
            moved = roll(u.reshape(rows, width), shift, 0).reshape(u.shape)
            head = jnp.where(lane_row < shift, CIRCULANT_ALPHA * moved[:1], moved[:1])
            moved = jnp.concatenate([head, moved[1:]], axis=0)
        else:
            k = shift // pack
            moved = jnp.concatenate([CIRCULANT_ALPHA * u[groups - k :], u[: groups - k]], axis=0)
        u = u + powers[j][None] * moved
    result = from_right(u.reshape(rows, width), high, low)
    for s in range(slabs):
        out_ref[pl.ds(s * rows, rows), :] = result[:, s * rows : (s + 1) * rows]


def sweep_kernel(y_ref, x_ref, excess_ref, high_ref, low_ref, out_ref, first_ref):
    high, low = high_ref[...], low_ref[...]
    first = from_left(high, low, y_ref[...]) - x_ref[...]
    first_ref[...] = first
    out_ref[...] = from_left(high, low, excess_ref[...] * first)


def finish_kernel(y_ref, first_ref, high_ref, low_ref, out_ref):
    out_ref[...] = (from_left(high_ref[...], low_ref[...], y_ref[...]) + first_ref[...]).T


def call(kernel, out_shapes, specs, scratch=(), flops=0, bytes_accessed=0):
    return pl.pallas_call(
        kernel,
        out_shape=out_shapes,
        in_specs=specs,
        out_specs=[VMEM] * len(out_shapes) if isinstance(out_shapes, (list, tuple)) else VMEM,
        scratch_shapes=list(scratch),
        compiler_params=pltpu.CompilerParams(vmem_limit_bytes=48 * 1024 * 1024),
        cost_estimate=pl.CostEstimate(flops=flops, bytes_accessed=bytes_accessed, transcendentals=0),
    )


def local(iterate, forcing, initial, levels):
    field = iterate[0]
    rows, width = field.shape
    steps, slabs = lax.axis_size("tm"), lax.axis_size("space")
    devices = steps * slabs
    comps = width // devices
    high, low = (jnp.asarray(t) for t in hartley_tables(width))
    step = lax.axis_index("tm").astype(jnp.int32).reshape(1)
    turned = jax.ShapeDtypeStruct((width, rows), jnp.float32)
    work = 6 * rows * width * width
    moved_bytes = 4 * width * width + 16 * rows * width

    ahead = [(i, (i + 1) % slabs) for i in range(slabs)]
    above = lax.ppermute(field[rows - 2 :], "space", ahead)
    below = lax.ppermute(field[:2], "space", [(j, i) for i, j in ahead])

    def exchange(block):
        return lax.all_to_all(
            block.reshape(devices, comps, rows), GROUP, split_axis=0, concat_axis=0, tiled=True
        ).reshape(width, rows)

    def waves(index):
        return 4.0 * jnp.sin(math.pi * index.astype(jnp.float32) / width) ** 2

    mine = lax.axis_index("space") * steps + lax.axis_index("tm")
    column = mine * comps + jnp.arange(8, dtype=jnp.int32) % comps
    modes = waves(column)[:, None] + waves(jnp.arange(width, dtype=jnp.int32))[None, :]
    gain = 1.0 / (1.0 + TIME_STEP * (modes * modes - modes + MEAN_DAMPING))

    sent = call(
        functools.partial(source_kernel, steps), turned, [SMEM] + [VMEM] * 8,
        scratch=[pltpu.VMEM((rows, width), jnp.float32)], flops=work, bytes_accessed=moved_bytes,
    )(step, field, above, below, forcing[0], initial, levels, high, low)
    kept, excess = call(
        functools.partial(turned_kernel, steps), [turned, turned], [SMEM, VMEM, VMEM],
        flops=16 * rows * width, bytes_accessed=16 * rows * width,
    )(step, field, levels)

    solve = call(
        functools.partial(solve_kernel, slabs, steps), turned, [VMEM] * 4,
        flops=2 * work, bytes_accessed=moved_bytes,
    )
    back = exchange(solve(exchange(sent), gain, high, low))
    error, first = call(
        sweep_kernel, [turned, turned], [VMEM] * 5, flops=2 * work, bytes_accessed=moved_bytes
    )(back, kept, excess, high, low)
    last = exchange(solve(exchange(error), gain, high, low))
    increment = call(
        finish_kernel, jax.ShapeDtypeStruct((rows, width), jnp.float32), [VMEM] * 4,
        flops=work, bytes_accessed=moved_bytes,
    )(last, first, high, low)
    return increment[None]


def solution(mesh):
    placed = (P("tm", "space", None), P("tm", "space", None), P("space", None), P("space", None))
    return jax.shard_map(
        local, mesh=mesh, in_specs=placed, out_specs=P("tm", "space", None), check_vma=False
    )
```

profile of v0, /device:TPU:1, one launch (start us, length us, event | category | flops | bytes accessed | tf_op | source)
XLA Modules:
  0.0 152.5 jit_solution(15434902637553129048)
XLA Ops:
  0.0 0.8 slice_bitcast_fusion
  0.8 4.6 %collective-permute-start.1 = (f32[2,1024]{1,0:T(2,128)S(1)}, f32[2,1024]{1,0:T(2,128)S(1)}, u32[]{:S(2)}, u32[]{:S(2)}) collective-permute-start(f32[2,1024]{1,0:T(2,128)S(1)} %get-tuple-element.13), channel_id=1, source_target_pairs={{1,0},{2,1},{3,2},{4,3},{5,4},{6,5},{7,6},{0,7},{9,8},{10,9},{11,1... | collective-permute-start | bytes 24584 | tf_op jit(solution)/shard_map/ppermute | solution.py:182
  5.3 0.0 collective-permute-start
  5.3 0.8 collective-permute-done.1.below_ref
  6.1 3.8 %collective-permute-done.above_ref = f32[2,1024]{1,0:T(2,128)S(1)} collective-permute-done((f32[2,1024]{1,0:T(2,128)S(1)}, f32[2,1024]{1,0:T(2,128)S(1)}, u32[]{:S(2)}, u32[]{:S(2)}) %collective-permute-start) | collective-permute-done | bytes 8224 | tf_op jit(solution)/shard_map/ppermute | solution.py:181
  9.9 0.0 copy-start.2
  10.0 1.6 %copy-done.2 = bf16[1024,1024]{1,0:T(8,128)(2,1)S(1)} copy-done((bf16[1024,1024]{1,0:T(8,128)(2,1)S(1)}, bf16[1024,1024]{1,0:T(8,128)(2,1)}, u32[]{:S(2)}) %copy-start.2) | copy-done | bytes 2097176
  11.5 0.0 copy-start.5
  11.5 1.0 copy-done.5
  12.6 0.0 copy-start.7
  12.6 1.0 copy-done.7
  13.6 0.0 copy-start.12
  13.6 1.0 copy-done.12
  14.7 0.0 copy-start.13
  14.7 1.0 copy-done.13
  15.7 0.0 copy-start
  15.7 4.5 %shard_map.64 = f32[1024,128]{1,0:T(8,128)} custom-call(s32[1]{0:T(128)} %bitcast.step_ref, f32[128,1024]{1,0:T(8,128)S(1)} %bitcast.16, f32[2,1024]{1,0:T(2,128)S(1)} %collective-permute-done.above_ref, f32[2,1024]{1,0:T(2,128)S(1)} %collective-permute-done.1.below_ref, f32[128,1024]{1,0:T(8,128)S(1)} %bitcast.24, f32[128,1024]{1,0:T(8,128)S(1)} %copy-done.13, ...), custom_call_target="tpu_custom_call" | custom-call | flops 805306368 | bytes 6291456 | tf_op jit(solution)/shard_map/pallas_call | solution.py:197
  20.2 13.3 %all-to-all-start = ((f32[256,4,128]{2,1,0:T(4,128)}), f32[256,4,128]{2,1,0:T(4,128)S(1)}, u32[]{:S(2)}, u32[]{:S(2)}) async-start(f32[256,4,128]{2,1,0:T(4,128)} %bitcast.5), calls=%async_computation | async-start | bytes 1048576 | tf_op jit(solution)/shard_map/all_to_all | solution.py:185
  33.7 0.1 fusion.3.gain_ref
  33.8 20.2 %all-to-all-done = f32[256,4,128]{2,1,0:T(4,128)S(1)} async-done(((f32[256,4,128]{2,1,0:T(4,128)}), f32[256,4,128]{2,1,0:T(4,128)S(1)}, u32[]{:S(2)}, u32[]{:S(2)}) %all-to-all-start) | async-done | bytes 524320 | tf_op jit(solution)/shard_map/all_to_all | solution.py:185
  54.0 0.0 copy-start.9
  54.0 0.8 copy-done.9
  54.8 0.0 copy-done
  54.8 0.0 copy-start.3
  54.8 1.6 %copy-done.3 = bf16[1024,1024]{1,0:T(8,128)(2,1)S(1)} copy-done((bf16[1024,1024]{1,0:T(8,128)(2,1)S(1)}, bf16[1024,1024]{1,0:T(8,128)(2,1)}, u32[]{:S(2)}) %copy-start.3) | copy-done | bytes 2097176
  56.4 0.0 copy-start.10
  56.4 1.0 copy-done.10
  57.4 0.0 copy-start.6
  57.4 0.0 copy-start.8
  57.4 1.9 %shard_map.65 = f32[1024,128]{1,0:T(8,128)S(1)} custom-call(f32[1024,128]{1,0:T(8,128)S(1)} %bitcast.19, f32[8,1024]{1,0:T(8,128)S(1)} %fusion.3.gain_ref, bf16[1024,1024]{1,0:T(8,128)(2,1)S(1)} %copy-done.3, bf16[1024,1024]{1,0:T(8,128)(2,1)S(1)} %copy-done), custom_call_target="tpu_custom_call" | custom-call | flops 1610612736 | bytes 6291456 | tf_op jit(solution)/shard_map/pallas_call | solution.py:210
  59.4 0.0 copy-start.11
  59.4 0.8 copy-done.11
  60.2 0.0 copy-start.4
  60.2 8.3 %all-to-all-start.1 = ((f32[256,4,128]{2,1,0:T(4,128)}), f32[256,4,128]{2,1,0:T(4,128)}, u32[]{:S(2)}, u32[]{:S(2)}) async-start(f32[256,4,128]{2,1,0:T(4,128)} %bitcast.20), calls=%async_computation.1 | async-start | bytes 1048576 | tf_op jit(solution)/shard_map/all_to_all | solution.py:185
  68.5 0.0 copy-done.6
  68.5 0.0 copy-done.8
  68.5 0.4 shard_map.66
  68.9 0.0 copy-start.14
  68.9 0.8 copy-done.14
  69.7 0.0 copy-start.16
  69.7 0.8 copy-done.16
  70.5 17.7 %all-to-all-done.1 = f32[256,4,128]{2,1,0:T(4,128)} async-done(((f32[256,4,128]{2,1,0:T(4,128)}), f32[256,4,128]{2,1,0:T(4,128)}, u32[]{:S(2)}, u32[]{:S(2)}) %all-to-all-start.1) | async-done | bytes 524320 | tf_op jit(solution)/shard_map/all_to_all | solution.py:185
  88.2 0.0 copy-done.4
  88.2 0.0 copy-start.15
  88.2 1.0 copy-done.15
  89.2 0.0 copy-start.17
  89.2 1.0 copy-done.17
  90.3 0.0 copy-start.1
  90.3 4.2 %shard_map.67 = (f32[1024,128]{1,0:T(8,128)S(1)}, f32[1024,128]{1,0:T(8,128)S(1)}) custom-call(f32[1024,128]{1,0:T(8,128)} %bitcast.8.y_ref, f32[1024,128]{1,0:T(8,128)S(1)} %copy-done.15, f32[1024,128]{1,0:T(8,128)S(1)} %copy-done.17, bf16[1024,1024]{1,0:T(8,128)(2,1)S(1)} %copy-done.4, bf16[1024,1024]{1,0:T(8,128)(2,1)} %constant.50.clone.low_ref), custom_call_target="tpu_custom_call" | custom-call | flops 1610612736 | bytes 6291456 | tf_op jit(solution)/shard_map/pallas_call | solution.py:211
  94.5 27.1 %all_to_all.20 = f32[256,4,128]{2,1,0:T(4,128)S(1)} all-to-all(f32[256,4,128]{2,1,0:T(4,128)S(1)} %bitcast.21), channel_id=1, replica_groups=mesh['tm'=32,'space'=8] {'space','tm'}, dimensions={0} | all-to-all | bytes 1048576 | tf_op jit(solution)/shard_map/all_to_all | solution.py:185
  121.6 0.0 copy-done.1
  121.6 1.9 %shard_map.68 = f32[1024,128]{1,0:T(8,128)S(1)} custom-call(f32[1024,128]{1,0:T(8,128)S(1)} %bitcast.22, f32[8,1024]{1,0:T(8,128)S(1)} %fusion.3.gain_ref, bf16[1024,1024]{1,0:T(8,128)(2,1)S(1)} %copy-done.4, bf16[1024,1024]{1,0:T(8,128)(2,1)S(1)} %copy-done.1), custom_call_target="tpu_custom_call" | custom-call | flops 1610612736 | bytes 6291456 | tf_op jit(solution)/shard_map/pallas_call | solution.py:214
  123.5 26.9 %all_to_all.21 = f32[256,4,128]{2,1,0:T(4,128)S(1)} all-to-all(f32[256,4,128]{2,1,0:T(4,128)S(1)} %bitcast.23), channel_id=1, replica_groups=mesh['tm'=32,'space'=8] {'space','tm'}, dimensions={0} | all-to-all | bytes 1048576 | tf_op jit(solution)/shard_map/all_to_all | solution.py:185
  150.4 2.1 %shard_map.69 = f32[128,1024]{1,0:T(8,128)} custom-call(f32[1024,128]{1,0:T(8,128)S(1)} %bitcast.18, f32[1024,128]{1,0:T(8,128)S(1)} %get-tuple-element.12.first_ref, bf16[1024,1024]{1,0:T(8,128)(2,1)S(1)} %copy-done.4, bf16[1024,1024]{1,0:T(8,128)(2,1)S(1)} %copy-done.1), custom_call_target="tpu_custom_call" | custom-call | flops 805306368 | bytes 6291456 | tf_op jit(solution)/shard_map/pallas_call | solution.py:215
  (2 shorter events, 0.1 us)
Async XLA Ops:
  0.8 5.3 %collective-permute-start.1 = (f32[2,1024]{1,0:T(2,128)S(1)}, f32[2,1024]{1,0:T(2,128)S(1)}, u32[]{:S(2)}, u32[]{:S(2)}) collective-permute-start(f32[2,1024]{1,0:T(2,128)S(1)} %get-tuple-element.13), channel_id=1, source_target_pairs={{1,0},{2,1},{3,2},{4,3},{5,4},{6,5},{7,6},{0,7},{9,8},{10,9},{11,1... | collective-permute-start | bytes 24584 | tf_op jit(solution)/shard_map/ppermute | solution.py:182
  5.3 4.6 %collective-permute-start = (f32[2,1024]{1,0:T(2,128)S(1)}, f32[2,1024]{1,0:T(2,128)S(1)}, u32[]{:S(2)}, u32[]{:S(2)}) collective-permute-start(f32[2,1024]{1,0:T(2,128)S(1)} %get-tuple-element.14), channel_id=1, source_target_pairs={{0,1},{1,2},{2,3},{3,4},{4,5},{5,6},{6,7},{7,0},{8,9},{9,10},{10,1... | collective-permute-start | bytes 24584 | tf_op jit(solution)/shard_map/ppermute | solution.py:181
  9.9 1.6 %copy-start.2 = (bf16[1024,1024]{1,0:T(8,128)(2,1)S(1)}, bf16[1024,1024]{1,0:T(8,128)(2,1)}, u32[]{:S(2)}) copy-start(bf16[1024,1024]{1,0:T(8,128)(2,1)} %constant.49.clone.high_ref) | copy-start | bytes 6291460
  11.5 1.0 copy-start.5
  12.6 1.0 copy-start.7
  13.6 1.0 copy-start.12
  14.7 1.0 copy-start.13
  15.7 39.1 %copy-start = (bf16[1024,1024]{1,0:T(8,128)(2,1)S(1)}, bf16[1024,1024]{1,0:T(8,128)(2,1)}, u32[]{:S(2)}) copy-start(bf16[1024,1024]{1,0:T(8,128)(2,1)} %constant.50.clone.low_ref) | copy-start | bytes 6291460
  20.2 33.8 %all-to-all-start = ((f32[256,4,128]{2,1,0:T(4,128)}), f32[256,4,128]{2,1,0:T(4,128)S(1)}, u32[]{:S(2)}, u32[]{:S(2)}) async-start(f32[256,4,128]{2,1,0:T(4,128)} %bitcast.5), calls=%async_computation | async-start | bytes 1048576 | tf_op jit(solution)/shard_map/all_to_all | solution.py:185
  54.0 0.8 copy-start.9
  54.8 1.6 %copy-start.3 = (bf16[1024,1024]{1,0:T(8,128)(2,1)S(1)}, bf16[1024,1024]{1,0:T(8,128)(2,1)}, u32[]{:S(2)}) copy-start(bf16[1024,1024]{1,0:T(8,128)(2,1)} %constant.49.clone.high_ref) | copy-start | bytes 6291460
  56.4 1.0 copy-start.10
  57.4 11.1 %copy-start.6 = (f32[1,128,1024]{2,1,0:T(8,128)S(1)}, f32[1,128,1024]{2,1,0:T(8,128)}, u32[]{:S(2)}) copy-start(f32[1,128,1024]{2,1,0:T(8,128)} %param.6) | copy-start | bytes 1572868
  57.4 11.1 %copy-start.8 = (s32[128,1024]{1,0:T(8,128)S(1)}, s32[128,1024]{1,0:T(8,128)}, u32[]{:S(2)}) copy-start(s32[128,1024]{1,0:T(8,128)} %levels_ref.3) | copy-start | bytes 1572868
  59.4 0.8 copy-start.11
  60.2 28.0 %copy-start.4 = (bf16[1024,1024]{1,0:T(8,128)(2,1)S(1)}, bf16[1024,1024]{1,0:T(8,128)(2,1)}, u32[]{:S(2)}) copy-start(bf16[1024,1024]{1,0:T(8,128)(2,1)} %constant.49.clone.high_ref) | copy-start | bytes 6291460
  60.2 28.0 %all-to-all-start.1 = ((f32[256,4,128]{2,1,0:T(4,128)}), f32[256,4,128]{2,1,0:T(4,128)}, u32[]{:S(2)}, u32[]{:S(2)}) async-start(f32[256,4,128]{2,1,0:T(4,128)} %bitcast.20), calls=%async_computation.1 | async-start | bytes 1048576 | tf_op jit(solution)/shard_map/all_to_all | solution.py:185
  68.9 0.8 copy-start.14
  69.7 0.8 copy-start.16
  88.2 1.0 copy-start.15
  89.2 1.0 copy-start.17
  90.3 31.3 %copy-start.1 = (bf16[1024,1024]{1,0:T(8,128)(2,1)S(1)}, bf16[1024,1024]{1,0:T(8,128)(2,1)}, u32[]{:S(2)}) copy-start(bf16[1024,1024]{1,0:T(8,128)(2,1)} %constant.50.clone.low_ref) | copy-start | bytes 6291460
where the time goes:
time: 153 us
  blocking collectives  53.9 us (35%)
  waiting for transfers between devices  42.5 us (28%)
  starting transfers between devices  26.2 us (17%)
  Pallas kernels  15.1 us (10%)
  local copies, waits for them, and re-layouts  14.5 us (9%)
    all_to_all x2, blocking collectives, exchange(): lax.all_to_all(block.reshape(devices, comps, rows), GROUP, split_axis=0,...  53.9 us
    all_to_all x2, waiting for transfers between devices, exchange(): lax.all_to_all(block.reshape(devices, comps, rows), GROUP, split_axis=0,...  37.9 us
    all_to_all x2, starting transfers between devices, exchange(): lax.all_to_all(block.reshape(devices, comps, rows), GROUP, split_axis=0,...  21.7 us
    unnamed x36, local copies, waits for them, and re-layouts  13.7 us
    ppermute x1, starting transfers between devices, local(): below = lax.ppermute(field[:2], 'space', [(j, i) for i, j in ahead])  4.55 us
    pallas_call x1, Pallas kernels, local(): call(functools.partial(source_kernel, steps), turned, [SMEM] + [VMEM] * 8...  4.5 us
    pallas_call x1, Pallas kernels, local(): call(sweep_kernel, [turned, turned], [VMEM] * 5, flops=2 * work, bytes_ac...  4.24 us
    ppermute x1, waiting for transfers between devices, local(): above = lax.ppermute(field[rows - 2:], 'space', ahead)  3.82 us
  transfers between devices with their start and end apart: 4, of which 4 were waited for; matrix products, arithmetic and copies ran while one was open for 0% of the time, Pallas kernels for 0%

commit v1 on v0

v1 whole, which is shorter than its diff:
```python
import functools
import math

import jax
import jax.numpy as jnp
import ml_dtypes
import numpy as np
from jax import lax
from jax.experimental import pallas as pl
from jax.experimental.pallas import tpu as pltpu
from jax.sharding import PartitionSpec as P

TIME_STEP = 0.05
CIRCULANT_ALPHA = 0.1
MEAN_DAMPING = 5.25
DAMPING_TABLE = (0.5, 1.0, 1.5, 2.5, 4.0, 6.0, 8.0, 10.0)
AXES = {"xh": 2, "z": 8, "c": 2, "xl": 2, "y": 4}
TIME = ("xh", "z", "c")
SLAB = ("xl", "y")
GROUP = ("xl", "y", "z", "c", "xh")
VMEM = pl.BlockSpec(memory_space=pltpu.VMEM)
SMEM = pl.BlockSpec(memory_space=pltpu.SMEM)
HBM = pl.BlockSpec(memory_space=pltpu.HBM)


def hartley_tables(length):
    positions = np.arange(length, dtype=np.int64)
    angle = (positions[:, None] * positions[None, :] % length) * (2.0 * math.pi / length)
    table = (np.cos(angle) + np.sin(angle)) / math.sqrt(length)
    high = table.astype(ml_dtypes.bfloat16)
    low = (table - high.astype(np.float64)).astype(ml_dtypes.bfloat16)
    return high, low


def pieces(block):
    high = block.astype(jnp.bfloat16)
    low = (block - high.astype(jnp.float32)).astype(jnp.bfloat16)
    return high, low


def product(a, b, dims):
    return lax.dot_general(a, b, (dims, ((), ())), preferred_element_type=jnp.float32)


def from_right(block, table_high, table_low):
    high, low = pieces(block)
    count = block.shape[0]
    dims = ((1,), (0,))
    tall = product(jnp.concatenate([high, low], axis=0), table_high, dims)
    return tall[:count] + tall[count:] + product(high, table_low, dims)


def excess_of(levels):
    excess = jnp.full(levels.shape, -TIME_STEP * (DAMPING_TABLE[0] - MEAN_DAMPING), jnp.float32)
    for level_id in range(1, len(DAMPING_TABLE)):
        value = -TIME_STEP * (DAMPING_TABLE[level_id] - MEAN_DAMPING)
        excess = jnp.where(levels == level_id, value, excess)
    return excess


def roll(block, amount, axis):
    return pltpu.roll(block, amount % block.shape[axis], axis)


def load_kernel(step_ref, x_hbm, forcing_hbm, initial_hbm, levels_hbm, high_hbm, low_hbm,
                x_ref, base_ref, excess_ref, high_ref, low_ref,
                forcing_ref, initial_ref, levels_ref, sems):
    pairs = [(x_hbm, x_ref), (levels_hbm, levels_ref), (forcing_hbm, forcing_ref),
             (initial_hbm, initial_ref), (high_hbm, high_ref), (low_hbm, low_ref)]
    copies = [pltpu.make_async_copy(a, b, sems.at[i]) for i, (a, b) in enumerate(pairs)]
    for copy in copies:
        copy.start()
    copies[0].wait()
    copies[1].wait()
    x = x_ref[...]
    excess = excess_of(levels_ref[...])
    excess_ref[...] = excess
    grad_cols = roll(x, -1, 1) - roll(x, 1, 1)
    copies[2].wait()
    base_ref[...] = (
        excess * x + TIME_STEP * forcing_ref[...] - (TIME_STEP / 8.0) * (grad_cols * grad_cols)
    )
    copies[3].wait()

    @pl.when(step_ref[0] == 0)
    def _():
        base_ref[...] += initial_ref[...]

    copies[4].wait()
    copies[5].wait()


def source_kernel(steps, step_ref, x_ref, above_ref, below_ref, base_ref, high_ref, low_ref,
                  out_ref, source_ref):
    x = x_ref[...]
    rows, width = x.shape
    row = lax.broadcasted_iota(jnp.int32, (rows, width), 0)
    above, below = above_ref[...], below_ref[...]

    def neighbours(block, before, after):
        up = jnp.where(row == 0, before, roll(block, 1, 0))
        down = jnp.where(row == rows - 1, after, roll(block, -1, 0))
        return up, down

    def sides(line):
        return roll(line, 1, 1) + roll(line, -1, 1)

    up, down = neighbours(x, above[1:2], below[0:1])
    grad_rows = down - up
    source_ref[...] = base_ref[...] - (TIME_STEP / 8.0) * (grad_rows * grad_rows)

    @pl.when(step_ref[0] == steps - 1)
    def _():
        lap = up + down + sides(x) - 4.0 * x
        lap_above = above[0:1] + x[0:1] + sides(above)[1:2] - 4.0 * above[1:2]
        lap_below = x[rows - 1 : rows] + below[1:2] + sides(below)[0:1] - 4.0 * below[0:1]
        up2, down2 = neighbours(lap, lap_above, lap_below)
        lap_two = up2 + down2 + sides(lap) - 4.0 * lap
        source_ref[...] -= x + TIME_STEP * (lap + lap_two + MEAN_DAMPING * x)

    out_ref[...] = from_right(source_ref[...], high_ref[...], low_ref[...]).T


def solve_kernel(slabs, steps, x_ref, gain_ref, high_ref, low_ref, out_ref):
    rows = x_ref.shape[0] // slabs
    high, low = high_ref[...], low_ref[...]
    fields = jnp.concatenate([x_ref[pl.ds(s * rows, rows), :] for s in range(slabs)], axis=1)
    spectrum = from_right(fields, high, low)
    width = spectrum.shape[1]
    gain = gain_ref[...]
    powers = [gain]
    while len(powers) < steps.bit_length():
        powers.append(powers[-1] * powers[-1])
    start = gain / (1.0 - CIRCULANT_ALPHA * powers[-1])
    pack = gain.shape[0]
    half = pack // 2
    groups = rows // pack
    lane_row = lax.broadcasted_iota(jnp.int32, (1, pack, width), 1)
    u = spectrum.reshape(groups, pack, width) * start[None]

    def around(block):
        turned = roll(block.reshape(-1, width), half, 0).reshape(block.shape)
        if block.shape[0] > 1:
            other = roll(block.reshape(-1, width), -half, 0).reshape(block.shape)
            turned = jnp.where(lane_row < half, other, turned)
        return jnp.where(lane_row < half, CIRCULANT_ALPHA, 1.0) * turned

    for j in range(steps.bit_length() - 1):
        k = 1 << j
        if k < groups:
            moved = jnp.concatenate([around(u[groups - k :]), u[: groups - k]], axis=0)
        else:
            moved = around(u)
        u = u + powers[j][None] * moved
    result = from_right(u.reshape(rows, width), high, low)
    for s in range(slabs):
        out_ref[pl.ds(s * rows, rows), :] = result[:, s * rows : (s + 1) * rows]


def sweep_kernel(steps, step_ref, y_ref, x_ref, excess_ref, high_ref, low_ref, out_ref, first_ref):
    high, low = high_ref[...], low_ref[...]
    keep = jnp.where(step_ref[0] == steps - 1, 0.0, 1.0)
    first = from_right(y_ref[...].T, high, low) - keep * x_ref[...]
    first_ref[...] = first
    out_ref[...] = from_right(excess_ref[...] * first, high, low).T


def finish_kernel(y_ref, first_ref, high_ref, low_ref, out_ref):
    out_ref[...] = from_right(y_ref[...].T, high_ref[...], low_ref[...]) + first_ref[...]


def call(kernel, out_shapes, specs, scratch=(), flops=0, bytes_accessed=0):
    return pl.pallas_call(
        kernel,
        out_shape=out_shapes,
        in_specs=specs,
        out_specs=[VMEM] * len(out_shapes) if isinstance(out_shapes, (list, tuple)) else VMEM,
        scratch_shapes=list(scratch),
        compiler_params=pltpu.CompilerParams(vmem_limit_bytes=16 * 1024 * 1024),
        cost_estimate=pl.CostEstimate(flops=flops, bytes_accessed=bytes_accessed, transcendentals=0),
    )


def local(iterate, forcing, initial, levels):
    field = iterate[0]
    rows, width = field.shape
    steps, slabs = lax.axis_size(TIME), lax.axis_size(SLAB)
    devices = steps * slabs
    comps = width // devices
    high, low = (jnp.asarray(t) for t in hartley_tables(width))
    step = lax.axis_index(TIME).astype(jnp.int32).reshape(1)
    plane = jax.ShapeDtypeStruct((rows, width), jnp.float32)
    turned = jax.ShapeDtypeStruct((width, rows), jnp.float32)
    table = jax.ShapeDtypeStruct((width, width), jnp.bfloat16)
    work = 6 * rows * width * width
    moved_bytes = 4 * width * width + 16 * rows * width

    ahead = [(i, (i + 1) % slabs) for i in range(slabs)]
    above = lax.ppermute(field[rows - 2 :], SLAB, ahead)
    below = lax.ppermute(field[:2], SLAB, [(j, i) for i, j in ahead])

    def exchange(block):
        return lax.all_to_all(
            block.reshape(devices, comps, rows), GROUP, split_axis=0, concat_axis=0, tiled=True
        ).reshape(width, rows)

    def waves(index):
        return 4.0 * jnp.sin(math.pi * index.astype(jnp.float32) / width) ** 2

    column = lax.axis_index(GROUP) * comps + jnp.arange(2 * comps, dtype=jnp.int32) % comps
    modes = waves(column)[:, None] + waves(jnp.arange(width, dtype=jnp.int32))[None, :]
    gain = 1.0 / (1.0 + TIME_STEP * (modes * modes - modes + MEAN_DAMPING))

    field, base, excess, high, low = call(
        load_kernel, [plane, plane, plane, table, table], [SMEM] + [HBM] * 6,
        scratch=[pltpu.VMEM((rows, width), jnp.float32), pltpu.VMEM((rows, width), jnp.float32),
                 pltpu.VMEM((rows, width), jnp.int32), pltpu.SemaphoreType.DMA((6,))],
        flops=32 * rows * width, bytes_accessed=moved_bytes,
    )(step, field, forcing[0], initial, levels, high, low)
    sent = call(
        functools.partial(source_kernel, steps), turned, [SMEM] + [VMEM] * 6,
        scratch=[pltpu.VMEM((rows, width), jnp.float32)], flops=work, bytes_accessed=moved_bytes,
    )(step, field, above, below, base, high, low)
    solve = call(
        functools.partial(solve_kernel, slabs, steps), turned, [VMEM] * 4,
        flops=2 * work, bytes_accessed=moved_bytes,
    )
    back = exchange(solve(exchange(sent), gain, high, low))
    error, first = call(
        functools.partial(sweep_kernel, steps), [turned, plane], [SMEM] + [VMEM] * 5,
        flops=2 * work, bytes_accessed=moved_bytes,
    )(step, back, field, excess, high, low)
    last = exchange(solve(exchange(error), gain, high, low))
    increment = call(
        finish_kernel, plane, [VMEM] * 4, flops=work, bytes_accessed=moved_bytes
    )(last, first, high, low)
    return increment[None]


def solution(mesh):
    fine = jax.sharding.Mesh(mesh.devices.reshape(tuple(AXES.values())), tuple(AXES))
    placed = (P(TIME, SLAB, None), P(TIME, SLAB, None), P(SLAB, None), P(SLAB, None))
    return jax.shard_map(
        local, mesh=fine, in_specs=placed, out_specs=P(TIME, SLAB, None), check_vma=False
    )
```

time: 153 us -> 139 us (0.908)
  blocking collectives: 53.9 us -> 77.1 us
  waiting for transfers between devices: 42.5 us -> 20.4 us
  starting transfers between devices: 26.2 us -> 19.7 us
  local copies, waits for them, and re-layouts: 14.5 us -> 9.73 us
  Pallas kernels: 15.1 us -> 11.4 us
    all_to_all x2 -> x3, blocking collectives: 53.9 us -> 77.1 us  [exchange(): lax.all_to_all(block.reshape(devices, comps, rows), GROUP, split_axis=0,...]
    all_to_all x2 -> x1, waiting for transfers between devices: 37.9 us -> 20.4 us  [exchange(): lax.all_to_all(block.reshape(devices, comps, rows), GROUP, split_axis=0,...]
    all_to_all x2 -> x1, starting transfers between devices: 21.7 us -> 15.1 us  [exchange(): lax.all_to_all(block.reshape(devices, comps, rows), GROUP, split_axis=0,...]
    unnamed x36 -> x22, local copies, waits for them, and re-layouts: 13.7 us -> 8.95 us
    ppermute x2, waiting for transfers between devices: 4.61 us -> 0.01 us  [the longest x1 0.01 us: local(): below = lax.ppermute(field[:2], SLAB, [(j, i) for i, j in ahead])]
    pallas_call x4, Pallas kernels: 11.3 us -> 7.3 us  [the longest x1 2.07 us: local(): call(functools.partial(source_kernel, steps), turned, [SMEM] + [VMEM] * 6...]
  transfers between devices with their start and end apart: 4 -> 3, of which waited for: 4 -> 1; matrix products, arithmetic and copies ran while one was open for 0% -> 0% of each run, Pallas kernels for 0% -> 1%
where the time goes in v1:
time: 139 us
  blocking collectives  77.1 us (55%)
  waiting for transfers between devices  20.4 us (15%)
  starting transfers between devices  19.7 us (14%)
  Pallas kernels  11.4 us (8%)
  local copies, waits for them, and re-layouts  9.73 us (7%)
    all_to_all x3, blocking collectives, exchange(): lax.all_to_all(block.reshape(devices, comps, rows), GROUP, split_axis=0,...  77.1 us
    all_to_all x1, waiting for transfers between devices, exchange(): lax.all_to_all(block.reshape(devices, comps, rows), GROUP, split_axis=0,...  20.4 us
    all_to_all x1, starting transfers between devices, exchange(): lax.all_to_all(block.reshape(devices, comps, rows), GROUP, split_axis=0,...  15.1 us
    unnamed x22, local copies, waits for them, and re-layouts  8.95 us
    ppermute x1, starting transfers between devices, local(): below = lax.ppermute(field[:2], SLAB, [(j, i) for i, j in ahead])  4.55 us
  transfers between devices with their start and end apart: 3, of which 1 were waited for; matrix products, arithmetic and copies ran while one was open for 0% of the time, Pallas kernels for 1%

profile of v1, /device:TPU:1, one launch (start us, length us, event | category | flops | bytes accessed | tf_op | source)
XLA Modules:
  0.0 138.6 jit_solution(2337185333290522091)
XLA Ops:
  0.0 0.8 slice_bitcast_fusion
  0.8 4.6 %collective-permute-start.1 = (f32[2,1024]{1,0:T(2,128)S(1)}, f32[2,1024]{1,0:T(2,128)S(1)}, u32[]{:S(2)}, u32[]{:S(2)}) collective-permute-start(f32[2,1024]{1,0:T(2,128)S(1)} %get-tuple-element.19), channel_id=1, source_target_pairs={{1,0},{2,1},{3,2},{4,3},{5,4},{6,5},{7,6},{0,7},{9,8},{10,9},{11,1... | collective-permute-start | bytes 24584 | tf_op jit(solution)/shard_map/ppermute | solution.py:200
  5.3 0.0 collective-permute-start
  5.3 0.0 copy-start.3
  5.3 1.6 %copy-done.3 = bf16[1024,1024]{1,0:T(8,128)(2,1)S(1)} copy-done((bf16[1024,1024]{1,0:T(8,128)(2,1)S(1)}, bf16[1024,1024]{1,0:T(8,128)(2,1)}, u32[]{:S(2)}) %copy-start.3) | copy-done | bytes 2097176
  6.9 0.0 copy-start.4
  6.9 1.6 %copy-done.4 = bf16[1024,1024]{1,0:T(8,128)(2,1)S(1)} copy-done((bf16[1024,1024]{1,0:T(8,128)(2,1)S(1)}, bf16[1024,1024]{1,0:T(8,128)(2,1)}, u32[]{:S(2)}) %copy-start.4) | copy-done | bytes 2097176
  8.5 0.0 copy-start.5
  8.5 1.0 copy-done.5
  9.6 0.0 copy-start.6
  9.6 1.0 copy-done.6
  10.6 0.0 copy-start.7
  10.6 1.0 copy-done.7
  11.7 0.0 copy-start.8
  11.7 1.0 copy-done.8
  12.7 1.4 %shard_map.64 = (f32[128,1024]{1,0:T(8,128)S(1)}, f32[128,1024]{1,0:T(8,128)S(1)}, f32[128,1024]{1,0:T(8,128)S(1)}, bf16[1024,1024]{1,0:T(8,128)(2,1)S(1)}, bf16[1024,1024]{1,0:T(8,128)(2,1)S(1)}) custom-call(s32[1]{0:T(128)} %bitcast.step_ref, f32[128,1024]{1,0:T(8,128)S(1)} %bitcast.17, f32[128,1024]{1,0:T(8,128)S(1)} %bitcast.18, ...), custom_call_target="tpu_custom_call" | custom-call | flops 4194304 | bytes 6291456 | tf_op jit(solution)/shard_map/pallas_call | solution.py:214
  14.1 0.0 copy-start
  14.1 0.0 copy-start.9
  14.1 0.0 collective-permute-done.1.below_ref
  14.1 0.0 collective-permute-done.above_ref
  14.1 2.1 %shard_map.65 = f32[1024,128]{1,0:T(8,128)} custom-call(s32[1]{0:T(128)} %bitcast.step_ref, f32[128,1024]{1,0:T(8,128)S(1)} %get-tuple-element.12.x_ref, f32[2,1024]{1,0:T(2,128)S(1)} %collective-permute-done.above_ref, f32[2,1024]{1,0:T(2,128)S(1)} %collective-permute-done.1.below_ref, f32[128,1024]{1,0:T(8,128)S(1)} %get-tuple-element.13.base_ref, ...), custom_call_target="tpu_custom_call" | custom-call | flops 805306368 | bytes 6291456 | tf_op jit(solution)/shard_map/pallas_call | solution.py:220
  16.2 0.0 copy-done
  16.2 0.0 copy-done.9
  16.2 15.1 %all-to-all-start = ((f32[256,4,128]{2,1,0:T(4,128)}), f32[256,4,128]{2,1,0:T(4,128)S(1)}, u32[]{:S(2)}, u32[]{:S(2)}) async-start(f32[256,4,128]{2,1,0:T(4,128)} %bitcast.5), calls=%async_computation | async-start | bytes 1048576 | tf_op jit(solution)/shard_map/all_to_all | solution.py:203
  31.5 0.1 fusion.3.gain_ref
  31.6 20.4 %all-to-all-done = f32[256,4,128]{2,1,0:T(4,128)S(1)} async-done(((f32[256,4,128]{2,1,0:T(4,128)}), f32[256,4,128]{2,1,0:T(4,128)S(1)}, u32[]{:S(2)}, u32[]{:S(2)}) %all-to-all-start) | async-done | bytes 524320 | tf_op jit(solution)/shard_map/all_to_all | solution.py:203
  52.0 0.0 copy-start.1
  52.0 1.6 %copy-done.1 = bf16[1024,1024]{1,0:T(8,128)(2,1)S(1)} copy-done((bf16[1024,1024]{1,0:T(8,128)(2,1)S(1)}, bf16[1024,1024]{1,0:T(8,128)(2,1)}, u32[]{:S(2)}) %copy-start.1) | copy-done | bytes 2097176
  53.6 0.0 copy-start.2
  53.6 0.0 copy-start.10
  53.6 2.0 %shard_map.66 = f32[1024,128]{1,0:T(8,128)S(1)} custom-call(f32[1024,128]{1,0:T(8,128)S(1)} %bitcast.19, f32[8,1024]{1,0:T(8,128)S(1)} %fusion.3.gain_ref, bf16[1024,1024]{1,0:T(8,128)(2,1)S(1)} %get-tuple-element.14.high_ref, bf16[1024,1024]{1,0:T(8,128)(2,1)S(1)} %copy-done.1), custom_call_target="tpu_custom_call" | custom-call | flops 1610612736 | bytes 6291456 | tf_op jit(solution)/shard_map/pallas_call | solution.py:228
  55.6 25.7 %all_to_all.20 = f32[256,4,128]{2,1,0:T(4,128)S(1)} all-to-all(f32[256,4,128]{2,1,0:T(4,128)S(1)} %bitcast.24), channel_id=1, replica_groups=mesh['xh'=2,'z'=8,'c'=2,'xl'=2,'y'=4] {'xl','y','z','c','xh'}, dimensions={0} | all-to-all | bytes 1048576 | tf_op jit(solution)/shard_map/all_to_all | solution.py:203
  81.3 0.0 copy-done.2
  81.3 0.0 copy-done.10
  81.3 2.0 %shard_map.67 = (f32[1024,128]{1,0:T(8,128)S(1)}, f32[128,1024]{1,0:T(8,128)S(1)}) custom-call(s32[1]{0:T(128)} %bitcast.step_ref, f32[1024,128]{1,0:T(8,128)S(1)} %bitcast.20, f32[128,1024]{1,0:T(8,128)S(1)} %get-tuple-element.12.x_ref, f32[128,1024]{1,0:T(8,128)S(1)} %copy-done.10, bf16[1024,1024]{1,0:T(8,128)(2,1)S(1)} %get-tuple-element.14.high_ref, ...), custom_call_target="tpu_custom_call" | custom-call | flops 1610612736 | bytes 6291456 | tf_op jit(solution)/shard_map/pallas_call | solution.py:229
  83.3 25.7 %all_to_all.21 = f32[256,4,128]{2,1,0:T(4,128)S(1)} all-to-all(f32[256,4,128]{2,1,0:T(4,128)S(1)} %bitcast.21), channel_id=1, replica_groups=mesh['xh'=2,'z'=8,'c'=2,'xl'=2,'y'=4] {'xl','y','z','c','xh'}, dimensions={0} | all-to-all | bytes 1048576 | tf_op jit(solution)/shard_map/all_to_all | solution.py:203
  109.0 2.0 %shard_map.68 = f32[1024,128]{1,0:T(8,128)S(1)} custom-call(f32[1024,128]{1,0:T(8,128)S(1)} %bitcast.22, f32[8,1024]{1,0:T(8,128)S(1)} %fusion.3.gain_ref, bf16[1024,1024]{1,0:T(8,128)(2,1)S(1)} %get-tuple-element.14.high_ref, bf16[1024,1024]{1,0:T(8,128)(2,1)S(1)} %copy-done.2), custom_call_target="tpu_custom_call" | custom-call | flops 1610612736 | bytes 6291456 | tf_op jit(solution)/shard_map/pallas_call | solution.py:233
  111.0 25.7 %all_to_all.22 = f32[256,4,128]{2,1,0:T(4,128)S(1)} all-to-all(f32[256,4,128]{2,1,0:T(4,128)S(1)} %bitcast.23), channel_id=1, replica_groups=mesh['xh'=2,'z'=8,'c'=2,'xl'=2,'y'=4] {'xl','y','z','c','xh'}, dimensions={0} | all-to-all | bytes 1048576 | tf_op jit(solution)/shard_map/all_to_all | solution.py:203
  136.7 1.8 %shard_map.69 = f32[128,1024]{1,0:T(8,128)} custom-call(f32[1024,128]{1,0:T(8,128)S(1)} %bitcast.16, f32[128,1024]{1,0:T(8,128)S(1)} %get-tuple-element.18.first_ref, bf16[1024,1024]{1,0:T(8,128)(2,1)S(1)} %get-tuple-element.14.high_ref, bf16[1024,1024]{1,0:T(8,128)(2,1)S(1)} %copy-done.2), custom_call_target="tpu_custom_call" | custom-call | flops 805306368 | bytes 6291456 | tf_op jit(solution)/shard_map/pallas_call | solution.py:234
  (2 shorter events, 0.1 us)
Async XLA Ops:
  0.8 13.3 %collective-permute-start.1 = (f32[2,1024]{1,0:T(2,128)S(1)}, f32[2,1024]{1,0:T(2,128)S(1)}, u32[]{:S(2)}, u32[]{:S(2)}) collective-permute-start(f32[2,1024]{1,0:T(2,128)S(1)} %get-tuple-element.19), channel_id=1, source_target_pairs={{1,0},{2,1},{3,2},{4,3},{5,4},{6,5},{7,6},{0,7},{9,8},{10,9},{11,1... | collective-permute-start | bytes 24584 | tf_op jit(solution)/shard_map/ppermute | solution.py:200
  5.3 8.8 %collective-permute-start = (f32[2,1024]{1,0:T(2,128)S(1)}, f32[2,1024]{1,0:T(2,128)S(1)}, u32[]{:S(2)}, u32[]{:S(2)}) collective-permute-start(f32[2,1024]{1,0:T(2,128)S(1)} %get-tuple-element.20), channel_id=1, source_target_pairs={{0,1},{1,2},{2,3},{3,4},{4,5},{5,6},{6,7},{7,0},{8,9},{9,10},{10,1... | collective-permute-start | bytes 24584 | tf_op jit(solution)/shard_map/ppermute | solution.py:199
  5.3 1.6 %copy-start.3 = (bf16[1024,1024]{1,0:T(8,128)(2,1)S(1)}, bf16[1024,1024]{1,0:T(8,128)(2,1)}, u32[]{:S(2)}) copy-start(bf16[1024,1024]{1,0:T(8,128)(2,1)} %constant.67.clone.low_hbm) | copy-start | bytes 6291460
  6.9 1.6 %copy-start.4 = (bf16[1024,1024]{1,0:T(8,128)(2,1)S(1)}, bf16[1024,1024]{1,0:T(8,128)(2,1)}, u32[]{:S(2)}) copy-start(bf16[1024,1024]{1,0:T(8,128)(2,1)} %constant.66.clone.high_hbm) | copy-start | bytes 6291460
  8.5 1.0 copy-start.5
  9.6 1.0 copy-start.6
  10.6 1.0 copy-start.7
  11.7 1.0 copy-start.8
  14.1 2.1 %copy-start = (bf16[1024,1024]{1,0:T(8,128)(2,1)}, bf16[1024,1024]{1,0:T(8,128)(2,1)S(1)}, u32[]{:S(2)}) copy-start(bf16[1024,1024]{1,0:T(8,128)(2,1)S(1)} %get-tuple-element.15.low_ref) | copy-start | bytes 6291460
  14.1 2.1 %copy-start.9 = (f32[128,1024]{1,0:T(8,128)}, f32[128,1024]{1,0:T(8,128)S(1)}, u32[]{:S(2)}) copy-start(f32[128,1024]{1,0:T(8,128)S(1)} %get-tuple-element.16.excess_ref) | copy-start | bytes 1572868
  16.2 35.7 %all-to-all-start = ((f32[256,4,128]{2,1,0:T(4,128)}), f32[256,4,128]{2,1,0:T(4,128)S(1)}, u32[]{:S(2)}, u32[]{:S(2)}) async-start(f32[256,4,128]{2,1,0:T(4,128)} %bitcast.5), calls=%async_computation | async-start | bytes 1048576 | tf_op jit(solution)/shard_map/all_to_all | solution.py:203
  52.0 1.6 %copy-start.1 = (bf16[1024,1024]{1,0:T(8,128)(2,1)S(1)}, bf16[1024,1024]{1,0:T(8,128)(2,1)}, u32[]{:S(2)}) copy-start(bf16[1024,1024]{1,0:T(8,128)(2,1)} %copy-done) | copy-start | bytes 6291460
  53.6 27.7 %copy-start.2 = (bf16[1024,1024]{1,0:T(8,128)(2,1)S(1)}, bf16[1024,1024]{1,0:T(8,128)(2,1)}, u32[]{:S(2)}) copy-start(bf16[1024,1024]{1,0:T(8,128)(2,1)} %copy-done) | copy-start | bytes 6291460
  53.6 27.7 %copy-start.10 = (f32[128,1024]{1,0:T(8,128)S(1)}, f32[128,1024]{1,0:T(8,128)}, u32[]{:S(2)}) copy-start(f32[128,1024]{1,0:T(8,128)} %copy-done.9) | copy-start | bytes 1572868

commit v2 on v1

--- a/solution.py
+++ b/solution.py
@@ -62,14 +62,25 @@
     return pltpu.roll(block, amount % block.shape[axis], axis)
 
 
-def load_kernel(step_ref, x_hbm, forcing_hbm, initial_hbm, levels_hbm, high_hbm, low_hbm,
-                x_ref, base_ref, excess_ref, high_ref, low_ref,
+def waves(index, width):
+    return 4.0 * jnp.sin(index.astype(jnp.float32) * (math.pi / width)) ** 2
+
+
+def load_kernel(step_ref, column_ref, x_hbm, forcing_hbm, initial_hbm, levels_hbm, high_hbm, low_hbm,
+                x_ref, base_ref, excess_ref, high_ref, low_ref, gain_ref,
                 forcing_ref, initial_ref, levels_ref, sems):
     pairs = [(x_hbm, x_ref), (levels_hbm, levels_ref), (forcing_hbm, forcing_ref),
              (initial_hbm, initial_ref), (high_hbm, high_ref), (low_hbm, low_ref)]
     copies = [pltpu.make_async_copy(a, b, sems.at[i]) for i, (a, b) in enumerate(pairs)]
     for copy in copies:
         copy.start()
+    shape = gain_ref.shape
+    comps = shape[0] // 2
+    lane = lax.broadcasted_iota(jnp.int32, shape, 1)
+    row = lax.broadcasted_iota(jnp.int32, shape, 0)
+    column = column_ref[0] + jnp.where(row >= comps, row - comps, row)
+    modes = waves(lane, shape[1]) + waves(column, shape[1])
+    gain_ref[...] = 1.0 / (1.0 + TIME_STEP * (modes * modes - modes + MEAN_DAMPING))
     copies[0].wait()
     copies[1].wait()
     x = x_ref[...]
@@ -204,19 +215,17 @@
             block.reshape(devices, comps, rows), GROUP, split_axis=0, concat_axis=0, tiled=True
         ).reshape(width, rows)
 
-    def waves(index):
-        return 4.0 * jnp.sin(math.pi * index.astype(jnp.float32) / width) ** 2
-
-    column = lax.axis_index(GROUP) * comps + jnp.arange(2 * comps, dtype=jnp.int32) % comps
-    modes = waves(column)[:, None] + waves(jnp.arange(width, dtype=jnp.int32))[None, :]
-    gain = 1.0 / (1.0 + TIME_STEP * (modes * modes - modes + MEAN_DAMPING))
-
-    field, base, excess, high, low = call(
-        load_kernel, [plane, plane, plane, table, table], [SMEM] + [HBM] * 6,
+    column = (lax.axis_index(GROUP) * comps).astype(jnp.int32).reshape(1)
+    gains = jax.ShapeDtypeStruct((2 * comps, width), jnp.float32)
+    stay = [pltpu.with_memory_space_constraint(a, pltpu.HBM)
+            for a in (field, forcing[0], initial, levels, high, low)]
+
+    field, base, excess, high, low, gain = call(
+        load_kernel, [plane, plane, plane, table, table, gains], [SMEM] * 2 + [HBM] * 6,
         scratch=[pltpu.VMEM((rows, width), jnp.float32), pltpu.VMEM((rows, width), jnp.float32),
                  pltpu.VMEM((rows, width), jnp.int32), pltpu.SemaphoreType.DMA((6,))],
         flops=32 * rows * width, bytes_accessed=moved_bytes,
-    )(step, field, forcing[0], initial, levels, high, low)
+    )(step, column, *stay)
     sent = call(
         functools.partial(source_kernel, steps), turned, [SMEM] + [VMEM] * 6,
         scratch=[pltpu.VMEM((rows, width), jnp.float32)], flops=work, bytes_accessed=moved_bytes,

time: 139 us -> 130 us (0.935)
  blocking collectives: 77.1 us -> 111 us
  waiting for transfers between devices: 20.4 us -> 1.66 us
  starting transfers between devices: 19.7 us -> 4.56 us
  local copies, waits for them, and re-layouts: 9.73 us -> 0.78 us
    all_to_all x3 -> x4, blocking collectives: 77.1 us -> 111 us  [exchange(): lax.all_to_all(block.reshape(devices, comps, rows), GROUP, split_axis=0,...]
    all_to_all x1 -> x0, waiting for transfers between devices: 20.4 us -> none  [exchange(): lax.all_to_all(block.reshape(devices, comps, rows), GROUP, split_axis=0,...]
    all_to_all x1 -> x0, starting transfers between devices: 15.1 us -> none  [exchange(): lax.all_to_all(block.reshape(devices, comps, rows), GROUP, split_axis=0,...]
    unnamed x22 -> x0, local copies, waits for them, and re-layouts: 8.95 us -> none
    ppermute x1, waiting for transfers between devices: 0.01 us -> 1.66 us  [local(): above = lax.ppermute(field[rows - 2:], SLAB, ahead)]
    pallas_call x1, Pallas kernels: 1.4 us -> 2.93 us  [local(): call(load_kernel, [plane, plane, plane, table, table, gains], [SMEM] * 2...]
  transfers between devices with their start and end apart: 3 -> 2, of which waited for: 1 -> 1; matrix products, arithmetic and copies ran while one was open for 0% -> 0% of each run, Pallas kernels for 1% -> 2%
where the time goes in v2:
time: 130 us
  blocking collectives  111 us (85%)
  Pallas kernels  12.2 us (9%)
  starting transfers between devices  4.56 us (4%)
  waiting for transfers between devices  1.66 us (1%)
    all_to_all x4, blocking collectives, exchange(): lax.all_to_all(block.reshape(devices, comps, rows), GROUP, split_axis=0,...  111 us
    ppermute x1, starting transfers between devices, local(): below = lax.ppermute(field[:2], SLAB, [(j, i) for i, j in ahead])  4.55 us
    pallas_call x1, Pallas kernels, local(): call(load_kernel, [plane, plane, plane, table, table, gains], [SMEM] * 2...  2.93 us
  transfers between devices with their start and end apart: 2, of which 1 were waited for; matrix products, arithmetic and copies ran while one was open for 0% of the time, Pallas kernels for 2%

profile of v2, /device:TPU:1, one launch (start us, length us, event | category | flops | bytes accessed | tf_op | source)
XLA Modules:
  0.0 130.2 jit_solution(16742425927326497027)
XLA Ops:
  0.0 0.8 slice_bitcast_fusion
  0.8 4.6 %collective-permute-start.1 = (f32[2,1024]{1,0:T(2,128)S(1)}, f32[2,1024]{1,0:T(2,128)S(1)}, u32[]{:S(2)}, u32[]{:S(2)}) collective-permute-start(f32[2,1024]{1,0:T(2,128)S(1)} %get-tuple-element.21), channel_id=1, source_target_pairs={{1,0},{2,1},{3,2},{4,3},{5,4},{6,5},{7,6},{0,7},{9,8},{10,9},{11,1... | collective-permute-start | bytes 24584 | tf_op jit(solution)/shard_map/ppermute | solution.py:211
  5.3 0.0 collective-permute-start
  5.3 2.9 %shard_map.64 = (f32[128,1024]{1,0:T(8,128)S(1)}, f32[128,1024]{1,0:T(8,128)S(1)}, f32[128,1024]{1,0:T(8,128)S(1)}, bf16[1024,1024]{1,0:T(8,128)(2,1)S(1)}, bf16...) custom-call(s32[1]{0:T(128)} %bitcast.step_ref, s32[1]{0:T(128)} %bitcast.1.column_ref, f32[128,1024]{1,0:T(8,128)} %bitcast.25, ...), custom_call_target="tpu_custom_call" | custom-call | flops 4194304 | bytes 6291456 | tf_op jit(solution)/shard_map/pallas_call | solution.py:223
  8.3 0.0 collective-permute-done.1.below_ref
  8.3 1.7 %collective-permute-done.above_ref = f32[2,1024]{1,0:T(2,128)S(1)} collective-permute-done((f32[2,1024]{1,0:T(2,128)S(1)}, f32[2,1024]{1,0:T(2,128)S(1)}, u32[]{:S(2)}, u32[]{:S(2)}) %collective-permute-start) | collective-permute-done | bytes 8224 | tf_op jit(solution)/shard_map/ppermute | solution.py:210
  9.9 1.3 shard_map.65
  11.2 33.9 %all_to_all.20 = f32[256,4,128]{2,1,0:T(4,128)S(1)} all-to-all(f32[256,4,128]{2,1,0:T(4,128)S(1)} %bitcast.17), channel_id=1, replica_groups=mesh['xh'=2,'z'=8,'c'=2,'xl'=2,'y'=4] {'xl','y','z','c','xh'}, dimensions={0} | all-to-all | bytes 1048576 | tf_op jit(solution)/shard_map/all_to_all | solution.py:214
  45.1 2.1 %shard_map.66 = f32[1024,128]{1,0:T(8,128)S(1)} custom-call(f32[1024,128]{1,0:T(8,128)S(1)} %bitcast.23, f32[8,1024]{1,0:T(8,128)S(1)} %get-tuple-element.17.gain_ref, bf16[1024,1024]{1,0:T(8,128)(2,1)S(1)} %get-tuple-element.15.high_ref, bf16[1024,1024]{1,0:T(8,128)(2,1)S(1)} %get-tuple-element.16.low_ref), custom_call_target="tpu_custom_call" | custom-call | flops 1610612736 | bytes 6291456 | tf_op jit(solution)/shard_map/pallas_call | solution.py:237
  47.2 25.7 %all_to_all.21 = f32[256,4,128]{2,1,0:T(4,128)S(1)} all-to-all(f32[256,4,128]{2,1,0:T(4,128)S(1)} %bitcast.24), channel_id=1, replica_groups=mesh['xh'=2,'z'=8,'c'=2,'xl'=2,'y'=4] {'xl','y','z','c','xh'}, dimensions={0} | all-to-all | bytes 1048576 | tf_op jit(solution)/shard_map/all_to_all | solution.py:214
  72.9 2.0 %shard_map.67 = (f32[1024,128]{1,0:T(8,128)S(1)}, f32[128,1024]{1,0:T(8,128)S(1)}) custom-call(s32[1]{0:T(128)} %bitcast.step_ref, f32[1024,128]{1,0:T(8,128)S(1)} %bitcast.19, f32[128,1024]{1,0:T(8,128)S(1)} %get-tuple-element.13.x_ref, f32[128,1024]{1,0:T(8,128)S(1)} %get-tuple-element.18.excess_ref, bf16[1024,1024]{1,0:T(8,128)(2,1)S(1)} %get-tuple-element.15.high_ref, ...), custom_call_target="tpu_custom_call" | custom-call | flops 1610612736 | bytes 6291456 | tf_op jit(solution)/shard_map/pallas_call | solution.py:238
  74.9 25.7 %all_to_all.22 = f32[256,4,128]{2,1,0:T(4,128)S(1)} all-to-all(f32[256,4,128]{2,1,0:T(4,128)S(1)} %bitcast.20), channel_id=1, replica_groups=mesh['xh'=2,'z'=8,'c'=2,'xl'=2,'y'=4] {'xl','y','z','c','xh'}, dimensions={0} | all-to-all | bytes 1048576 | tf_op jit(solution)/shard_map/all_to_all | solution.py:214
  100.6 2.1 %shard_map.68 = f32[1024,128]{1,0:T(8,128)S(1)} custom-call(f32[1024,128]{1,0:T(8,128)S(1)} %bitcast.21, f32[8,1024]{1,0:T(8,128)S(1)} %get-tuple-element.17.gain_ref, bf16[1024,1024]{1,0:T(8,128)(2,1)S(1)} %get-tuple-element.15.high_ref, bf16[1024,1024]{1,0:T(8,128)(2,1)S(1)} %get-tuple-element.16.low_ref), custom_call_target="tpu_custom_call" | custom-call | flops 1610612736 | bytes 6291456 | tf_op jit(solution)/shard_map/pallas_call | solution.py:242
  102.7 25.7 %all_to_all.23 = f32[256,4,128]{2,1,0:T(4,128)S(1)} all-to-all(f32[256,4,128]{2,1,0:T(4,128)S(1)} %bitcast.22), channel_id=1, replica_groups=mesh['xh'=2,'z'=8,'c'=2,'xl'=2,'y'=4] {'xl','y','z','c','xh'}, dimensions={0} | all-to-all | bytes 1048576 | tf_op jit(solution)/shard_map/all_to_all | solution.py:214
  128.4 1.8 %shard_map.69 = f32[128,1024]{1,0:T(8,128)} custom-call(f32[1024,128]{1,0:T(8,128)S(1)} %bitcast.18, f32[128,1024]{1,0:T(8,128)S(1)} %get-tuple-element.20.first_ref, bf16[1024,1024]{1,0:T(8,128)(2,1)S(1)} %get-tuple-element.15.high_ref, bf16[1024,1024]{1,0:T(8,128)(2,1)S(1)} %get-tuple-element.16.low_ref), custom_call_target="tpu_custom_call" | custom-call | flops 805306368 | bytes 6291456 | tf_op jit(solution)/shard_map/pallas_call | solution.py:243
Async XLA Ops:
  0.8 7.5 %collective-permute-start.1 = (f32[2,1024]{1,0:T(2,128)S(1)}, f32[2,1024]{1,0:T(2,128)S(1)}, u32[]{:S(2)}, u32[]{:S(2)}) collective-permute-start(f32[2,1024]{1,0:T(2,128)S(1)} %get-tuple-element.21), channel_id=1, source_target_pairs={{1,0},{2,1},{3,2},{4,3},{5,4},{6,5},{7,6},{0,7},{9,8},{10,9},{11,1... | collective-permute-start | bytes 24584 | tf_op jit(solution)/shard_map/ppermute | solution.py:211
  5.3 4.6 %collective-permute-start = (f32[2,1024]{1,0:T(2,128)S(1)}, f32[2,1024]{1,0:T(2,128)S(1)}, u32[]{:S(2)}, u32[]{:S(2)}) collective-permute-start(f32[2,1024]{1,0:T(2,128)S(1)} %get-tuple-element.22), channel_id=1, source_target_pairs={{0,1},{1,2},{2,3},{3,4},{4,5},{5,6},{6,7},{7,0},{8,9},{9,10},{10,1... | collective-permute-start | bytes 24584 | tf_op jit(solution)/shard_map/ppermute | solution.py:210

commit v3 on v2

v3 whole, which is shorter than its diff:
```python
import functools
import math

import jax
import jax.numpy as jnp
import ml_dtypes
import numpy as np
from jax import lax
from jax.experimental import pallas as pl
from jax.experimental.pallas import tpu as pltpu
from jax.sharding import PartitionSpec as P

TIME_STEP = 0.05
CIRCULANT_ALPHA = 0.1
MEAN_DAMPING = 5.25
DAMPING_TABLE = (0.5, 1.0, 1.5, 2.5, 4.0, 6.0, 8.0, 10.0)
AXES = {"xh": 2, "z": 8, "c": 2, "xl": 2, "y": 4}
TIME = ("xh", "z", "c")
SLAB = ("xl", "y")
GROUP = ("xl", "y", "z", "c", "xh")
TILE = 8
SHIFT = 2
VMEM = pl.BlockSpec(memory_space=pltpu.VMEM)
SMEM = pl.BlockSpec(memory_space=pltpu.SMEM)
HBM = pl.BlockSpec(memory_space=pltpu.HBM)


def hartley_tables(length):
    def parts(table):
        table = table / math.sqrt(length)
        high = table.astype(ml_dtypes.bfloat16)
        return high, (table - high.astype(np.float64)).astype(ml_dtypes.bfloat16)

    def cas(angle):
        return np.cos(angle) + np.sin(angle)

    quarter = np.arange(length // 4, dtype=np.int64)
    odd = 2 * quarter + 1
    whole = cas((quarter[:, None] * quarter[None, :] % (length // 4)) * (8.0 * math.pi / length))
    twice = cas((odd[:, None] * odd[None, :] % length) * (2.0 * math.pi / length))
    odd = 2 * np.arange(length // 2, dtype=np.int64) + 1
    half = cas((odd[:, None] * odd[None, :] % (2 * length)) * (math.pi / length))
    return parts(np.concatenate([whole, twice], axis=1)) + parts(half)


def pieces(block):
    high = block.astype(jnp.bfloat16)
    low = (block - high.astype(jnp.float32)).astype(jnp.bfloat16)
    return high, low


def product(a, b, dims):
    return lax.dot_general(a, b, (dims, ((), ())), preferred_element_type=jnp.float32)


def from_right(block, table_high, table_low):
    high, low = pieces(block)
    count = block.shape[0]
    dims = ((1,), (0,))
    tall = product(jnp.concatenate([high, low], axis=0), table_high, dims)
    return tall[:count] + tall[count:] + product(high, table_low, dims)


def transform(block, tables):
    quarter_high, quarter_low, half_high, half_low = tables
    half = half_high.shape[0]
    quarter = half // 2
    left, right = block[:, :half], block[:, half:]
    even, odd = left + right, left - right
    left, right = even[:, :quarter], even[:, quarter:]
    return jnp.concatenate([
        from_right(left + right, quarter_high[:, :quarter], quarter_low[:, :quarter]),
        from_right(left - right, quarter_high[:, quarter:], quarter_low[:, quarter:]),
        from_right(odd, half_high, half_low),
    ], axis=1)


def restore(block, tables):
    quarter_high, quarter_low, half_high, half_low = tables
    half = half_high.shape[0]
    quarter = half // 2
    left = from_right(block[:, :quarter], quarter_high[:, :quarter], quarter_low[:, :quarter])
    right = from_right(block[:, quarter:half], quarter_high[:, quarter:], quarter_low[:, quarter:])
    odd = from_right(block[:, half:], half_high, half_low)
    even = jnp.concatenate([left + right, left - right], axis=1)
    return jnp.concatenate([even + odd, even - odd], axis=1)


def read(tables):
    return [ref[...] for ref in tables]


def excess_of(levels):
    excess = jnp.full(levels.shape, -TIME_STEP * (DAMPING_TABLE[0] - MEAN_DAMPING), jnp.float32)
    for level_id in range(1, len(DAMPING_TABLE)):
        value = -TIME_STEP * (DAMPING_TABLE[level_id] - MEAN_DAMPING)
        excess = jnp.where(levels == level_id, value, excess)
    return excess


def roll(block, amount, axis):
    return pltpu.roll(block, amount % block.shape[axis], axis)


def waves(place, width):
    quarter, half = width // 4, width // 2
    even = jnp.where(place < quarter, 4 * place, 4 * (place - quarter) + 2)
    index = jnp.where(place < half, even, 2 * (place - half) + 1)
    return 4.0 * jnp.sin(index.astype(jnp.float32) * (math.pi / width)) ** 2


def own_terms(x, forcing, levels):
    excess = excess_of(levels)
    grad_cols = roll(x, -1, 1) - roll(x, 1, 1)
    terms = excess * x + TIME_STEP * forcing - (TIME_STEP / 8.0) * (grad_cols * grad_cols)
    return excess, terms


def start_all(pairs, sems):
    copies = [pltpu.make_async_copy(a, b, sems.at[i]) for i, (a, b) in enumerate(pairs)]
    for copy in copies:
        copy.start()
    return copies


def edge_kernel(step_ref, x_hbm, forcing_hbm, initial_hbm, levels_hbm, out_ref,
                x_ref, forcing_ref, initial_ref, levels_ref, sems):
    tile = x_ref.shape[0]
    last = pl.ds(x_hbm.shape[0] - tile, tile)
    copies = start_all([(x_hbm.at[last], x_ref), (forcing_hbm.at[last], forcing_ref),
                        (initial_hbm.at[last], initial_ref), (levels_hbm.at[last], levels_ref)], sems)
    for copy in copies:
        copy.wait()
    x = x_ref[...]
    _, terms = own_terms(x, forcing_ref[...], levels_ref[...])
    out_ref[:tile] = x
    out_ref[tile:] = terms + jnp.where(step_ref[0] == 0, initial_ref[...], 0.0)


def load_kernel(step_ref, column_ref, x_hbm, forcing_hbm, initial_hbm, levels_hbm, *refs):
    count = (len(refs) - 8) // 2
    tables_hbm = refs[:count]
    x_ref, base_ref, excess_ref, gain_ref = refs[count : count + 4]
    tables = refs[count + 4 : 2 * count + 4]
    forcing_ref, initial_ref, levels_ref, sems = refs[2 * count + 4 :]
    copies = start_all(
        [(x_hbm, x_ref), (levels_hbm, levels_ref), (forcing_hbm, forcing_ref), (initial_hbm, initial_ref)]
        + list(zip(tables_hbm, tables)), sems)
    shape = gain_ref.shape
    comps = shape[0] // 2
    lane = lax.broadcasted_iota(jnp.int32, shape, 1)
    row = lax.broadcasted_iota(jnp.int32, shape, 0)
    column = column_ref[0] + jnp.where(row >= comps, row - comps, row)
    modes = waves(lane, shape[1]) + waves(column, shape[1])
    gain_ref[...] = 1.0 / (1.0 + TIME_STEP * (modes * modes - modes + MEAN_DAMPING))
    for copy in copies[:3]:
        copy.wait()
    excess, terms = own_terms(x_ref[...], forcing_ref[...], levels_ref[...])
    excess_ref[...] = excess
    base_ref[...] = terms
    copies[3].wait()

    @pl.when(step_ref[0] == 0)
    def _():
        base_ref[...] += initial_ref[...]

    for copy in copies[4:]:
        copy.wait()


def source_kernel(steps, shift, step_ref, x_ref, base_ref, edge_ref, *refs):
    tables, (out_ref, source_ref) = refs[:-2], refs[-2:]
    rows = x_ref.shape[0]
    tile = edge_ref.shape[0] // 2
    x = jnp.concatenate([edge_ref[:tile], x_ref[...]], axis=0)
    base = jnp.concatenate([edge_ref[tile:], base_ref[...]], axis=0)
    up, down = roll(x, 1, 0), roll(x, -1, 0)
    grad_rows = down - up
    source_ref[...] = base - (TIME_STEP / 8.0) * (grad_rows * grad_rows)

    @pl.when(step_ref[0] == steps - 1)
    def _():
        lap = up + down + roll(x, 1, 1) + roll(x, -1, 1) - 4.0 * x
        lap_two = (
            roll(lap, 1, 0) + roll(lap, -1, 0) + roll(lap, 1, 1) + roll(lap, -1, 1) - 4.0 * lap
        )
        source_ref[...] -= x + TIME_STEP * (lap + lap_two + MEAN_DAMPING * x)

    source = roll(source_ref[...], shift - tile, 0)[:rows]
    out_ref[...] = transform(source, read(tables)).T


def solve_kernel(slabs, steps, shift, x_ref, gain_ref, *refs):
    tables, out_ref = read(refs[:-1]), refs[-1]
    rows = x_ref.shape[0] // slabs
    fields = jnp.concatenate([x_ref[pl.ds(s * rows, rows), :] for s in range(slabs)], axis=1)
    spectrum = transform(fields, tables)
    width = spectrum.shape[1]
    gain = gain_ref[...]
    powers = [gain]
    while len(powers) < steps.bit_length():
        powers.append(powers[-1] * powers[-1])
    start = gain / (1.0 - CIRCULANT_ALPHA * powers[-1])
    pack = gain.shape[0]
    half = pack // 2
    groups = rows // pack
    lane_row = lax.broadcasted_iota(jnp.int32, (1, pack, width), 1)
    u = spectrum.reshape(groups, pack, width) * start[None]

    def around(block):
        turned = roll(block.reshape(-1, width), half, 0).reshape(block.shape)
        if block.shape[0] > 1:
            other = roll(block.reshape(-1, width), -half, 0).reshape(block.shape)
            turned = jnp.where(lane_row < half, other, turned)
        return jnp.where(lane_row < half, CIRCULANT_ALPHA, 1.0) * turned

    for j in range(steps.bit_length() - 1):
        k = 1 << j
        if k < groups:
            moved = jnp.concatenate([around(u[groups - k :]), u[: groups - k]], axis=0)
        else:
            moved = around(u)
        u = u + powers[j][None] * moved
    result = restore(u.reshape(rows, width), tables)
    if shift:
        result = roll(result, -shift, 1)
    for s in range(slabs):
        out_ref[pl.ds(s * rows, rows), :] = result[:, s * rows : (s + 1) * rows]


def sweep_kernel(steps, step_ref, y_ref, x_ref, excess_ref, *refs):
    tables, (out_ref, first_ref) = read(refs[:-2]), refs[-2:]
    keep = jnp.where(step_ref[0] == steps - 1, 0.0, 1.0)
    first = restore(y_ref[...].T, tables) - keep * x_ref[...]
    first_ref[...] = first
    out_ref[...] = transform(excess_ref[...] * first, tables).T


def finish_kernel(y_ref, first_ref, *refs):
    refs[-1][...] = restore(y_ref[...].T, read(refs[:-1])) + first_ref[...]


def call(kernel, out_shapes, specs, scratch=(), flops=0, bytes_accessed=0):
    return pl.pallas_call(
        kernel,
        out_shape=out_shapes,
        in_specs=specs,
        out_specs=[VMEM] * len(out_shapes) if isinstance(out_shapes, (list, tuple)) else VMEM,
        scratch_shapes=list(scratch),
        compiler_params=pltpu.CompilerParams(vmem_limit_bytes=16 * 1024 * 1024),
        cost_estimate=pl.CostEstimate(flops=flops, bytes_accessed=bytes_accessed, transcendentals=0),
    )


def local(iterate, forcing, initial, levels):
    field = iterate[0]
    rows, width = field.shape
    steps, slabs = lax.axis_size(TIME), lax.axis_size(SLAB)
    devices = steps * slabs
    comps = width // devices
    tables = [jnp.asarray(t) for t in hartley_tables(width)]
    step = lax.axis_index(TIME).astype(jnp.int32).reshape(1)
    column = (lax.axis_index(GROUP) * comps).astype(jnp.int32).reshape(1)
    plane = jax.ShapeDtypeStruct((rows, width), jnp.float32)
    turned = jax.ShapeDtypeStruct((width, rows), jnp.float32)
    gains = jax.ShapeDtypeStruct((2 * comps, width), jnp.float32)
    work = 6 * 6 * rows * width * width // 16
    moved_bytes = 2 * width * width + 16 * rows * width

    def exchange(block):
        return lax.all_to_all(
            block.reshape(devices, comps, rows), GROUP, split_axis=0, concat_axis=0, tiled=True
        ).reshape(width, rows)

    stay = [pltpu.with_memory_space_constraint(a, pltpu.HBM)
            for a in (field, forcing[0], initial, levels)]
    stay_tables = [pltpu.with_memory_space_constraint(a, pltpu.HBM) for a in tables]
    buffers = [jnp.float32, jnp.float32, jnp.int32]

    edge = call(
        edge_kernel, jax.ShapeDtypeStruct((2 * TILE, width), jnp.float32), [SMEM] + [HBM] * 4,
        scratch=[pltpu.VMEM((TILE, width), kind) for kind in [jnp.float32] + buffers]
        + [pltpu.SemaphoreType.DMA((4,))],
        flops=32 * TILE * width, bytes_accessed=24 * TILE * width,
    )(step, *stay)
    edge = lax.ppermute(edge, SLAB, [(i, (i + 1) % slabs) for i in range(slabs)])
    field, base, excess, gain, *tables = call(
        load_kernel,
        [plane, plane, plane, gains] + [jax.ShapeDtypeStruct(t.shape, t.dtype) for t in tables],
        [SMEM] * 2 + [HBM] * (4 + len(tables)),
        scratch=[pltpu.VMEM((rows, width), kind) for kind in buffers]
        + [pltpu.SemaphoreType.DMA((4 + len(tables),))],
        flops=32 * rows * width, bytes_accessed=moved_bytes,
    )(step, column, *stay, *stay_tables)
    sent = call(
        functools.partial(source_kernel, steps, SHIFT), turned, [SMEM] + [VMEM] * (3 + len(tables)),
        scratch=[pltpu.VMEM((rows + TILE, width), jnp.float32)], flops=work, bytes_accessed=moved_bytes,
    )(step, field, base, edge, *tables)

    def solve(block, shift):
        return exchange(call(
            functools.partial(solve_kernel, slabs, steps, shift), turned, [VMEM] * (2 + len(tables)),
            flops=2 * work, bytes_accessed=moved_bytes,
        )(exchange(block), gain, *tables))

    error, first = call(
        functools.partial(sweep_kernel, steps), [turned, plane], [SMEM] + [VMEM] * (3 + len(tables)),
        flops=2 * work, bytes_accessed=moved_bytes,
    )(step, solve(sent, SHIFT), field, excess, *tables)
    increment = call(
        finish_kernel, plane, [VMEM] * (2 + len(tables)), flops=work, bytes_accessed=moved_bytes
    )(solve(error, 0), first, *tables)
    return increment[None]


def solution(mesh):
    fine = jax.sharding.Mesh(mesh.devices.reshape(tuple(AXES.values())), tuple(AXES))
    placed = (P(TIME, SLAB, None), P(TIME, SLAB, None), P(SLAB, None), P(SLAB, None))
    return jax.shard_map(
        local, mesh=fine, in_specs=placed, out_specs=P(TIME, SLAB, None), check_vma=False
    )
```

time: 130 us -> 125 us (0.962)
  Pallas kernels: 12.2 us -> 8.82 us
  starting transfers between devices: 4.56 us -> 2.2 us
    pallas_call x5 -> x6, Pallas kernels: 10.2 us -> 7.65 us  [the longest x2 2.47 us: solve(): call(functools.partial(solve_kernel, slabs, steps, shift), turned, [VMEM]...]
    ppermute x2 -> x1, starting transfers between devices: 4.56 us -> 2.2 us  [local(): lax.ppermute(edge, SLAB, [(i, (i + 1) % slabs) for i in range(slabs)])]
  transfers between devices with their start and end apart: 2 -> 1, of which waited for: 1 -> 1; matrix products, arithmetic and copies ran while one was open for 0% -> 0% of each run, Pallas kernels for 2% -> 2%
where the time goes in v3:
time: 125 us; the launch traced here: 124 us
  blocking collectives  111 us (89%)
  Pallas kernels  8.82 us (7%)
  starting transfers between devices  2.2 us (2%)
  waiting for transfers between devices  1.95 us (2%)
    all_to_all x4, blocking collectives, exchange(): lax.all_to_all(block.reshape(devices, comps, rows), GROUP, split_axis=0,...  111 us
  transfers between devices with their start and end apart: 1, of which 1 were waited for; matrix products, arithmetic and copies ran while one was open for 0% of the time, Pallas kernels for 2%

profile of v3, /device:TPU:1, one launch (start us, length us, event | category | flops | bytes accessed | tf_op | source)
XLA Modules:
  0.0 124.3 jit_solution(5448127882346014105)
XLA Ops:
  0.0 0.9 shard_map.83
  0.9 2.2 %collective-permute-start = (f32[16,1024]{1,0:T(8,128)S(1)}, f32[16,1024]{1,0:T(8,128)S(1)}, u32[]{:S(2)}, u32[]{:S(2)}) collective-permute-start(f32[16,1024]{1,0:T(8,128)S(1)} %shard_map.83), channel_id=1, source_target_pairs={{0,1},{1,2},{2,3},{3,4},{4,5},{5,6},{6,7},{7,0},{8,9},{9,10},{10,1... | collective-permute-start | bytes 196616 | tf_op jit(solution)/shard_map/ppermute | solution.py:286
  3.1 2.1 %shard_map.82 = (f32[128,1024]{1,0:T(8,128)S(1)}, f32[128,1024]{1,0:T(8,128)S(1)}, f32[128,1024]{1,0:T(8,128)S(1)}, f32[8,1024]{1,0:T(8,128)S(1)}, bf16[256,512]...) custom-call(s32[1]{0:T(128)} %bitcast.step_ref, ...), custom_call_target="tpu_custom_call" | custom-call | flops 4194304 | bytes 4194304 | tf_op jit(solution)/shard_map/pallas_call | solution.py:287
  5.2 2.0 %collective-permute-done.edge_ref = f32[16,1024]{1,0:T(8,128)S(1)} collective-permute-done((f32[16,1024]{1,0:T(8,128)S(1)}, f32[16,1024]{1,0:T(8,128)S(1)}, u32[]{:S(2)}, u32[]{:S(2)}) %collective-permute-start) | collective-permute-done | bytes 65568 | tf_op jit(solution)/shard_map/ppermute | solution.py:286
  7.2 0.8 shard_map.84
  8.0 34.2 %all_to_all.20 = f32[256,4,128]{2,1,0:T(4,128)S(1)} all-to-all(f32[256,4,128]{2,1,0:T(4,128)S(1)} %bitcast.15), channel_id=1, replica_groups=mesh['xh'=2,'z'=8,'c'=2,'xl'=2,'y'=4] {'xl','y','z','c','xh'}, dimensions={0} | all-to-all | bytes 1048576 | tf_op jit(solution)/shard_map/all_to_all | solution.py:271
  42.2 1.3 %shard_map.85 = f32[1024,128]{1,0:T(8,128)S(1)} custom-call(f32[1024,128]{1,0:T(8,128)S(1)} %bitcast.18, f32[8,1024]{1,0:T(8,128)S(1)} %get-tuple-element.21.gain_ref, bf16[256,512]{1,0:T(8,128)(2,1)S(1)} %get-tuple-element.17.refs_0_, bf16[256,512]{1,0:T(8,128)(2,1)S(1)} %get-tuple-element.18.refs_1_, bf16[512,512]{1,0:T(8,128)(2,1)S(1)} %get-tuple-element.19.refs_2_, ...), custom_call_target="tpu_custom_call" | custom-call | flops 603979776 | bytes 4194304 | tf_op jit(solution)/shard_map/pallas_call | solution.py:301
  43.5 25.7 %all_to_all.21 = f32[256,4,128]{2,1,0:T(4,128)S(1)} all-to-all(f32[256,4,128]{2,1,0:T(4,128)S(1)} %bitcast.19), channel_id=1, replica_groups=mesh['xh'=2,'z'=8,'c'=2,'xl'=2,'y'=4] {'xl','y','z','c','xh'}, dimensions={0} | all-to-all | bytes 1048576 | tf_op jit(solution)/shard_map/all_to_all | solution.py:271
  69.2 1.2 shard_map.86
  70.4 25.7 %all_to_all.22 = f32[256,4,128]{2,1,0:T(4,128)S(1)} all-to-all(f32[256,4,128]{2,1,0:T(4,128)S(1)} %bitcast.20), channel_id=1, replica_groups=mesh['xh'=2,'z'=8,'c'=2,'xl'=2,'y'=4] {'xl','y','z','c','xh'}, dimensions={0} | all-to-all | bytes 1048576 | tf_op jit(solution)/shard_map/all_to_all | solution.py:271
  96.1 1.2 shard_map.87
  97.2 25.7 %all_to_all.23 = f32[256,4,128]{2,1,0:T(4,128)S(1)} all-to-all(f32[256,4,128]{2,1,0:T(4,128)S(1)} %bitcast.17), channel_id=1, replica_groups=mesh['xh'=2,'z'=8,'c'=2,'xl'=2,'y'=4] {'xl','y','z','c','xh'}, dimensions={0} | all-to-all | bytes 1048576 | tf_op jit(solution)/shard_map/all_to_all | solution.py:271
  122.9 1.4 %shard_map.88 = f32[128,1024]{1,0:T(8,128)} custom-call(f32[1024,128]{1,0:T(8,128)S(1)} %bitcast.14, f32[128,1024]{1,0:T(8,128)S(1)} %get-tuple-element.24.first_ref, bf16[256,512]{1,0:T(8,128)(2,1)S(1)} %get-tuple-element.17.refs_0_, bf16[256,512]{1,0:T(8,128)(2,1)S(1)} %get-tuple-element.18.refs_1_, bf16[512,512]{1,0:T(8,128)(2,1)S(1)} %get-tuple-element.19.refs_2_, ...), custom_call_target="tpu_custom_call" | custom-call | flops 301989888 | bytes 4194304 | tf_op jit(solution)/shard_map/pallas_call | solution.py:310
Async XLA Ops:
  0.9 6.2 %collective-permute-start = (f32[16,1024]{1,0:T(8,128)S(1)}, f32[16,1024]{1,0:T(8,128)S(1)}, u32[]{:S(2)}, u32[]{:S(2)}) collective-permute-start(f32[16,1024]{1,0:T(8,128)S(1)} %shard_map.83), channel_id=1, source_target_pairs={{0,1},{1,2},{2,3},{3,4},{4,5},{5,6},{6,7},{7,0},{8,9},{9,10},{10,1... | collective-permute-start | bytes 196616 | tf_op jit(solution)/shard_map/ppermute | solution.py:286

commit v4 on v3

--- a/solution.py
+++ b/solution.py
@@ -55,10 +55,8 @@
 
 def from_right(block, table_high, table_low):
     high, low = pieces(block)
-    count = block.shape[0]
     dims = ((1,), (0,))
-    tall = product(jnp.concatenate([high, low], axis=0), table_high, dims)
-    return tall[:count] + tall[count:] + product(high, table_low, dims)
+    return product(high, table_high, dims) + product(low, table_high, dims) + product(high, table_low, dims)
 
 
 def transform(block, tables):
@@ -133,16 +131,31 @@
         copy.wait()
     x = x_ref[...]
     _, terms = own_terms(x, forcing_ref[...], levels_ref[...])
-    out_ref[:tile] = x
-    out_ref[tile:] = terms + jnp.where(step_ref[0] == 0, initial_ref[...], 0.0)
-
-
-def load_kernel(step_ref, column_ref, x_hbm, forcing_hbm, initial_hbm, levels_hbm, *refs):
-    count = (len(refs) - 8) // 2
+    terms = terms + jnp.where(step_ref[0] == 0, initial_ref[...], 0.0)
+    row = lax.broadcasted_iota(jnp.int32, x.shape, 0)
+    out_ref[...] = jnp.where(row < tile // 2, roll(terms, tile // 2, 0), x)
+
+
+def add_rows(x, last_step, source_ref):
+    up, down = roll(x, 1, 0), roll(x, -1, 0)
+    grad_rows = down - up
+    source_ref[...] -= (TIME_STEP / 8.0) * (grad_rows * grad_rows)
+
+    @pl.when(last_step)
+    def _():
+        lap = up + down + roll(x, 1, 1) + roll(x, -1, 1) - 4.0 * x
+        lap_two = (
+            roll(lap, 1, 0) + roll(lap, -1, 0) + roll(lap, 1, 1) + roll(lap, -1, 1) - 4.0 * lap
+        )
+        source_ref[...] -= x + TIME_STEP * (lap + lap_two + MEAN_DAMPING * x)
+
+
+def load_kernel(steps, shift, step_ref, column_ref, x_hbm, forcing_hbm, initial_hbm, levels_hbm, *refs):
+    count = (len(refs) - 10) // 2
     tables_hbm = refs[:count]
-    x_ref, base_ref, excess_ref, gain_ref = refs[count : count + 4]
-    tables = refs[count + 4 : 2 * count + 4]
-    forcing_ref, initial_ref, levels_ref, sems = refs[2 * count + 4 :]
+    x_ref, head_ref, ready_ref, excess_ref, gain_ref = refs[count : count + 5]
+    tables = refs[count + 5 : 2 * count + 5]
+    source_ref, forcing_ref, initial_ref, levels_ref, sems = refs[2 * count + 5 :]
     copies = start_all(
         [(x_hbm, x_ref), (levels_hbm, levels_ref), (forcing_hbm, forcing_ref), (initial_hbm, initial_ref)]
         + list(zip(tables_hbm, tables)), sems)
@@ -155,39 +168,32 @@
     gain_ref[...] = 1.0 / (1.0 + TIME_STEP * (modes * modes - modes + MEAN_DAMPING))
     for copy in copies[:3]:
         copy.wait()
-    excess, terms = own_terms(x_ref[...], forcing_ref[...], levels_ref[...])
+    x = x_ref[...]
+    excess, terms = own_terms(x, forcing_ref[...], levels_ref[...])
     excess_ref[...] = excess
-    base_ref[...] = terms
+    source_ref[...] = terms
     copies[3].wait()
 
     @pl.when(step_ref[0] == 0)
     def _():
-        base_ref[...] += initial_ref[...]
-
+        source_ref[...] += initial_ref[...]
+
+    head_ref[...] = source_ref[: head_ref.shape[0]]
+    add_rows(x, step_ref[0] == steps - 1, source_ref)
     for copy in copies[4:]:
         copy.wait()
-
-
-def source_kernel(steps, shift, step_ref, x_ref, base_ref, edge_ref, *refs):
+    ready_ref[...] = transform(roll(source_ref[...], shift, 0), read(tables))
+
+
+def source_kernel(steps, shift, step_ref, x_ref, head_ref, ready_ref, edge_ref, *refs):
     tables, (out_ref, source_ref) = refs[:-2], refs[-2:]
-    rows = x_ref.shape[0]
-    tile = edge_ref.shape[0] // 2
-    x = jnp.concatenate([edge_ref[:tile], x_ref[...]], axis=0)
-    base = jnp.concatenate([edge_ref[tile:], base_ref[...]], axis=0)
-    up, down = roll(x, 1, 0), roll(x, -1, 0)
-    grad_rows = down - up
-    source_ref[...] = base - (TIME_STEP / 8.0) * (grad_rows * grad_rows)
-
-    @pl.when(step_ref[0] == steps - 1)
-    def _():
-        lap = up + down + roll(x, 1, 1) + roll(x, -1, 1) - 4.0 * x
-        lap_two = (
-            roll(lap, 1, 0) + roll(lap, -1, 0) + roll(lap, 1, 1) + roll(lap, -1, 1) - 4.0 * lap
-        )
-        source_ref[...] -= x + TIME_STEP * (lap + lap_two + MEAN_DAMPING * x)
-
-    source = roll(source_ref[...], shift - tile, 0)[:rows]
-    out_ref[...] = transform(source, read(tables)).T
+    tile = edge_ref.shape[0]
+    edge = edge_ref[...]
+    x = jnp.concatenate([edge, x_ref[:tile]], axis=0)
+    source_ref[...] = jnp.concatenate([roll(edge, tile // 2, 0), head_ref[...]], axis=0)
+    add_rows(x, step_ref[0] == steps - 1, source_ref)
+    first = transform(roll(source_ref[...], shift - tile, 0), read(tables))
+    out_ref[...] = jnp.concatenate([first[:tile], ready_ref[tile:]], axis=0).T
 
 
 def solve_kernel(slabs, steps, shift, x_ref, gain_ref, *refs):
@@ -263,6 +269,7 @@
     column = (lax.axis_index(GROUP) * comps).astype(jnp.int32).reshape(1)
     plane = jax.ShapeDtypeStruct((rows, width), jnp.float32)
     turned = jax.ShapeDtypeStruct((width, rows), jnp.float32)
+    strip = jax.ShapeDtypeStruct((TILE, width), jnp.float32)
     gains = jax.ShapeDtypeStruct((2 * comps, width), jnp.float32)
     work = 6 * 6 * rows * width * width // 16
     moved_bytes = 2 * width * width + 16 * rows * width
@@ -278,24 +285,24 @@
     buffers = [jnp.float32, jnp.float32, jnp.int32]
 
     edge = call(
-        edge_kernel, jax.ShapeDtypeStruct((2 * TILE, width), jnp.float32), [SMEM] + [HBM] * 4,
+        edge_kernel, strip, [SMEM] + [HBM] * 4,
         scratch=[pltpu.VMEM((TILE, width), kind) for kind in [jnp.float32] + buffers]
         + [pltpu.SemaphoreType.DMA((4,))],
         flops=32 * TILE * width, bytes_accessed=24 * TILE * width,
     )(step, *stay)
     edge = lax.ppermute(edge, SLAB, [(i, (i + 1) % slabs) for i in range(slabs)])
-    field, base, excess, gain, *tables = call(
-        load_kernel,
-        [plane, plane, plane, gains] + [jax.ShapeDtypeStruct(t.shape, t.dtype) for t in tables],
+    field, head, ready, excess, gain, *tables = call(
+        functools.partial(load_kernel, steps, SHIFT),
+        [plane, strip, plane, plane, gains] + [jax.ShapeDtypeStruct(t.shape, t.dtype) for t in tables],
         [SMEM] * 2 + [HBM] * (4 + len(tables)),
-        scratch=[pltpu.VMEM((rows, width), kind) for kind in buffers]
+        scratch=[pltpu.VMEM((rows, width), kind) for kind in [jnp.float32] + buffers]
         + [pltpu.SemaphoreType.DMA((4 + len(tables),))],
-        flops=32 * rows * width, bytes_accessed=moved_bytes,
+        flops=work, bytes_accessed=moved_bytes,
     )(step, column, *stay, *stay_tables)
     sent = call(
-        functools.partial(source_kernel, steps, SHIFT), turned, [SMEM] + [VMEM] * (3 + len(tables)),
-        scratch=[pltpu.VMEM((rows + TILE, width), jnp.float32)], flops=work, bytes_accessed=moved_bytes,
-    )(step, field, base, edge, *tables)
+        functools.partial(source_kernel, steps, SHIFT), turned, [SMEM] + [VMEM] * (4 + len(tables)),
+        scratch=[pltpu.VMEM((2 * TILE, width), jnp.float32)], flops=work, bytes_accessed=moved_bytes,
+    )(step, field, head, ready, edge, *tables)
 
     def solve(block, shift):
         return exchange(call(

time: 125 us -> 124 us (level)
  no operation moved by 1% of the time
where the time goes in v4:
time: 124 us
  blocking collectives  111 us (90%)
  Pallas kernels  9.02 us (7%)
  starting transfers between devices  2.2 us (2%)
    all_to_all x4, blocking collectives, exchange(): lax.all_to_all(block.reshape(devices, comps, rows), GROUP, split_axis=0,...  111 us
    pallas_call x1, Pallas kernels, local(): call(functools.partial(load_kernel, steps, SHIFT), [plane, strip, plane,...  2.64 us
  transfers between devices with their start and end apart: 1, of which 1 were waited for; matrix products, arithmetic and copies ran while one was open for 0% of the time, Pallas kernels for 2%

profile of v4, /device:TPU:1, one launch (start us, length us, event | category | flops | bytes accessed | tf_op | source)
XLA Modules:
  0.0 123.6 jit_solution(3623774255128360658)
XLA Ops:
  0.0 0.9 shard_map.83
  0.9 2.2 %collective-permute-start = (f32[8,1024]{1,0:T(8,128)S(1)}, f32[8,1024]{1,0:T(8,128)S(1)}, u32[]{:S(2)}, u32[]{:S(2)}) collective-permute-start(f32[8,1024]{1,0:T(8,128)S(1)} %shard_map.83), channel_id=1, source_target_pairs={{0,1},{1,2},{2,3},{3,4},{4,5},{5,6},{6,7},{7,0},{8,9},{9,10},{10,1... | collective-permute-start | bytes 98312 | tf_op jit(solution)/shard_map/ppermute | solution.py:293
  3.1 2.6 %shard_map.82 = (f32[128,1024]{1,0:T(8,128)S(1)}, f32[8,1024]{1,0:T(8,128)S(1)}, f32[128,1024]{1,0:T(8,128)S(1)}, f32[128,1024]{1,0:T(8,128)S(1)}, f32[8,1024]{1...) custom-call(s32[1]{0:T(128)} %bitcast.step_ref, ...), custom_call_target="tpu_custom_call" | custom-call | flops 301989888 | bytes 4194304 | tf_op jit(solution)/shard_map/pallas_call | solution.py:294
  5.8 1.0 collective-permute-done.edge_ref
  6.8 0.6 shard_map.84
  7.4 34.2 %all_to_all.20 = f32[256,4,128]{2,1,0:T(4,128)S(1)} all-to-all(f32[256,4,128]{2,1,0:T(4,128)S(1)} %bitcast.15), channel_id=1, replica_groups=mesh['xh'=2,'z'=8,'c'=2,'xl'=2,'y'=4] {'xl','y','z','c','xh'}, dimensions={0} | all-to-all | bytes 1048576 | tf_op jit(solution)/shard_map/all_to_all | solution.py:278
  41.6 1.2 shard_map.85
  42.9 25.7 %all_to_all.21 = f32[256,4,128]{2,1,0:T(4,128)S(1)} all-to-all(f32[256,4,128]{2,1,0:T(4,128)S(1)} %bitcast.19), channel_id=1, replica_groups=mesh['xh'=2,'z'=8,'c'=2,'xl'=2,'y'=4] {'xl','y','z','c','xh'}, dimensions={0} | all-to-all | bytes 1048576 | tf_op jit(solution)/shard_map/all_to_all | solution.py:278
  68.6 1.2 shard_map.86
  69.8 25.7 %all_to_all.22 = f32[256,4,128]{2,1,0:T(4,128)S(1)} all-to-all(f32[256,4,128]{2,1,0:T(4,128)S(1)} %bitcast.20), channel_id=1, replica_groups=mesh['xh'=2,'z'=8,'c'=2,'xl'=2,'y'=4] {'xl','y','z','c','xh'}, dimensions={0} | all-to-all | bytes 1048576 | tf_op jit(solution)/shard_map/all_to_all | solution.py:278
  95.4 1.1 shard_map.87
  96.5 25.7 %all_to_all.23 = f32[256,4,128]{2,1,0:T(4,128)S(1)} all-to-all(f32[256,4,128]{2,1,0:T(4,128)S(1)} %bitcast.17), channel_id=1, replica_groups=mesh['xh'=2,'z'=8,'c'=2,'xl'=2,'y'=4] {'xl','y','z','c','xh'}, dimensions={0} | all-to-all | bytes 1048576 | tf_op jit(solution)/shard_map/all_to_all | solution.py:278
  122.2 1.4 %shard_map.88 = f32[128,1024]{1,0:T(8,128)} custom-call(f32[1024,128]{1,0:T(8,128)S(1)} %bitcast.14, f32[128,1024]{1,0:T(8,128)S(1)} %get-tuple-element.26.first_ref, bf16[256,512]{1,0:T(8,128)(2,1)S(1)} %get-tuple-element.19.refs_0_, bf16[256,512]{1,0:T(8,128)(2,1)S(1)} %get-tuple-element.20.refs_1_, bf16[512,512]{1,0:T(8,128)(2,1)S(1)} %get-tuple-element.21.refs_2_, ...), custom_call_target="tpu_custom_call" | custom-call | flops 301989888 | bytes 4194304 | tf_op jit(solution)/shard_map/pallas_call | solution.py:317
Async XLA Ops:
  0.9 5.9 %collective-permute-start = (f32[8,1024]{1,0:T(8,128)S(1)}, f32[8,1024]{1,0:T(8,128)S(1)}, u32[]{:S(2)}, u32[]{:S(2)}) collective-permute-start(f32[8,1024]{1,0:T(8,128)S(1)} %shard_map.83), channel_id=1, source_target_pairs={{0,1},{1,2},{2,3},{3,4},{4,5},{5,6},{6,7},{7,0},{8,9},{9,10},{10,1... | collective-permute-start | bytes 98312 | tf_op jit(solution)/shard_map/ppermute | solution.py:293

commit v5 on v4

--- a/solution.py
+++ b/solution.py
@@ -17,7 +17,7 @@
 AXES = {"xh": 2, "z": 8, "c": 2, "xl": 2, "y": 4}
 TIME = ("xh", "z", "c")
 SLAB = ("xl", "y")
-GROUP = ("xl", "y", "z", "c", "xh")
+GROUP = ("z", "xl", "y")
 TILE = 8
 SHIFT = 2
 VMEM = pl.BlockSpec(memory_space=pltpu.VMEM)
@@ -160,10 +160,8 @@
         [(x_hbm, x_ref), (levels_hbm, levels_ref), (forcing_hbm, forcing_ref), (initial_hbm, initial_ref)]
         + list(zip(tables_hbm, tables)), sems)
     shape = gain_ref.shape
-    comps = shape[0] // 2
     lane = lax.broadcasted_iota(jnp.int32, shape, 1)
-    row = lax.broadcasted_iota(jnp.int32, shape, 0)
-    column = column_ref[0] + jnp.where(row >= comps, row - comps, row)
+    column = column_ref[0] + lax.broadcasted_iota(jnp.int32, shape, 0)
     modes = waves(lane, shape[1]) + waves(column, shape[1])
     gain_ref[...] = 1.0 / (1.0 + TIME_STEP * (modes * modes - modes + MEAN_DAMPING))
     for copy in copies[:3]:
@@ -196,42 +194,60 @@
     out_ref[...] = jnp.concatenate([first[:tile], ready_ref[tile:]], axis=0).T
 
 
-def solve_kernel(slabs, steps, shift, x_ref, gain_ref, *refs):
+def spectrum_kernel(slabs, x_ref, gain_ref, *refs):
+    tables, (out_ref, end_ref) = read(refs[:-2]), refs[-2:]
+    comps = gain_ref.shape[0]
+    blocks = x_ref[...].reshape(-1, slabs, comps, x_ref.shape[1])
+    planes = blocks.shape[0]
+    fields = jnp.concatenate(
+        [blocks[:, s].reshape(planes * comps, -1) for s in range(slabs)], axis=1
+    )
+    spectrum = transform(fields, tables)
+    out_ref[...] = spectrum
+    ratio = gain_ref[...] * gain_ref[...]
+    end = spectrum[:comps]
+    for z in range(1, planes):
+        end = spectrum[z * comps : (z + 1) * comps] + ratio * end
+    end_ref[...] = end
+
+
+def solve_kernel(slabs, shift, core_ref, half_ref, own_ref, other_ref, same_ref, cross_ref, gain_ref, *refs):
     tables, out_ref = read(refs[:-1]), refs[-1]
-    rows = x_ref.shape[0] // slabs
-    fields = jnp.concatenate([x_ref[pl.ds(s * rows, rows), :] for s in range(slabs)], axis=1)
-    spectrum = transform(fields, tables)
-    width = spectrum.shape[1]
     gain = gain_ref[...]
-    powers = [gain]
-    while len(powers) < steps.bit_length():
-        powers.append(powers[-1] * powers[-1])
-    start = gain / (1.0 - CIRCULANT_ALPHA * powers[-1])
-    pack = gain.shape[0]
-    half = pack // 2
-    groups = rows // pack
-    lane_row = lax.broadcasted_iota(jnp.int32, (1, pack, width), 1)
-    u = spectrum.reshape(groups, pack, width) * start[None]
-
-    def around(block):
-        turned = roll(block.reshape(-1, width), half, 0).reshape(block.shape)
-        if block.shape[0] > 1:
-            other = roll(block.reshape(-1, width), -half, 0).reshape(block.shape)
-            turned = jnp.where(lane_row < half, other, turned)
-        return jnp.where(lane_row < half, CIRCULANT_ALPHA, 1.0) * turned
-
-    for j in range(steps.bit_length() - 1):
-        k = 1 << j
-        if k < groups:
-            moved = jnp.concatenate([around(u[groups - k :]), u[: groups - k]], axis=0)
-        else:
-            moved = around(u)
-        u = u + powers[j][None] * moved
-    result = restore(u.reshape(rows, width), tables)
+    comps, width = gain.shape
+    planes = own_ref.shape[0] // comps
+    first_core = core_ref[0] == 0
+    ratio = gain * gain
+    power = ratio
+    for _ in range(planes.bit_length() - 1):
+        power = power * power
+    own, other = own_ref[...], other_ref[...]
+    even, odd = jnp.where(first_core, own, other), jnp.where(first_core, other, own)
+    same, cross = same_ref[...], cross_ref[...]
+    even_end, odd_end = jnp.where(first_core, same, cross), jnp.where(first_core, cross, same)
+    even = [even[z * comps : (z + 1) * comps] for z in range(planes)]
+    pairs = [gain * odd[z * comps : (z + 1) * comps] + ratio * even[z] for z in range(planes)]
+    own_end = pairs[0]
+    for z in range(1, planes):
+        own_end = pairs[z] + ratio * own_end
+    other_end = gain * odd_end + ratio * even_end
+    weight = jnp.where(half_ref[0] == 0, CIRCULANT_ALPHA, 1.0)
+    before = (weight * other_end + CIRCULANT_ALPHA * power * own_end) / (
+        1.0 - CIRCULANT_ALPHA * power * power
+    )
+    solved = []
+    for z in range(planes):
+        after = pairs[z] + ratio * before
+        solved.append(jnp.where(first_core, gain * (even[z] + before), after))
+        before = after
+    result = restore(jnp.concatenate(solved, axis=0), tables)
     if shift:
         result = roll(result, -shift, 1)
+    rows = width // slabs
     for s in range(slabs):
-        out_ref[pl.ds(s * rows, rows), :] = result[:, s * rows : (s + 1) * rows]
+        part = result[:, s * rows : (s + 1) * rows]
+        for z in range(planes):
+            out_ref[pl.ds((z * slabs + s) * comps, comps), :] = part[z * comps : (z + 1) * comps]
 
 
 def sweep_kernel(steps, step_ref, y_ref, x_ref, excess_ref, *refs):
@@ -261,22 +277,21 @@
 def local(iterate, forcing, initial, levels):
     field = iterate[0]
     rows, width = field.shape
-    steps, slabs = lax.axis_size(TIME), lax.axis_size(SLAB)
-    devices = steps * slabs
-    comps = width // devices
+    steps, slabs, peers = (lax.axis_size(axes) for axes in (TIME, SLAB, GROUP))
+    comps = width // peers
     tables = [jnp.asarray(t) for t in hartley_tables(width)]
     step = lax.axis_index(TIME).astype(jnp.int32).reshape(1)
     column = (lax.axis_index(GROUP) * comps).astype(jnp.int32).reshape(1)
     plane = jax.ShapeDtypeStruct((rows, width), jnp.float32)
     turned = jax.ShapeDtypeStruct((width, rows), jnp.float32)
     strip = jax.ShapeDtypeStruct((TILE, width), jnp.float32)
-    gains = jax.ShapeDtypeStruct((2 * comps, width), jnp.float32)
+    gains = jax.ShapeDtypeStruct((comps, width), jnp.float32)
     work = 6 * 6 * rows * width * width // 16
     moved_bytes = 2 * width * width + 16 * rows * width
 
     def exchange(block):
         return lax.all_to_all(
-            block.reshape(devices, comps, rows), GROUP, split_axis=0, concat_axis=0, tiled=True
+            block.reshape(peers, comps, rows), GROUP, split_axis=0, concat_axis=0, tiled=True
         ).reshape(width, rows)
 
     stay = [pltpu.with_memory_space_constraint(a, pltpu.HBM)
@@ -304,11 +319,21 @@
         scratch=[pltpu.VMEM((2 * TILE, width), jnp.float32)], flops=work, bytes_accessed=moved_bytes,
     )(step, field, head, ready, edge, *tables)
 
+    core, half = (lax.axis_index(axis).astype(jnp.int32).reshape(1) for axis in ("c", "xh"))
+    swap = [(0, 1), (1, 0)]
+
     def solve(block, shift):
+        own, end = call(
+            functools.partial(spectrum_kernel, slabs), [plane, gains], [VMEM] * (2 + len(tables)),
+            flops=work, bytes_accessed=moved_bytes,
+        )(exchange(block), gain, *tables)
+        same = lax.ppermute(end, "xh", swap)
+        cross = lax.ppermute(end, ("xh", "c"), [(i, 3 - i) for i in range(4)])
+        other = lax.ppermute(own, "c", swap)
         return exchange(call(
-            functools.partial(solve_kernel, slabs, steps, shift), turned, [VMEM] * (2 + len(tables)),
-            flops=2 * work, bytes_accessed=moved_bytes,
-        )(exchange(block), gain, *tables))
+            functools.partial(solve_kernel, slabs, shift), turned,
+            [SMEM] * 2 + [VMEM] * (5 + len(tables)), flops=work, bytes_accessed=moved_bytes,
+        )(core, half, own, other, same, cross, gain, *tables))
 
     error, first = call(
         functools.partial(sweep_kernel, steps), [turned, plane], [SMEM] + [VMEM] * (3 + len(tables)),

time: 124 us -> 126 us (1.016)
  the two profiles are of different devices: /device:TPU:1 before, /device:TPU:2 now
where the time goes in v5:
time: 126 us; the launch traced here: 125 us
  blocking collectives  96.8 us (77%)
  waiting for transfers between devices  9.88 us (8%)
  Pallas kernels  9.4 us (7%)
  starting transfers between devices  9.14 us (7%)
    all_to_all x4, blocking collectives, exchange(): lax.all_to_all(block.reshape(peers, comps, rows), GROUP, split_axis=0, co...  96.8 us
    ppermute x2, waiting for transfers between devices, solve(): same = lax.ppermute(end, 'xh', swap)  4.57 us
    ppermute x2, starting transfers between devices, solve(): cross = lax.ppermute(end, ('xh', 'c'), [(i, 3 - i) for i in range(4)])  3.89 us
    ppermute x2, waiting for transfers between devices, solve(): cross = lax.ppermute(end, ('xh', 'c'), [(i, 3 - i) for i in range(4)])  3.56 us
    ppermute x2, starting transfers between devices, solve(): same = lax.ppermute(end, 'xh', swap)  3.41 us
    pallas_call x1, Pallas kernels, local(): call(functools.partial(load_kernel, steps, SHIFT), [plane, strip, plane,...  2.69 us
  transfers between devices with their start and end apart: 7, of which 5 were waited for; matrix products, arithmetic and copies ran while one was open for 0% of the time, Pallas kernels for 2%

profile of v5, /device:TPU:2, one launch (start us, length us, event | category | flops | bytes accessed | tf_op | source)
XLA Modules:
  0.0 125.3 jit_solution(3528572322232074741)
XLA Ops:
  0.0 0.9 shard_map.83
  0.9 1.7 %collective-permute-start = (f32[8,1024]{1,0:T(8,128)S(1)}, f32[8,1024]{1,0:T(8,128)S(1)}, u32[]{:S(2)}, u32[]{:S(2)}) collective-permute-start(f32[8,1024]{1,0:T(8,128)S(1)} %shard_map.83), channel_id=1, source_target_pairs={{0,1},{1,2},{2,3},{3,4},{4,5},{5,6},{6,7},{7,0},{8,9},{9,10},{10,1... | collective-permute-start | bytes 98312 | tf_op jit(solution)/shard_map/ppermute | solution.py:308
  2.6 2.7 %shard_map.82 = (f32[128,1024]{1,0:T(8,128)S(1)}, f32[8,1024]{1,0:T(8,128)S(1)}, f32[128,1024]{1,0:T(8,128)S(1)}, f32[128,1024]{1,0:T(8,128)S(1)}, f32[16,1024]{...) custom-call(s32[1]{0:T(128)} %bitcast.2.step_ref, ...), custom_call_target="tpu_custom_call" | custom-call | flops 301989888 | bytes 4194304 | tf_op jit(solution)/shard_map/pallas_call | solution.py:309
  5.3 1.8 %collective-permute-done.edge_ref = f32[8,1024]{1,0:T(8,128)S(1)} collective-permute-done((f32[8,1024]{1,0:T(8,128)S(1)}, f32[8,1024]{1,0:T(8,128)S(1)}, u32[]{:S(2)}, u32[]{:S(2)}) %collective-permute-start) | collective-permute-done | bytes 32800 | tf_op jit(solution)/shard_map/ppermute | solution.py:308
  7.0 0.6 shard_map.84
  7.6 28.3 %all_to_all.20 = f32[64,16,128]{2,1,0:T(8,128)S(1)} all-to-all(f32[64,16,128]{2,1,0:T(8,128)S(1)} %bitcast.19), channel_id=1, replica_groups=mesh['xh'=2,'z'=8,'c'=2,'xl'=2,'y'=4] {'z','xl','y'}, dimensions={0} | all-to-all | bytes 1048576 | tf_op jit(solution)/shard_map/all_to_all | solution.py:293
  35.9 0.5 shard_map.85
  36.4 0.1 collective-permute-start.1
  36.5 2.2 %collective-permute-start.3 = (f32[16,1024]{1,0:T(8,128)S(1)}, f32[16,1024]{1,0:T(8,128)S(1)}, u32[]{:S(2)}, u32[]{:S(2)}) collective-permute-start(f32[16,1024]{1,0:T(8,128)S(1)} %get-tuple-element.29), channel_id=1, source_target_pairs={{0,136},{8,128},{128,8},{136,0},{1,137},{9,129},{129,9},{137,1},{2... | collective-permute-start | bytes 196616 | tf_op jit(solution)/shard_map/ppermute | solution.py:331
  38.7 1.4 %collective-permute-start.2 = (f32[16,1024]{1,0:T(8,128)S(1)}, f32[16,1024]{1,0:T(8,128)S(1)}, u32[]{:S(2)}, u32[]{:S(2)}) collective-permute-start(f32[16,1024]{1,0:T(8,128)S(1)} %get-tuple-element.29), channel_id=1, source_target_pairs={{0,128},{128,0},{1,129},{129,1},{2,130},{130,2},{3,131},{131,3},{4... | collective-permute-start | bytes 196616 | tf_op jit(solution)/shard_map/ppermute | solution.py:330
  40.1 1.8 %collective-permute-done.3.cross_ref = f32[16,1024]{1,0:T(8,128)S(1)} collective-permute-done((f32[16,1024]{1,0:T(8,128)S(1)}, f32[16,1024]{1,0:T(8,128)S(1)}, u32[]{:S(2)}, u32[]{:S(2)}) %collective-permute-start.3) | collective-permute-done | bytes 65568 | tf_op jit(solution)/shard_map/ppermute | solution.py:331
  41.9 2.6 %collective-permute-done.2.same_ref = f32[16,1024]{1,0:T(8,128)S(1)} collective-permute-done((f32[16,1024]{1,0:T(8,128)S(1)}, f32[16,1024]{1,0:T(8,128)S(1)}, u32[]{:S(2)}, u32[]{:S(2)}) %collective-permute-start.2) | collective-permute-done | bytes 65568 | tf_op jit(solution)/shard_map/ppermute | solution.py:330
  44.5 0.0 collective-permute-done.1.other_ref
  44.5 0.9 shard_map.86
  45.4 23.2 %all_to_all.21 = f32[64,16,128]{2,1,0:T(8,128)S(1)} all-to-all(f32[64,16,128]{2,1,0:T(8,128)S(1)} %bitcast.18), channel_id=1, replica_groups=mesh['xh'=2,'z'=8,'c'=2,'xl'=2,'y'=4] {'z','xl','y'}, dimensions={0} | all-to-all | bytes 1048576 | tf_op jit(solution)/shard_map/all_to_all | solution.py:293
  68.6 1.2 shard_map.87
  69.8 22.3 %all_to_all.22 = f32[64,16,128]{2,1,0:T(8,128)S(1)} all-to-all(f32[64,16,128]{2,1,0:T(8,128)S(1)} %bitcast.22), channel_id=1, replica_groups=mesh['xh'=2,'z'=8,'c'=2,'xl'=2,'y'=4] {'z','xl','y'}, dimensions={0} | all-to-all | bytes 1048576 | tf_op jit(solution)/shard_map/all_to_all | solution.py:293
  92.1 0.5 shard_map.88
  92.6 0.1 collective-permute-start.4
  92.7 1.6 %collective-permute-start.6 = (f32[16,1024]{1,0:T(8,128)S(1)}, f32[16,1024]{1,0:T(8,128)S(1)}, u32[]{:S(2)}, u32[]{:S(2)}) collective-permute-start(f32[16,1024]{1,0:T(8,128)S(1)} %get-tuple-element.33), channel_id=1, source_target_pairs={{0,136},{8,128},{128,8},{136,0},{1,137},{9,129},{129,9},{137,1},{2... | collective-permute-start | bytes 196616 | tf_op jit(solution)/shard_map/ppermute | solution.py:331
  94.3 2.0 %collective-permute-start.5 = (f32[16,1024]{1,0:T(8,128)S(1)}, f32[16,1024]{1,0:T(8,128)S(1)}, u32[]{:S(2)}, u32[]{:S(2)}) collective-permute-start(f32[16,1024]{1,0:T(8,128)S(1)} %get-tuple-element.33), channel_id=1, source_target_pairs={{0,128},{128,0},{1,129},{129,1},{2,130},{130,2},{3,131},{131,3},{4... | collective-permute-start | bytes 196616 | tf_op jit(solution)/shard_map/ppermute | solution.py:330
  96.3 1.8 %collective-permute-done.6.cross_ref = f32[16,1024]{1,0:T(8,128)S(1)} collective-permute-done((f32[16,1024]{1,0:T(8,128)S(1)}, f32[16,1024]{1,0:T(8,128)S(1)}, u32[]{:S(2)}, u32[]{:S(2)}) %collective-permute-start.6) | collective-permute-done | bytes 65568 | tf_op jit(solution)/shard_map/ppermute | solution.py:331
  98.1 2.0 %collective-permute-done.5.same_ref = f32[16,1024]{1,0:T(8,128)S(1)} collective-permute-done((f32[16,1024]{1,0:T(8,128)S(1)}, f32[16,1024]{1,0:T(8,128)S(1)}, u32[]{:S(2)}, u32[]{:S(2)}) %collective-permute-start.5) | collective-permute-done | bytes 65568 | tf_op jit(solution)/shard_map/ppermute | solution.py:330
  100.1 0.0 collective-permute-done.4.other_ref
  100.1 0.7 shard_map.89
  100.8 23.0 %all_to_all.23 = f32[64,16,128]{2,1,0:T(8,128)S(1)} all-to-all(f32[64,16,128]{2,1,0:T(8,128)S(1)} %bitcast.16), channel_id=1, replica_groups=mesh['xh'=2,'z'=8,'c'=2,'xl'=2,'y'=4] {'z','xl','y'}, dimensions={0} | all-to-all | bytes 1048576 | tf_op jit(solution)/shard_map/all_to_all | solution.py:293
  123.9 1.4 %shard_map.90 = f32[128,1024]{1,0:T(8,128)} custom-call(f32[1024,128]{1,0:T(8,128)S(1)} %bitcast.17, f32[128,1024]{1,0:T(8,128)S(1)} %get-tuple-element.34.first_ref, bf16[256,512]{1,0:T(8,128)(2,1)S(1)} %get-tuple-element.23.refs_0_, bf16[256,512]{1,0:T(8,128)(2,1)S(1)} %get-tuple-element.24.refs_1_, bf16[512,512]{1,0:T(8,128)(2,1)S(1)} %get-tuple-element.25.refs_2_, ...), custom_call_target="tpu_custom_call" | custom-call | flops 301989888 | bytes 4194304 | tf_op jit(solution)/shard_map/pallas_call | solution.py:342
Async XLA Ops:
  0.9 6.1 %collective-permute-start = (f32[8,1024]{1,0:T(8,128)S(1)}, f32[8,1024]{1,0:T(8,128)S(1)}, u32[]{:S(2)}, u32[]{:S(2)}) collective-permute-start(f32[8,1024]{1,0:T(8,128)S(1)} %shard_map.83), channel_id=1, source_target_pairs={{0,1},{1,2},{2,3},{3,4},{4,5},{5,6},{6,7},{7,0},{8,9},{9,10},{10,1... | collective-permute-start | bytes 98312 | tf_op jit(solution)/shard_map/ppermute | solution.py:308
  36.4 8.1 %collective-permute-start.1 = (f32[128,1024]{1,0:T(8,128)S(1)}, f32[128,1024]{1,0:T(8,128)S(1)}, u32[]{:S(2)}, u32[]{:S(2)}) collective-permute-start(f32[128,1024]{1,0:T(8,128)S(1)} %get-tuple-element.28.own_ref), channel_id=1, source_target_pairs={{0,8},{8,0},{1,9},{9,1},{2,10},{10,2},{3,11},{11,3},{4,12},{12,4},... | collective-permute-start | bytes 1572872 | tf_op jit(solution)/shard_map/ppermute | solution.py:332
  36.5 5.4 %collective-permute-start.3 = (f32[16,1024]{1,0:T(8,128)S(1)}, f32[16,1024]{1,0:T(8,128)S(1)}, u32[]{:S(2)}, u32[]{:S(2)}) collective-permute-start(f32[16,1024]{1,0:T(8,128)S(1)} %get-tuple-element.29), channel_id=1, source_target_pairs={{0,136},{8,128},{128,8},{136,0},{1,137},{9,129},{129,9},{137,1},{2... | collective-permute-start | bytes 196616 | tf_op jit(solution)/shard_map/ppermute | solution.py:331
  38.7 5.8 %collective-permute-start.2 = (f32[16,1024]{1,0:T(8,128)S(1)}, f32[16,1024]{1,0:T(8,128)S(1)}, u32[]{:S(2)}, u32[]{:S(2)}) collective-permute-start(f32[16,1024]{1,0:T(8,128)S(1)} %get-tuple-element.29), channel_id=1, source_target_pairs={{0,128},{128,0},{1,129},{129,1},{2,130},{130,2},{3,131},{131,3},{4... | collective-permute-start | bytes 196616 | tf_op jit(solution)/shard_map/ppermute | solution.py:330
  92.6 7.5 %collective-permute-start.4 = (f32[128,1024]{1,0:T(8,128)S(1)}, f32[128,1024]{1,0:T(8,128)S(1)}, u32[]{:S(2)}, u32[]{:S(2)}) collective-permute-start(f32[128,1024]{1,0:T(8,128)S(1)} %get-tuple-element.32.own_ref), channel_id=1, source_target_pairs={{0,8},{8,0},{1,9},{9,1},{2,10},{10,2},{3,11},{11,3},{4,12},{12,4},... | collective-permute-start | bytes 1572872 | tf_op jit(solution)/shard_map/ppermute | solution.py:332
  92.7 5.4 %collective-permute-start.6 = (f32[16,1024]{1,0:T(8,128)S(1)}, f32[16,1024]{1,0:T(8,128)S(1)}, u32[]{:S(2)}, u32[]{:S(2)}) collective-permute-start(f32[16,1024]{1,0:T(8,128)S(1)} %get-tuple-element.33), channel_id=1, source_target_pairs={{0,136},{8,128},{128,8},{136,0},{1,137},{9,129},{129,9},{137,1},{2... | collective-permute-start | bytes 196616 | tf_op jit(solution)/shard_map/ppermute | solution.py:331
  94.3 5.8 %collective-permute-start.5 = (f32[16,1024]{1,0:T(8,128)S(1)}, f32[16,1024]{1,0:T(8,128)S(1)}, u32[]{:S(2)}, u32[]{:S(2)}) collective-permute-start(f32[16,1024]{1,0:T(8,128)S(1)} %get-tuple-element.33), channel_id=1, source_target_pairs={{0,128},{128,0},{1,129},{129,1},{2,130},{130,2},{3,131},{131,3},{4... | collective-permute-start | bytes 196616 | tf_op jit(solution)/shard_map/ppermute | solution.py:330

commit v6 on v5

--- a/solution.py
+++ b/solution.py
@@ -17,7 +17,7 @@
 AXES = {"xh": 2, "z": 8, "c": 2, "xl": 2, "y": 4}
 TIME = ("xh", "z", "c")
 SLAB = ("xl", "y")
-GROUP = ("z", "xl", "y")
+GROUP = ("z", "xl", "y", "xh")
 TILE = 8
 SHIFT = 2
 VMEM = pl.BlockSpec(memory_space=pltpu.VMEM)
@@ -194,60 +194,48 @@
     out_ref[...] = jnp.concatenate([first[:tile], ready_ref[tile:]], axis=0).T
 
 
-def spectrum_kernel(slabs, x_ref, gain_ref, *refs):
-    tables, (out_ref, end_ref) = read(refs[:-2]), refs[-2:]
-    comps = gain_ref.shape[0]
-    blocks = x_ref[...].reshape(-1, slabs, comps, x_ref.shape[1])
-    planes = blocks.shape[0]
+def spectrum_kernel(slabs, planes, x_ref, *refs):
+    tables, out_ref = read(refs[:-1]), refs[-1]
+    blocks = x_ref[...].reshape(planes, slabs, -1, x_ref.shape[1])
     fields = jnp.concatenate(
-        [blocks[:, s].reshape(planes * comps, -1) for s in range(slabs)], axis=1
+        [blocks[:, s].reshape(-1, x_ref.shape[1]) for s in range(slabs)], axis=1
     )
-    spectrum = transform(fields, tables)
-    out_ref[...] = spectrum
-    ratio = gain_ref[...] * gain_ref[...]
-    end = spectrum[:comps]
-    for z in range(1, planes):
-        end = spectrum[z * comps : (z + 1) * comps] + ratio * end
-    end_ref[...] = end
-
-
-def solve_kernel(slabs, shift, core_ref, half_ref, own_ref, other_ref, same_ref, cross_ref, gain_ref, *refs):
+    out_ref[...] = transform(fields, tables)
+
+
+def solve_kernel(slabs, planes, shift, core_ref, own_ref, other_ref, gain_ref, *refs):
     tables, out_ref = read(refs[:-1]), refs[-1]
     gain = gain_ref[...]
     comps, width = gain.shape
-    planes = own_ref.shape[0] // comps
+    count = own_ref.shape[0] // comps
+    halves = count // planes
     first_core = core_ref[0] == 0
     ratio = gain * gain
     power = ratio
-    for _ in range(planes.bit_length() - 1):
+    for _ in range(count.bit_length() - 1):
         power = power * power
     own, other = own_ref[...], other_ref[...]
     even, odd = jnp.where(first_core, own, other), jnp.where(first_core, other, own)
-    same, cross = same_ref[...], cross_ref[...]
-    even_end, odd_end = jnp.where(first_core, same, cross), jnp.where(first_core, cross, same)
-    even = [even[z * comps : (z + 1) * comps] for z in range(planes)]
-    pairs = [gain * odd[z * comps : (z + 1) * comps] + ratio * even[z] for z in range(planes)]
-    own_end = pairs[0]
-    for z in range(1, planes):
-        own_end = pairs[z] + ratio * own_end
-    other_end = gain * odd_end + ratio * even_end
-    weight = jnp.where(half_ref[0] == 0, CIRCULANT_ALPHA, 1.0)
-    before = (weight * other_end + CIRCULANT_ALPHA * power * own_end) / (
-        1.0 - CIRCULANT_ALPHA * power * power
-    )
-    solved = []
-    for z in range(planes):
-        after = pairs[z] + ratio * before
-        solved.append(jnp.where(first_core, gain * (even[z] + before), after))
+    order = [z * halves + half for half in range(halves) for z in range(planes)]
+    even = [even[i * comps : (i + 1) * comps] for i in order]
+    pairs = [gain * odd[i * comps : (i + 1) * comps] + ratio * e for i, e in zip(order, even)]
+    end = pairs[0]
+    for pair in pairs[1:]:
+        end = pair + ratio * end
+    before = end * (CIRCULANT_ALPHA / (1.0 - CIRCULANT_ALPHA * power))
+    solved = [None] * count
+    for i, pair, e in zip(order, pairs, even):
+        after = pair + ratio * before
+        solved[i] = jnp.where(first_core, gain * (e + before), after)
         before = after
     result = restore(jnp.concatenate(solved, axis=0), tables)
     if shift:
         result = roll(result, -shift, 1)
-    rows = width // slabs
+    rows, chunk = width // slabs, halves * comps
     for s in range(slabs):
         part = result[:, s * rows : (s + 1) * rows]
         for z in range(planes):
-            out_ref[pl.ds((z * slabs + s) * comps, comps), :] = part[z * comps : (z + 1) * comps]
+            out_ref[pl.ds((z * slabs + s) * chunk, chunk), :] = part[z * chunk : (z + 1) * chunk]
 
 
 def sweep_kernel(steps, step_ref, y_ref, x_ref, excess_ref, *refs):
@@ -319,21 +307,19 @@
         scratch=[pltpu.VMEM((2 * TILE, width), jnp.float32)], flops=work, bytes_accessed=moved_bytes,
     )(step, field, head, ready, edge, *tables)
 
-    core, half = (lax.axis_index(axis).astype(jnp.int32).reshape(1) for axis in ("c", "xh"))
-    swap = [(0, 1), (1, 0)]
+    core = lax.axis_index("c").astype(jnp.int32).reshape(1)
+    planes = lax.axis_size("z")
 
     def solve(block, shift):
-        own, end = call(
-            functools.partial(spectrum_kernel, slabs), [plane, gains], [VMEM] * (2 + len(tables)),
+        own = call(
+            functools.partial(spectrum_kernel, slabs, planes), plane, [VMEM] * (1 + len(tables)),
             flops=work, bytes_accessed=moved_bytes,
-        )(exchange(block), gain, *tables)
-        same = lax.ppermute(end, "xh", swap)
-        cross = lax.ppermute(end, ("xh", "c"), [(i, 3 - i) for i in range(4)])
-        other = lax.ppermute(own, "c", swap)
+        )(exchange(block), *tables)
+        other = lax.ppermute(own, "c", [(0, 1), (1, 0)])
         return exchange(call(
-            functools.partial(solve_kernel, slabs, shift), turned,
-            [SMEM] * 2 + [VMEM] * (5 + len(tables)), flops=work, bytes_accessed=moved_bytes,
-        )(core, half, own, other, same, cross, gain, *tables))
+            functools.partial(solve_kernel, slabs, planes, shift), turned,
+            [SMEM] + [VMEM] * (3 + len(tables)), flops=work, bytes_accessed=moved_bytes,
+        )(core, own, other, gain, *tables))
 
     error, first = call(
         functools.partial(sweep_kernel, steps), [turned, plane], [SMEM] + [VMEM] * (3 + len(tables)),

time: 126 us -> 127 us (level)
  the two profiles are of different devices: /device:TPU:2 before, /device:TPU:1 now
where the time goes in v6:
time: 127 us; the launch traced here: 124 us
  blocking collectives  100 us (79%)
  starting transfers between devices  10.8 us (9%)
  Pallas kernels  9.36 us (7%)
  waiting for transfers between devices  4.1 us (3%)
    all_to_all x4, blocking collectives, exchange(): lax.all_to_all(block.reshape(peers, comps, rows), GROUP, split_axis=0, co...  100 us
    ppermute x2, starting transfers between devices, solve(): other = lax.ppermute(own, 'c', [(0, 1), (1, 0)])  8.55 us
    ppermute x2, waiting for transfers between devices, solve(): other = lax.ppermute(own, 'c', [(0, 1), (1, 0)])  3.07 us
    pallas_call x1, Pallas kernels, local(): call(functools.partial(load_kernel, steps, SHIFT), [plane, strip, plane,...  2.64 us
  transfers between devices with their start and end apart: 3, of which 3 were waited for; matrix products, arithmetic and copies ran while one was open for 0% of the time, Pallas kernels for 2%

profile of v6, /device:TPU:1, one launch (start us, length us, event | category | flops | bytes accessed | tf_op | source)
XLA Modules:
  0.0 124.5 jit_solution(3813433868018311646)
XLA Ops:
  0.0 0.9 shard_map.83
  0.9 2.2 %collective-permute-start = (f32[8,1024]{1,0:T(8,128)S(1)}, f32[8,1024]{1,0:T(8,128)S(1)}, u32[]{:S(2)}, u32[]{:S(2)}) collective-permute-start(f32[8,1024]{1,0:T(8,128)S(1)} %shard_map.83), channel_id=1, source_target_pairs={{0,1},{1,2},{2,3},{3,4},{4,5},{5,6},{6,7},{7,0},{8,9},{9,10},{10,1... | collective-permute-start | bytes 98312 | tf_op jit(solution)/shard_map/ppermute | solution.py:296
  3.1 2.6 %shard_map.82 = (f32[128,1024]{1,0:T(8,128)S(1)}, f32[8,1024]{1,0:T(8,128)S(1)}, f32[128,1024]{1,0:T(8,128)S(1)}, f32[128,1024]{1,0:T(8,128)S(1)}, f32[8,1024]{1...) custom-call(s32[1]{0:T(128)} %bitcast.1.step_ref, ...), custom_call_target="tpu_custom_call" | custom-call | flops 301989888 | bytes 4194304 | tf_op jit(solution)/shard_map/pallas_call | solution.py:297
  5.8 1.0 collective-permute-done.edge_ref
  6.8 0.6 shard_map.84
  7.4 29.8 %all_to_all.20 = f32[128,8,128]{2,1,0:T(8,128)S(1)} all-to-all(f32[128,8,128]{2,1,0:T(8,128)S(1)} %bitcast.19), channel_id=1, replica_groups=mesh['xh'=2,'z'=8,'c'=2,'xl'=2,'y'=4] {'z','xl','y','xh'}, dimensions={0} | all-to-all | bytes 1048576 | tf_op jit(solution)/shard_map/all_to_all | solution.py:281
  37.2 0.5 shard_map.85.own_ref
  37.7 3.9 %collective-permute-start.1 = (f32[128,1024]{1,0:T(8,128)S(1)}, f32[128,1024]{1,0:T(8,128)S(1)}, u32[]{:S(2)}, u32[]{:S(2)}) collective-permute-start(f32[128,1024]{1,0:T(8,128)S(1)} %shard_map.85.own_ref), channel_id=1, source_target_pairs={{0,8},{8,0},{1,9},{9,1},{2,10},{10,2},{3,11},{11,3},{4,12},{12,4},... | collective-permute-start | bytes 1572872 | tf_op jit(solution)/shard_map/ppermute | solution.py:318
  41.6 1.5 %collective-permute-done.1.other_ref = f32[128,1024]{1,0:T(8,128)S(1)} collective-permute-done((f32[128,1024]{1,0:T(8,128)S(1)}, f32[128,1024]{1,0:T(8,128)S(1)}, u32[]{:S(2)}, u32[]{:S(2)}) %collective-permute-start.1) | collective-permute-done | bytes 524320 | tf_op jit(solution)/shard_map/ppermute | solution.py:318
  43.2 0.9 shard_map.86
  44.1 23.4 %all_to_all.21 = f32[128,8,128]{2,1,0:T(8,128)S(1)} all-to-all(f32[128,8,128]{2,1,0:T(8,128)S(1)} %bitcast.20), channel_id=1, replica_groups=mesh['xh'=2,'z'=8,'c'=2,'xl'=2,'y'=4] {'z','xl','y','xh'}, dimensions={0} | all-to-all | bytes 1048576 | tf_op jit(solution)/shard_map/all_to_all | solution.py:281
  67.4 1.2 shard_map.87
  68.6 23.5 %all_to_all.22 = f32[128,8,128]{2,1,0:T(8,128)S(1)} all-to-all(f32[128,8,128]{2,1,0:T(8,128)S(1)} %bitcast.21), channel_id=1, replica_groups=mesh['xh'=2,'z'=8,'c'=2,'xl'=2,'y'=4] {'z','xl','y','xh'}, dimensions={0} | all-to-all | bytes 1048576 | tf_op jit(solution)/shard_map/all_to_all | solution.py:281
  92.2 0.5 shard_map.88.own_ref
  92.7 4.6 %collective-permute-start.2 = (f32[128,1024]{1,0:T(8,128)S(1)}, f32[128,1024]{1,0:T(8,128)S(1)}, u32[]{:S(2)}, u32[]{:S(2)}) collective-permute-start(f32[128,1024]{1,0:T(8,128)S(1)} %shard_map.88.own_ref), channel_id=1, source_target_pairs={{0,8},{8,0},{1,9},{9,1},{2,10},{10,2},{3,11},{11,3},{4,12},{12,4},... | collective-permute-start | bytes 1572872 | tf_op jit(solution)/shard_map/ppermute | solution.py:318
  97.3 1.5 %collective-permute-done.2.other_ref = f32[128,1024]{1,0:T(8,128)S(1)} collective-permute-done((f32[128,1024]{1,0:T(8,128)S(1)}, f32[128,1024]{1,0:T(8,128)S(1)}, u32[]{:S(2)}, u32[]{:S(2)}) %collective-permute-start.2) | collective-permute-done | bytes 524320 | tf_op jit(solution)/shard_map/ppermute | solution.py:318
  98.8 0.7 shard_map.89
  99.6 23.5 %all_to_all.23 = f32[128,8,128]{2,1,0:T(8,128)S(1)} all-to-all(f32[128,8,128]{2,1,0:T(8,128)S(1)} %bitcast.18), channel_id=1, replica_groups=mesh['xh'=2,'z'=8,'c'=2,'xl'=2,'y'=4] {'z','xl','y','xh'}, dimensions={0} | all-to-all | bytes 1048576 | tf_op jit(solution)/shard_map/all_to_all | solution.py:281
  123.1 1.4 %shard_map.90 = f32[128,1024]{1,0:T(8,128)} custom-call(f32[1024,128]{1,0:T(8,128)S(1)} %bitcast.17, f32[128,1024]{1,0:T(8,128)S(1)} %get-tuple-element.26.first_ref, bf16[256,512]{1,0:T(8,128)(2,1)S(1)} %get-tuple-element.19.refs_0_, bf16[256,512]{1,0:T(8,128)(2,1)S(1)} %get-tuple-element.20.refs_1_, bf16[512,512]{1,0:T(8,128)(2,1)S(1)} %get-tuple-element.21.refs_2_, ...), custom_call_target="tpu_custom_call" | custom-call | flops 301989888 | bytes 4194304 | tf_op jit(solution)/shard_map/pallas_call | solution.py:328
Async XLA Ops:
  0.9 5.9 %collective-permute-start = (f32[8,1024]{1,0:T(8,128)S(1)}, f32[8,1024]{1,0:T(8,128)S(1)}, u32[]{:S(2)}, u32[]{:S(2)}) collective-permute-start(f32[8,1024]{1,0:T(8,128)S(1)} %shard_map.83), channel_id=1, source_target_pairs={{0,1},{1,2},{2,3},{3,4},{4,5},{5,6},{6,7},{7,0},{8,9},{9,10},{10,1... | collective-permute-start | bytes 98312 | tf_op jit(solution)/shard_map/ppermute | solution.py:296
  37.7 5.5 %collective-permute-start.1 = (f32[128,1024]{1,0:T(8,128)S(1)}, f32[128,1024]{1,0:T(8,128)S(1)}, u32[]{:S(2)}, u32[]{:S(2)}) collective-permute-start(f32[128,1024]{1,0:T(8,128)S(1)} %shard_map.85.own_ref), channel_id=1, source_target_pairs={{0,8},{8,0},{1,9},{9,1},{2,10},{10,2},{3,11},{11,3},{4,12},{12,4},... | collective-permute-start | bytes 1572872 | tf_op jit(solution)/shard_map/ppermute | solution.py:318
  92.7 6.2 %collective-permute-start.2 = (f32[128,1024]{1,0:T(8,128)S(1)}, f32[128,1024]{1,0:T(8,128)S(1)}, u32[]{:S(2)}, u32[]{:S(2)}) collective-permute-start(f32[128,1024]{1,0:T(8,128)S(1)} %shard_map.88.own_ref), channel_id=1, source_target_pairs={{0,8},{8,0},{1,9},{9,1},{2,10},{10,2},{3,11},{11,3},{4,12},{12,4},... | collective-permute-start | bytes 1572872 | tf_op jit(solution)/shard_map/ppermute | solution.py:318

commit v7 on v4

--- a/solution.py
+++ b/solution.py
@@ -19,6 +19,7 @@
 SLAB = ("xl", "y")
 GROUP = ("xl", "y", "z", "c", "xh")
 TILE = 8
+LANES = 128
 SHIFT = 2
 VMEM = pl.BlockSpec(memory_space=pltpu.VMEM)
 SMEM = pl.BlockSpec(memory_space=pltpu.SMEM)
@@ -157,8 +158,14 @@
     tables = refs[count + 5 : 2 * count + 5]
     source_ref, forcing_ref, initial_ref, levels_ref, sems = refs[2 * count + 5 :]
     copies = start_all(
-        [(x_hbm, x_ref), (levels_hbm, levels_ref), (forcing_hbm, forcing_ref), (initial_hbm, initial_ref)]
+        [(x_hbm, x_ref), (levels_hbm, levels_ref), (forcing_hbm, forcing_ref)]
         + list(zip(tables_hbm, tables)), sems)
+    late = pltpu.make_async_copy(initial_hbm, initial_ref, sems.at[len(copies)])
+
+    @pl.when(step_ref[0] == 0)
+    def _():
+        late.start()
+
     shape = gain_ref.shape
     comps = shape[0] // 2
     lane = lax.broadcasted_iota(jnp.int32, shape, 1)
@@ -172,17 +179,17 @@
     excess, terms = own_terms(x, forcing_ref[...], levels_ref[...])
     excess_ref[...] = excess
     source_ref[...] = terms
-    copies[3].wait()
 
     @pl.when(step_ref[0] == 0)
     def _():
+        late.wait()
         source_ref[...] += initial_ref[...]
 
     head_ref[...] = source_ref[: head_ref.shape[0]]
     add_rows(x, step_ref[0] == steps - 1, source_ref)
-    for copy in copies[4:]:
+    for copy in copies[3:]:
         copy.wait()
-    ready_ref[...] = transform(roll(source_ref[...], shift, 0), read(tables))
+    ready_ref[...] = transform(roll(source_ref[...], shift, 0), read(tables)).T
 
 
 def source_kernel(steps, shift, step_ref, x_ref, head_ref, ready_ref, edge_ref, *refs):
@@ -193,16 +200,12 @@
     source_ref[...] = jnp.concatenate([roll(edge, tile // 2, 0), head_ref[...]], axis=0)
     add_rows(x, step_ref[0] == steps - 1, source_ref)
     first = transform(roll(source_ref[...], shift - tile, 0), read(tables))
-    out_ref[...] = jnp.concatenate([first[:tile], ready_ref[tile:]], axis=0).T
-
-
-def solve_kernel(slabs, steps, shift, x_ref, gain_ref, *refs):
-    tables, out_ref = read(refs[:-1]), refs[-1]
-    rows = x_ref.shape[0] // slabs
-    fields = jnp.concatenate([x_ref[pl.ds(s * rows, rows), :] for s in range(slabs)], axis=1)
-    spectrum = transform(fields, tables)
-    width = spectrum.shape[1]
-    gain = gain_ref[...]
+    out_ref[...] = ready_ref[...]
+    out_ref[:, :tile] = first.T[:, :tile]
+
+
+def circulate(block, gain, steps):
+    rows, lanes = block.shape
     powers = [gain]
     while len(powers) < steps.bit_length():
         powers.append(powers[-1] * powers[-1])
@@ -210,24 +213,30 @@
     pack = gain.shape[0]
     half = pack // 2
     groups = rows // pack
-    lane_row = lax.broadcasted_iota(jnp.int32, (1, pack, width), 1)
-    u = spectrum.reshape(groups, pack, width) * start[None]
-
-    def around(block):
-        turned = roll(block.reshape(-1, width), half, 0).reshape(block.shape)
-        if block.shape[0] > 1:
-            other = roll(block.reshape(-1, width), -half, 0).reshape(block.shape)
-            turned = jnp.where(lane_row < half, other, turned)
-        return jnp.where(lane_row < half, CIRCULANT_ALPHA, 1.0) * turned
-
+    weight = jnp.where(
+        lax.broadcasted_iota(jnp.int32, (pack, lanes), 0) < half, CIRCULANT_ALPHA, 1.0
+    )
+    u = [block[i * pack : (i + 1) * pack] * start for i in range(groups)]
     for j in range(steps.bit_length() - 1):
         k = 1 << j
-        if k < groups:
-            moved = jnp.concatenate([around(u[groups - k :]), u[: groups - k]], axis=0)
-        else:
-            moved = around(u)
-        u = u + powers[j][None] * moved
-    result = restore(u.reshape(rows, width), tables)
+        around = [weight * roll(part, half, 0) for part in u[groups - min(k, groups) :]]
+        moved = around + u[: groups - len(around)]
+        u = [part + powers[j] * other for part, other in zip(u, moved)]
+    return jnp.concatenate(u, axis=0)
+
+
+def solve_kernel(slabs, steps, shift, x_ref, gain_ref, *refs):
+    tables, out_ref = read(refs[:-1]), refs[-1]
+    rows = x_ref.shape[0] // slabs
+    fields = jnp.concatenate([x_ref[pl.ds(s * rows, rows), :] for s in range(slabs)], axis=1)
+    spectrum = transform(fields, tables)
+    width = spectrum.shape[1]
+    lanes = min(LANES, width)
+    u = jnp.concatenate(
+        [circulate(spectrum[:, i : i + lanes], gain_ref[:, i : i + lanes], steps)
+         for i in range(0, width, lanes)], axis=1
+    )
+    result = restore(u, tables)
     if shift:
         result = roll(result, -shift, 1)
     for s in range(slabs):
@@ -293,7 +302,7 @@
     edge = lax.ppermute(edge, SLAB, [(i, (i + 1) % slabs) for i in range(slabs)])
     field, head, ready, excess, gain, *tables = call(
         functools.partial(load_kernel, steps, SHIFT),
-        [plane, strip, plane, plane, gains] + [jax.ShapeDtypeStruct(t.shape, t.dtype) for t in tables],
+        [plane, strip, turned, plane, gains] + [jax.ShapeDtypeStruct(t.shape, t.dtype) for t in tables],
         [SMEM] * 2 + [HBM] * (4 + len(tables)),
         scratch=[pltpu.VMEM((rows, width), kind) for kind in [jnp.float32] + buffers]
         + [pltpu.SemaphoreType.DMA((4 + len(tables),))],

time: 124 us -> 124 us (level)
  no operation moved by 1% of the time
where the time goes in v7:
time: 124 us
  blocking collectives  111 us (90%)
  Pallas kernels  9.04 us (7%)
  starting transfers between devices  2.2 us (2%)
    all_to_all x4, blocking collectives, exchange(): lax.all_to_all(block.reshape(devices, comps, rows), GROUP, split_axis=0,...  111 us
    pallas_call x1, Pallas kernels, local(): call(functools.partial(load_kernel, steps, SHIFT), [plane, strip, turned,...  2.74 us
  transfers between devices with their start and end apart: 1, of which 1 were waited for; matrix products, arithmetic and copies ran while one was open for 0% of the time, Pallas kernels for 2%

profile of v7, /device:TPU:1, one launch (start us, length us, event | category | flops | bytes accessed | tf_op | source)
XLA Modules:
  0.0 123.6 jit_solution(6575210913617851529)
XLA Ops:
  0.0 0.9 shard_map.83
  0.9 2.2 %collective-permute-start = (f32[8,1024]{1,0:T(8,128)S(1)}, f32[8,1024]{1,0:T(8,128)S(1)}, u32[]{:S(2)}, u32[]{:S(2)}) collective-permute-start(f32[8,1024]{1,0:T(8,128)S(1)} %shard_map.83), channel_id=1, source_target_pairs={{0,1},{1,2},{2,3},{3,4},{4,5},{5,6},{6,7},{7,0},{8,9},{9,10},{10,1... | collective-permute-start | bytes 98312 | tf_op jit(solution)/shard_map/ppermute | solution.py:302
  3.1 2.7 %shard_map.82 = (f32[128,1024]{1,0:T(8,128)S(1)}, f32[8,1024]{1,0:T(8,128)S(1)}, f32[1024,128]{1,0:T(8,128)S(1)}, f32[128,1024]{1,0:T(8,128)S(1)}, f32[8,1024]{1...) custom-call(s32[1]{0:T(128)} %bitcast.step_ref, ...), custom_call_target="tpu_custom_call" | custom-call | flops 301989888 | bytes 4194304 | tf_op jit(solution)/shard_map/pallas_call | solution.py:303
  5.9 0.9 collective-permute-done.edge_ref
  6.8 0.6 shard_map.84
  7.4 34.3 %all_to_all.20 = f32[256,4,128]{2,1,0:T(4,128)S(1)} all-to-all(f32[256,4,128]{2,1,0:T(4,128)S(1)} %bitcast.15), channel_id=1, replica_groups=mesh['xh'=2,'z'=8,'c'=2,'xl'=2,'y'=4] {'xl','y','z','c','xh'}, dimensions={0} | all-to-all | bytes 1048576 | tf_op jit(solution)/shard_map/all_to_all | solution.py:287
  41.7 1.2 shard_map.85
  42.9 25.7 %all_to_all.21 = f32[256,4,128]{2,1,0:T(4,128)S(1)} all-to-all(f32[256,4,128]{2,1,0:T(4,128)S(1)} %bitcast.19), channel_id=1, replica_groups=mesh['xh'=2,'z'=8,'c'=2,'xl'=2,'y'=4] {'xl','y','z','c','xh'}, dimensions={0} | all-to-all | bytes 1048576 | tf_op jit(solution)/shard_map/all_to_all | solution.py:287
  68.6 1.2 shard_map.86
  69.8 25.7 %all_to_all.22 = f32[256,4,128]{2,1,0:T(4,128)S(1)} all-to-all(f32[256,4,128]{2,1,0:T(4,128)S(1)} %bitcast.20), channel_id=1, replica_groups=mesh['xh'=2,'z'=8,'c'=2,'xl'=2,'y'=4] {'xl','y','z','c','xh'}, dimensions={0} | all-to-all | bytes 1048576 | tf_op jit(solution)/shard_map/all_to_all | solution.py:287
  95.5 1.0 shard_map.87
  96.5 25.7 %all_to_all.23 = f32[256,4,128]{2,1,0:T(4,128)S(1)} all-to-all(f32[256,4,128]{2,1,0:T(4,128)S(1)} %bitcast.17), channel_id=1, replica_groups=mesh['xh'=2,'z'=8,'c'=2,'xl'=2,'y'=4] {'xl','y','z','c','xh'}, dimensions={0} | all-to-all | bytes 1048576 | tf_op jit(solution)/shard_map/all_to_all | solution.py:287
  122.2 1.4 %shard_map.88 = f32[128,1024]{1,0:T(8,128)} custom-call(f32[1024,128]{1,0:T(8,128)S(1)} %bitcast.14, f32[128,1024]{1,0:T(8,128)S(1)} %get-tuple-element.26.first_ref, bf16[256,512]{1,0:T(8,128)(2,1)S(1)} %get-tuple-element.19.refs_0_, bf16[256,512]{1,0:T(8,128)(2,1)S(1)} %get-tuple-element.20.refs_1_, bf16[512,512]{1,0:T(8,128)(2,1)S(1)} %get-tuple-element.21.refs_2_, ...), custom_call_target="tpu_custom_call" | custom-call | flops 301989888 | bytes 4194304 | tf_op jit(solution)/shard_map/pallas_call | solution.py:326
Async XLA Ops:
  0.9 5.9 %collective-permute-start = (f32[8,1024]{1,0:T(8,128)S(1)}, f32[8,1024]{1,0:T(8,128)S(1)}, u32[]{:S(2)}, u32[]{:S(2)}) collective-permute-start(f32[8,1024]{1,0:T(8,128)S(1)} %shard_map.83), channel_id=1, source_target_pairs={{0,1},{1,2},{2,3},{3,4},{4,5},{5,6},{6,7},{7,0},{8,9},{9,10},{10,1... | collective-permute-start | bytes 98312 | tf_op jit(solution)/shard_map/ppermute | solution.py:302

commit v8 on v7

--- a/solution.py
+++ b/solution.py
@@ -55,8 +55,14 @@
 
 
 def from_right(block, table_high, table_low):
+    dims = ((1,), (0,))
+    count = block.shape[0]
+    if count <= TILE:
+        high = block.astype(jnp.bfloat16).astype(jnp.float32)
+        both = jnp.concatenate([high, block - high], axis=0).astype(jnp.bfloat16)
+        main, rest = product(both, table_high, dims), product(both, table_low, dims)
+        return main[:count] + main[count:] + rest[:count]
     high, low = pieces(block)
-    dims = ((1,), (0,))
     return product(high, table_high, dims) + product(low, table_high, dims) + product(high, table_low, dims)
 
 
@@ -199,9 +205,9 @@
     x = jnp.concatenate([edge, x_ref[:tile]], axis=0)
     source_ref[...] = jnp.concatenate([roll(edge, tile // 2, 0), head_ref[...]], axis=0)
     add_rows(x, step_ref[0] == steps - 1, source_ref)
-    first = transform(roll(source_ref[...], shift - tile, 0), read(tables))
+    first = transform(roll(source_ref[...], shift - tile, 0)[:tile], read(tables))
     out_ref[...] = ready_ref[...]
-    out_ref[:, :tile] = first.T[:, :tile]
+    out_ref[:, :tile] = first.T
 
 
 def circulate(block, gain, steps):

time: 124 us -> 124 us (level)
  no operation moved by 1% of the time
where the time goes in v8:
time: 124 us; the launch traced here: 123 us
  blocking collectives  111 us (90%)
  Pallas kernels  8.92 us (7%)
  starting transfers between devices  2.2 us (2%)
    all_to_all x4, blocking collectives, exchange(): lax.all_to_all(block.reshape(devices, comps, rows), GROUP, split_axis=0,...  111 us
    pallas_call x1, Pallas kernels, local(): call(functools.partial(load_kernel, steps, SHIFT), [plane, strip, turned,...  2.74 us
  transfers between devices with their start and end apart: 1, of which 1 were waited for; matrix products, arithmetic and copies ran while one was open for 0% of the time, Pallas kernels for 2%

profile of v8, /device:TPU:1, one launch (start us, length us, event | category | flops | bytes accessed | tf_op | source)
XLA Modules:
  0.0 123.5 jit_solution(9638755460655281881)
XLA Ops:
  0.0 0.9 shard_map.83
  0.9 2.2 %collective-permute-start = (f32[8,1024]{1,0:T(8,128)S(1)}, f32[8,1024]{1,0:T(8,128)S(1)}, u32[]{:S(2)}, u32[]{:S(2)}) collective-permute-start(f32[8,1024]{1,0:T(8,128)S(1)} %shard_map.83), channel_id=1, source_target_pairs={{0,1},{1,2},{2,3},{3,4},{4,5},{5,6},{6,7},{7,0},{8,9},{9,10},{10,1... | collective-permute-start | bytes 98312 | tf_op jit(solution)/shard_map/ppermute | solution.py:308
  3.1 2.7 %shard_map.82 = (f32[128,1024]{1,0:T(8,128)S(1)}, f32[8,1024]{1,0:T(8,128)S(1)}, f32[1024,128]{1,0:T(8,128)S(1)}, f32[128,1024]{1,0:T(8,128)S(1)}, f32[8,1024]{1...) custom-call(s32[1]{0:T(128)} %bitcast.step_ref, ...), custom_call_target="tpu_custom_call" | custom-call | flops 301989888 | bytes 4194304 | tf_op jit(solution)/shard_map/pallas_call | solution.py:309
  5.9 0.9 collective-permute-done.edge_ref
  6.8 0.4 shard_map.84
  7.3 34.3 %all_to_all.20 = f32[256,4,128]{2,1,0:T(4,128)S(1)} all-to-all(f32[256,4,128]{2,1,0:T(4,128)S(1)} %bitcast.15), channel_id=1, replica_groups=mesh['xh'=2,'z'=8,'c'=2,'xl'=2,'y'=4] {'xl','y','z','c','xh'}, dimensions={0} | all-to-all | bytes 1048576 | tf_op jit(solution)/shard_map/all_to_all | solution.py:293
  41.6 1.2 shard_map.85
  42.8 25.7 %all_to_all.21 = f32[256,4,128]{2,1,0:T(4,128)S(1)} all-to-all(f32[256,4,128]{2,1,0:T(4,128)S(1)} %bitcast.19), channel_id=1, replica_groups=mesh['xh'=2,'z'=8,'c'=2,'xl'=2,'y'=4] {'xl','y','z','c','xh'}, dimensions={0} | all-to-all | bytes 1048576 | tf_op jit(solution)/shard_map/all_to_all | solution.py:293
  68.5 1.2 shard_map.86
  69.7 25.7 %all_to_all.22 = f32[256,4,128]{2,1,0:T(4,128)S(1)} all-to-all(f32[256,4,128]{2,1,0:T(4,128)S(1)} %bitcast.20), channel_id=1, replica_groups=mesh['xh'=2,'z'=8,'c'=2,'xl'=2,'y'=4] {'xl','y','z','c','xh'}, dimensions={0} | all-to-all | bytes 1048576 | tf_op jit(solution)/shard_map/all_to_all | solution.py:293
  95.4 1.0 shard_map.87
  96.4 25.7 %all_to_all.23 = f32[256,4,128]{2,1,0:T(4,128)S(1)} all-to-all(f32[256,4,128]{2,1,0:T(4,128)S(1)} %bitcast.17), channel_id=1, replica_groups=mesh['xh'=2,'z'=8,'c'=2,'xl'=2,'y'=4] {'xl','y','z','c','xh'}, dimensions={0} | all-to-all | bytes 1048576 | tf_op jit(solution)/shard_map/all_to_all | solution.py:293
  122.1 1.4 %shard_map.88 = f32[128,1024]{1,0:T(8,128)} custom-call(f32[1024,128]{1,0:T(8,128)S(1)} %bitcast.14, f32[128,1024]{1,0:T(8,128)S(1)} %get-tuple-element.26.first_ref, bf16[256,512]{1,0:T(8,128)(2,1)S(1)} %get-tuple-element.19.refs_0_, bf16[256,512]{1,0:T(8,128)(2,1)S(1)} %get-tuple-element.20.refs_1_, bf16[512,512]{1,0:T(8,128)(2,1)S(1)} %get-tuple-element.21.refs_2_, ...), custom_call_target="tpu_custom_call" | custom-call | flops 301989888 | bytes 4194304 | tf_op jit(solution)/shard_map/pallas_call | solution.py:332
Async XLA Ops:
  0.9 5.9 %collective-permute-start = (f32[8,1024]{1,0:T(8,128)S(1)}, f32[8,1024]{1,0:T(8,128)S(1)}, u32[]{:S(2)}, u32[]{:S(2)}) collective-permute-start(f32[8,1024]{1,0:T(8,128)S(1)} %shard_map.83), channel_id=1, source_target_pairs={{0,1},{1,2},{2,3},{3,4},{4,5},{5,6},{6,7},{7,0},{8,9},{9,10},{10,1... | collective-permute-start | bytes 98312 | tf_op jit(solution)/shard_map/ppermute | solution.py:308

commit v9 on v8

--- a/solution.py
+++ b/solution.py
@@ -26,7 +26,7 @@
 HBM = pl.BlockSpec(memory_space=pltpu.HBM)
 
 
-def hartley_tables(length):
+def hartley_tables(length, shift=0):
     def parts(table):
         table = table / math.sqrt(length)
         high = table.astype(ml_dtypes.bfloat16)
@@ -34,6 +34,9 @@
 
     def cas(angle):
         return np.cos(angle) + np.sin(angle)
+
+    def moved(table, sign):
+        return np.concatenate([table[:, shift:], sign * table[:, :shift]], axis=1)
 
     quarter = np.arange(length // 4, dtype=np.int64)
     odd = 2 * quarter + 1
@@ -41,7 +44,7 @@
     twice = cas((odd[:, None] * odd[None, :] % length) * (2.0 * math.pi / length))
     odd = 2 * np.arange(length // 2, dtype=np.int64) + 1
     half = cas((odd[:, None] * odd[None, :] % (2 * length)) * (math.pi / length))
-    return parts(np.concatenate([whole, twice], axis=1)) + parts(half)
+    return parts(np.concatenate([moved(whole, 1), moved(twice, -1)], axis=1)) + parts(moved(half, -1))
 
 
 def pieces(block):
@@ -231,8 +234,9 @@
     return jnp.concatenate(u, axis=0)
 
 
-def solve_kernel(slabs, steps, shift, x_ref, gain_ref, *refs):
-    tables, out_ref = read(refs[:-1]), refs[-1]
+def solve_kernel(slabs, steps, x_ref, gain_ref, *refs):
+    count = len(refs) // 2
+    tables, inverse, out_ref = read(refs[:count]), read(refs[count:-1]), refs[-1]
     rows = x_ref.shape[0] // slabs
     fields = jnp.concatenate([x_ref[pl.ds(s * rows, rows), :] for s in range(slabs)], axis=1)
     spectrum = transform(fields, tables)
@@ -242,9 +246,7 @@
         [circulate(spectrum[:, i : i + lanes], gain_ref[:, i : i + lanes], steps)
          for i in range(0, width, lanes)], axis=1
     )
-    result = restore(u, tables)
-    if shift:
-        result = roll(result, -shift, 1)
+    result = restore(u, inverse)
     for s in range(slabs):
         out_ref[pl.ds(s * rows, rows), :] = result[:, s * rows : (s + 1) * rows]
 
@@ -280,6 +282,7 @@
     devices = steps * slabs
     comps = width // devices
     tables = [jnp.asarray(t) for t in hartley_tables(width)]
+    shifted = [jnp.asarray(t) for t in hartley_tables(width, SHIFT)]
     step = lax.axis_index(TIME).astype(jnp.int32).reshape(1)
     column = (lax.axis_index(GROUP) * comps).astype(jnp.int32).reshape(1)
     plane = jax.ShapeDtypeStruct((rows, width), jnp.float32)
@@ -319,19 +322,19 @@
         scratch=[pltpu.VMEM((2 * TILE, width), jnp.float32)], flops=work, bytes_accessed=moved_bytes,
     )(step, field, head, ready, edge, *tables)
 
-    def solve(block, shift):
+    def solve(block, inverse):
         return exchange(call(
-            functools.partial(solve_kernel, slabs, steps, shift), turned, [VMEM] * (2 + len(tables)),
+            functools.partial(solve_kernel, slabs, steps), turned, [VMEM] * (2 + 2 * len(tables)),
             flops=2 * work, bytes_accessed=moved_bytes,
-        )(exchange(block), gain, *tables))
+        )(exchange(block), gain, *tables, *inverse))
 
     error, first = call(
         functools.partial(sweep_kernel, steps), [turned, plane], [SMEM] + [VMEM] * (3 + len(tables)),
         flops=2 * work, bytes_accessed=moved_bytes,
-    )(step, solve(sent, SHIFT), field, excess, *tables)
+    )(step, solve(sent, shifted), field, excess, *tables)
     increment = call(
         finish_kernel, plane, [VMEM] * (2 + len(tables)), flops=work, bytes_accessed=moved_bytes
-    )(solve(error, 0), first, *tables)
+    )(solve(error, tables), first, *tables)
     return increment[None]
 
 

time: 124 us -> 123 us (level)
  no operation moved by 1% of the time
where the time goes in v9:
time: 123 us
  blocking collectives  111 us (90%)
  Pallas kernels  8.55 us (7%)
  starting transfers between devices  2.2 us (2%)
    all_to_all x4, blocking collectives, exchange(): lax.all_to_all(block.reshape(devices, comps, rows), GROUP, split_axis=0,...  111 us
    pallas_call x1, Pallas kernels, local(): call(functools.partial(load_kernel, steps, SHIFT), [plane, strip, turned,...  2.7 us
  transfers between devices with their start and end apart: 1, of which 1 were waited for; matrix products, arithmetic and copies ran while one was open for 0% of the time, Pallas kernels for 2%

profile of v9, /device:TPU:1, one launch (start us, length us, event | category | flops | bytes accessed | tf_op | source)
XLA Modules:
  0.0 123.2 jit_solution(11919046786807731158)
XLA Ops:
  0.0 0.9 shard_map.119
  0.9 2.2 %collective-permute-start = (f32[8,1024]{1,0:T(8,128)S(1)}, f32[8,1024]{1,0:T(8,128)S(1)}, u32[]{:S(2)}, u32[]{:S(2)}) collective-permute-start(f32[8,1024]{1,0:T(8,128)S(1)} %shard_map.119), channel_id=1, source_target_pairs={{0,1},{1,2},{2,3},{3,4},{4,5},{5,6},{6,7},{7,0},{8,9},{9,10},{10,1... | collective-permute-start | bytes 98312 | tf_op jit(solution)/shard_map/ppermute | solution.py:311
  3.1 2.7 %shard_map.118 = (f32[128,1024]{1,0:T(8,128)S(1)}, f32[8,1024]{1,0:T(8,128)S(1)}, f32[1024,128]{1,0:T(8,128)S(1)}, f32[128,1024]{1,0:T(8,128)S(1)}, f32[8,1024]{...) custom-call(s32[1]{0:T(128)} %bitcast.step_ref, ...), custom_call_target="tpu_custom_call" | custom-call | flops 301989888 | bytes 4194304 | tf_op jit(solution)/shard_map/pallas_call | solution.py:312
  5.9 1.0 collective-permute-done.edge_ref
  6.8 0.0 copy-start.2
  6.8 0.0 copy-start.3
  6.8 0.4 shard_map.120
  7.3 0.0 copy-start
  7.3 0.0 copy-start.1
  7.3 34.3 %all_to_all.20 = f32[256,4,128]{2,1,0:T(4,128)S(1)} all-to-all(f32[256,4,128]{2,1,0:T(4,128)S(1)} %bitcast.15), channel_id=1, replica_groups=mesh['xh'=2,'z'=8,'c'=2,'xl'=2,'y'=4] {'xl','y','z','c','xh'}, dimensions={0} | all-to-all | bytes 1048576 | tf_op jit(solution)/shard_map/all_to_all | solution.py:296
  41.6 0.0 copy-done.2
  41.6 0.0 copy-done.3
  41.6 0.0 copy-done
  41.6 0.0 copy-done.1
  41.6 1.0 shard_map.121
  42.6 25.7 %all_to_all.21 = f32[256,4,128]{2,1,0:T(4,128)S(1)} all-to-all(f32[256,4,128]{2,1,0:T(4,128)S(1)} %bitcast.17), channel_id=1, replica_groups=mesh['xh'=2,'z'=8,'c'=2,'xl'=2,'y'=4] {'xl','y','z','c','xh'}, dimensions={0} | all-to-all | bytes 1048576 | tf_op jit(solution)/shard_map/all_to_all | solution.py:296
  68.3 1.2 shard_map.122
  69.5 25.7 %all_to_all.22 = f32[256,4,128]{2,1,0:T(4,128)S(1)} all-to-all(f32[256,4,128]{2,1,0:T(4,128)S(1)} %bitcast.20), channel_id=1, replica_groups=mesh['xh'=2,'z'=8,'c'=2,'xl'=2,'y'=4] {'xl','y','z','c','xh'}, dimensions={0} | all-to-all | bytes 1048576 | tf_op jit(solution)/shard_map/all_to_all | solution.py:296
  95.2 1.0 shard_map.123
  96.1 25.7 %all_to_all.23 = f32[256,4,128]{2,1,0:T(4,128)S(1)} all-to-all(f32[256,4,128]{2,1,0:T(4,128)S(1)} %bitcast.19), channel_id=1, replica_groups=mesh['xh'=2,'z'=8,'c'=2,'xl'=2,'y'=4] {'xl','y','z','c','xh'}, dimensions={0} | all-to-all | bytes 1048576 | tf_op jit(solution)/shard_map/all_to_all | solution.py:296
  121.8 1.4 %shard_map.124 = f32[128,1024]{1,0:T(8,128)} custom-call(f32[1024,128]{1,0:T(8,128)S(1)} %bitcast.14, f32[128,1024]{1,0:T(8,128)S(1)} %get-tuple-element.26.first_ref, bf16[256,512]{1,0:T(8,128)(2,1)S(1)} %get-tuple-element.19.refs_0_.refs_4_, bf16[256,512]{1,0:T(8,128)(2,1)S(1)} %get-tuple-element.20.refs_1_.refs_5_, ...), custom_call_target="tpu_custom_call" | custom-call | flops 301989888 | bytes 4194304 | tf_op jit(solution)/shard_map/pallas_call | solution.py:335
Async XLA Ops:
  0.9 5.9 %collective-permute-start = (f32[8,1024]{1,0:T(8,128)S(1)}, f32[8,1024]{1,0:T(8,128)S(1)}, u32[]{:S(2)}, u32[]{:S(2)}) collective-permute-start(f32[8,1024]{1,0:T(8,128)S(1)} %shard_map.119), channel_id=1, source_target_pairs={{0,1},{1,2},{2,3},{3,4},{4,5},{5,6},{6,7},{7,0},{8,9},{9,10},{10,1... | collective-permute-start | bytes 98312 | tf_op jit(solution)/shard_map/ppermute | solution.py:311
  6.8 34.8 %copy-start.2 = (bf16[256,512]{1,0:T(8,128)(2,1)S(1)}, bf16[256,512]{1,0:T(8,128)(2,1)}, u32[]{:S(2)}) copy-start(bf16[256,512]{1,0:T(8,128)(2,1)} %constant.51.clone.refs_5_) | copy-start | bytes 786436
  6.8 34.8 %copy-start.3 = (bf16[256,512]{1,0:T(8,128)(2,1)S(1)}, bf16[256,512]{1,0:T(8,128)(2,1)}, u32[]{:S(2)}) copy-start(bf16[256,512]{1,0:T(8,128)(2,1)} %constant.50.clone.refs_4_) | copy-start | bytes 786436
  7.3 34.3 %copy-start = (bf16[512,512]{1,0:T(8,128)(2,1)S(1)}, bf16[512,512]{1,0:T(8,128)(2,1)}, u32[]{:S(2)}) copy-start(bf16[512,512]{1,0:T(8,128)(2,1)} %constant.53.clone.refs_7_) | copy-start | bytes 1572868
  7.3 34.3 %copy-start.1 = (bf16[512,512]{1,0:T(8,128)(2,1)S(1)}, bf16[512,512]{1,0:T(8,128)(2,1)}, u32[]{:S(2)}) copy-start(bf16[512,512]{1,0:T(8,128)(2,1)} %constant.52.clone.refs_6_) | copy-start | bytes 1572868

commit v10 on v9

--- a/solution.py
+++ b/solution.py
@@ -69,29 +69,49 @@
     return product(high, table_high, dims) + product(low, table_high, dims) + product(high, table_low, dims)
 
 
-def transform(block, tables):
+def pieces_of(block, tables):
     quarter_high, quarter_low, half_high, half_low = tables
     half = half_high.shape[0]
     quarter = half // 2
     left, right = block[:, :half], block[:, half:]
     even, odd = left + right, left - right
     left, right = even[:, :quarter], even[:, quarter:]
-    return jnp.concatenate([
+    return [
         from_right(left + right, quarter_high[:, :quarter], quarter_low[:, :quarter]),
         from_right(left - right, quarter_high[:, quarter:], quarter_low[:, quarter:]),
         from_right(odd, half_high, half_low),
-    ], axis=1)
-
-
-def restore(block, tables):
+    ]
+
+
+def transform(block, tables):
+    return jnp.concatenate(pieces_of(block, tables), axis=1)
+
+
+def transform_turned(block, tables, out_ref):
+    start = 0
+    for piece in pieces_of(block, tables):
+        out_ref[start : start + piece.shape[1]] = piece.T
+        start += piece.shape[1]
+
+
+def joined(first, second, third, tables):
     quarter_high, quarter_low, half_high, half_low = tables
-    half = half_high.shape[0]
-    quarter = half // 2
-    left = from_right(block[:, :quarter], quarter_high[:, :quarter], quarter_low[:, :quarter])
-    right = from_right(block[:, quarter:half], quarter_high[:, quarter:], quarter_low[:, quarter:])
-    odd = from_right(block[:, half:], half_high, half_low)
+    quarter = half_high.shape[0] // 2
+    left = from_right(first, quarter_high[:, :quarter], quarter_low[:, :quarter])
+    right = from_right(second, quarter_high[:, quarter:], quarter_low[:, quarter:])
+    odd = from_right(third, half_high, half_low)
     even = jnp.concatenate([left + right, left - right], axis=1)
     return jnp.concatenate([even + odd, even - odd], axis=1)
+
+
+def restore(block, tables):
+    half = tables[2].shape[0]
+    return joined(block[:, : half // 2], block[:, half // 2 : half], block[:, half:], tables)
+
+
+def restore_turned(ref, tables):
+    half = tables[2].shape[0]
+    return joined(ref[: half // 2].T, ref[half // 2 : half].T, ref[half:].T, tables)
 
 
 def read(tables):
@@ -198,7 +218,7 @@
     add_rows(x, step_ref[0] == steps - 1, source_ref)
     for copy in copies[3:]:
         copy.wait()
-    ready_ref[...] = transform(roll(source_ref[...], shift, 0), read(tables)).T
+    transform_turned(roll(source_ref[...], shift, 0), read(tables), ready_ref)
 
 
 def source_kernel(steps, shift, step_ref, x_ref, head_ref, ready_ref, edge_ref, *refs):
@@ -254,13 +274,13 @@
 def sweep_kernel(steps, step_ref, y_ref, x_ref, excess_ref, *refs):
     tables, (out_ref, first_ref) = read(refs[:-2]), refs[-2:]
     keep = jnp.where(step_ref[0] == steps - 1, 0.0, 1.0)
-    first = restore(y_ref[...].T, tables) - keep * x_ref[...]
+    first = restore_turned(y_ref, tables) - keep * x_ref[...]
     first_ref[...] = first
-    out_ref[...] = transform(excess_ref[...] * first, tables).T
+    transform_turned(excess_ref[...] * first, tables, out_ref)
 
 
 def finish_kernel(y_ref, first_ref, *refs):
-    refs[-1][...] = restore(y_ref[...].T, read(refs[:-1])) + first_ref[...]
+    refs[-1][...] = restore_turned(y_ref, read(refs[:-1])) + first_ref[...]
 
 
 def call(kernel, out_shapes, specs, scratch=(), flops=0, bytes_accessed=0):

time: 123 us -> 123 us (level)
  no operation moved by 1% of the time
where the time goes in v10:
time: 123 us
  blocking collectives  111 us (90%)
  Pallas kernels  8.55 us (7%)
  starting transfers between devices  2.2 us (2%)
    all_to_all x4, blocking collectives, exchange(): lax.all_to_all(block.reshape(devices, comps, rows), GROUP, split_axis=0,...  111 us
    pallas_call x1, Pallas kernels, local(): call(functools.partial(load_kernel, steps, SHIFT), [plane, strip, turned,...  2.7 us
  transfers between devices with their start and end apart: 1, of which 1 were waited for; matrix products, arithmetic and copies ran while one was open for 0% of the time, Pallas kernels for 2%

profile of v10, /device:TPU:1, one launch (start us, length us, event | category | flops | bytes accessed | tf_op | source)
XLA Modules:
  0.0 123.2 jit_solution(13426209569536317900)
XLA Ops:
  0.0 0.9 shard_map.119
  0.9 2.2 %collective-permute-start = (f32[8,1024]{1,0:T(8,128)S(1)}, f32[8,1024]{1,0:T(8,128)S(1)}, u32[]{:S(2)}, u32[]{:S(2)}) collective-permute-start(f32[8,1024]{1,0:T(8,128)S(1)} %shard_map.119), channel_id=1, source_target_pairs={{0,1},{1,2},{2,3},{3,4},{4,5},{5,6},{6,7},{7,0},{8,9},{9,10},{10,1... | collective-permute-start | bytes 98312 | tf_op jit(solution)/shard_map/ppermute | solution.py:331
  3.1 2.7 %shard_map.118 = (f32[128,1024]{1,0:T(8,128)S(1)}, f32[8,1024]{1,0:T(8,128)S(1)}, f32[1024,128]{1,0:T(8,128)S(1)}, f32[128,1024]{1,0:T(8,128)S(1)}, f32[8,1024]{...) custom-call(s32[1]{0:T(128)} %bitcast.step_ref, ...), custom_call_target="tpu_custom_call" | custom-call | flops 301989888 | bytes 4194304 | tf_op jit(solution)/shard_map/pallas_call | solution.py:332
  5.9 1.0 collective-permute-done.edge_ref
  6.8 0.0 copy-start.2
  6.8 0.0 copy-start.3
  6.8 0.4 shard_map.120
  7.3 0.0 copy-start
  7.3 0.0 copy-start.1
  7.3 34.3 %all_to_all.20 = f32[256,4,128]{2,1,0:T(4,128)S(1)} all-to-all(f32[256,4,128]{2,1,0:T(4,128)S(1)} %bitcast.15), channel_id=1, replica_groups=mesh['xh'=2,'z'=8,'c'=2,'xl'=2,'y'=4] {'xl','y','z','c','xh'}, dimensions={0} | all-to-all | bytes 1048576 | tf_op jit(solution)/shard_map/all_to_all | solution.py:316
  41.6 0.0 copy-done.2
  41.6 0.0 copy-done.3
  41.6 0.0 copy-done
  41.6 0.0 copy-done.1
  41.6 1.0 shard_map.121
  42.6 25.7 %all_to_all.21 = f32[256,4,128]{2,1,0:T(4,128)S(1)} all-to-all(f32[256,4,128]{2,1,0:T(4,128)S(1)} %bitcast.17), channel_id=1, replica_groups=mesh['xh'=2,'z'=8,'c'=2,'xl'=2,'y'=4] {'xl','y','z','c','xh'}, dimensions={0} | all-to-all | bytes 1048576 | tf_op jit(solution)/shard_map/all_to_all | solution.py:316
  68.3 1.2 shard_map.122
  69.5 25.7 %all_to_all.22 = f32[256,4,128]{2,1,0:T(4,128)S(1)} all-to-all(f32[256,4,128]{2,1,0:T(4,128)S(1)} %bitcast.20), channel_id=1, replica_groups=mesh['xh'=2,'z'=8,'c'=2,'xl'=2,'y'=4] {'xl','y','z','c','xh'}, dimensions={0} | all-to-all | bytes 1048576 | tf_op jit(solution)/shard_map/all_to_all | solution.py:316
  95.2 1.0 shard_map.123
  96.1 25.7 %all_to_all.23 = f32[256,4,128]{2,1,0:T(4,128)S(1)} all-to-all(f32[256,4,128]{2,1,0:T(4,128)S(1)} %bitcast.19), channel_id=1, replica_groups=mesh['xh'=2,'z'=8,'c'=2,'xl'=2,'y'=4] {'xl','y','z','c','xh'}, dimensions={0} | all-to-all | bytes 1048576 | tf_op jit(solution)/shard_map/all_to_all | solution.py:316
  121.8 1.4 %shard_map.124 = f32[128,1024]{1,0:T(8,128)} custom-call(f32[1024,128]{1,0:T(8,128)S(1)} %bitcast.14, f32[128,1024]{1,0:T(8,128)S(1)} %get-tuple-element.26.first_ref, bf16[256,512]{1,0:T(8,128)(2,1)S(1)} %get-tuple-element.19.refs_0_.refs_4_, bf16[256,512]{1,0:T(8,128)(2,1)S(1)} %get-tuple-element.20.refs_1_.refs_5_, ...), custom_call_target="tpu_custom_call" | custom-call | flops 301989888 | bytes 4194304 | tf_op jit(solution)/shard_map/pallas_call | solution.py:355
Async XLA Ops:
  0.9 5.9 %collective-permute-start = (f32[8,1024]{1,0:T(8,128)S(1)}, f32[8,1024]{1,0:T(8,128)S(1)}, u32[]{:S(2)}, u32[]{:S(2)}) collective-permute-start(f32[8,1024]{1,0:T(8,128)S(1)} %shard_map.119), channel_id=1, source_target_pairs={{0,1},{1,2},{2,3},{3,4},{4,5},{5,6},{6,7},{7,0},{8,9},{9,10},{10,1... | collective-permute-start | bytes 98312 | tf_op jit(solution)/shard_map/ppermute | solution.py:331
  6.8 34.8 %copy-start.2 = (bf16[256,512]{1,0:T(8,128)(2,1)S(1)}, bf16[256,512]{1,0:T(8,128)(2,1)}, u32[]{:S(2)}) copy-start(bf16[256,512]{1,0:T(8,128)(2,1)} %constant.51.clone.refs_5_) | copy-start | bytes 786436
  6.8 34.8 %copy-start.3 = (bf16[256,512]{1,0:T(8,128)(2,1)S(1)}, bf16[256,512]{1,0:T(8,128)(2,1)}, u32[]{:S(2)}) copy-start(bf16[256,512]{1,0:T(8,128)(2,1)} %constant.50.clone.refs_4_) | copy-start | bytes 786436
  7.3 34.3 %copy-start = (bf16[512,512]{1,0:T(8,128)(2,1)S(1)}, bf16[512,512]{1,0:T(8,128)(2,1)}, u32[]{:S(2)}) copy-start(bf16[512,512]{1,0:T(8,128)(2,1)} %constant.53.clone.refs_7_) | copy-start | bytes 1572868
  7.3 34.3 %copy-start.1 = (bf16[512,512]{1,0:T(8,128)(2,1)S(1)}, bf16[512,512]{1,0:T(8,128)(2,1)}, u32[]{:S(2)}) copy-start(bf16[512,512]{1,0:T(8,128)(2,1)} %constant.52.clone.refs_6_) | copy-start | bytes 1572868

commit v11 on v9

--- a/solution.py
+++ b/solution.py
@@ -19,7 +19,7 @@
 SLAB = ("xl", "y")
 GROUP = ("xl", "y", "z", "c", "xh")
 TILE = 8
-LANES = 128
+LANES = 256
 SHIFT = 2
 VMEM = pl.BlockSpec(memory_space=pltpu.VMEM)
 SMEM = pl.BlockSpec(memory_space=pltpu.SMEM)

time: 123 us -> 123 us (level)
  no operation moved by 1% of the time
where the time goes in v11:
time: 123 us
  blocking collectives  111 us (90%)
  Pallas kernels  8.55 us (7%)
  starting transfers between devices  2.2 us (2%)
    all_to_all x4, blocking collectives, exchange(): lax.all_to_all(block.reshape(devices, comps, rows), GROUP, split_axis=0,...  111 us
    pallas_call x1, Pallas kernels, local(): call(functools.partial(load_kernel, steps, SHIFT), [plane, strip, turned,...  2.7 us
  transfers between devices with their start and end apart: 1, of which 1 were waited for; matrix products, arithmetic and copies ran while one was open for 0% of the time, Pallas kernels for 2%

profile of v11, /device:TPU:1, one launch (start us, length us, event | category | flops | bytes accessed | tf_op | source)
XLA Modules:
  0.0 123.2 jit_solution(11919046786807731158)
XLA Ops:
  0.0 0.9 shard_map.119
  0.9 2.2 %collective-permute-start = (f32[8,1024]{1,0:T(8,128)S(1)}, f32[8,1024]{1,0:T(8,128)S(1)}, u32[]{:S(2)}, u32[]{:S(2)}) collective-permute-start(f32[8,1024]{1,0:T(8,128)S(1)} %shard_map.119), channel_id=1, source_target_pairs={{0,1},{1,2},{2,3},{3,4},{4,5},{5,6},{6,7},{7,0},{8,9},{9,10},{10,1... | collective-permute-start | bytes 98312 | tf_op jit(solution)/shard_map/ppermute | solution.py:311
  3.1 2.7 %shard_map.118 = (f32[128,1024]{1,0:T(8,128)S(1)}, f32[8,1024]{1,0:T(8,128)S(1)}, f32[1024,128]{1,0:T(8,128)S(1)}, f32[128,1024]{1,0:T(8,128)S(1)}, f32[8,1024]{...) custom-call(s32[1]{0:T(128)} %bitcast.step_ref, ...), custom_call_target="tpu_custom_call" | custom-call | flops 301989888 | bytes 4194304 | tf_op jit(solution)/shard_map/pallas_call | solution.py:312
  5.9 1.0 collective-permute-done.edge_ref
  6.8 0.0 copy-start.2
  6.8 0.0 copy-start.3
  6.8 0.4 shard_map.120
  7.3 0.0 copy-start
  7.3 0.0 copy-start.1
  7.3 34.3 %all_to_all.20 = f32[256,4,128]{2,1,0:T(4,128)S(1)} all-to-all(f32[256,4,128]{2,1,0:T(4,128)S(1)} %bitcast.15), channel_id=1, replica_groups=mesh['xh'=2,'z'=8,'c'=2,'xl'=2,'y'=4] {'xl','y','z','c','xh'}, dimensions={0} | all-to-all | bytes 1048576 | tf_op jit(solution)/shard_map/all_to_all | solution.py:296
  41.6 0.0 copy-done.2
  41.6 0.0 copy-done.3
  41.6 0.0 copy-done
  41.6 0.0 copy-done.1
  41.6 1.0 shard_map.121
  42.6 25.7 %all_to_all.21 = f32[256,4,128]{2,1,0:T(4,128)S(1)} all-to-all(f32[256,4,128]{2,1,0:T(4,128)S(1)} %bitcast.17), channel_id=1, replica_groups=mesh['xh'=2,'z'=8,'c'=2,'xl'=2,'y'=4] {'xl','y','z','c','xh'}, dimensions={0} | all-to-all | bytes 1048576 | tf_op jit(solution)/shard_map/all_to_all | solution.py:296
  68.3 1.2 shard_map.122
  69.5 25.7 %all_to_all.22 = f32[256,4,128]{2,1,0:T(4,128)S(1)} all-to-all(f32[256,4,128]{2,1,0:T(4,128)S(1)} %bitcast.20), channel_id=1, replica_groups=mesh['xh'=2,'z'=8,'c'=2,'xl'=2,'y'=4] {'xl','y','z','c','xh'}, dimensions={0} | all-to-all | bytes 1048576 | tf_op jit(solution)/shard_map/all_to_all | solution.py:296
  95.2 1.0 shard_map.123
  96.1 25.7 %all_to_all.23 = f32[256,4,128]{2,1,0:T(4,128)S(1)} all-to-all(f32[256,4,128]{2,1,0:T(4,128)S(1)} %bitcast.19), channel_id=1, replica_groups=mesh['xh'=2,'z'=8,'c'=2,'xl'=2,'y'=4] {'xl','y','z','c','xh'}, dimensions={0} | all-to-all | bytes 1048576 | tf_op jit(solution)/shard_map/all_to_all | solution.py:296
  121.8 1.4 %shard_map.124 = f32[128,1024]{1,0:T(8,128)} custom-call(f32[1024,128]{1,0:T(8,128)S(1)} %bitcast.14, f32[128,1024]{1,0:T(8,128)S(1)} %get-tuple-element.26.first_ref, bf16[256,512]{1,0:T(8,128)(2,1)S(1)} %get-tuple-element.19.refs_0_.refs_4_, bf16[256,512]{1,0:T(8,128)(2,1)S(1)} %get-tuple-element.20.refs_1_.refs_5_, ...), custom_call_target="tpu_custom_call" | custom-call | flops 301989888 | bytes 4194304 | tf_op jit(solution)/shard_map/pallas_call | solution.py:335
Async XLA Ops:
  0.9 5.9 %collective-permute-start = (f32[8,1024]{1,0:T(8,128)S(1)}, f32[8,1024]{1,0:T(8,128)S(1)}, u32[]{:S(2)}, u32[]{:S(2)}) collective-permute-start(f32[8,1024]{1,0:T(8,128)S(1)} %shard_map.119), channel_id=1, source_target_pairs={{0,1},{1,2},{2,3},{3,4},{4,5},{5,6},{6,7},{7,0},{8,9},{9,10},{10,1... | collective-permute-start | bytes 98312 | tf_op jit(solution)/shard_map/ppermute | solution.py:311
  6.8 34.8 %copy-start.2 = (bf16[256,512]{1,0:T(8,128)(2,1)S(1)}, bf16[256,512]{1,0:T(8,128)(2,1)}, u32[]{:S(2)}) copy-start(bf16[256,512]{1,0:T(8,128)(2,1)} %constant.51.clone.refs_5_) | copy-start | bytes 786436
  6.8 34.8 %copy-start.3 = (bf16[256,512]{1,0:T(8,128)(2,1)S(1)}, bf16[256,512]{1,0:T(8,128)(2,1)}, u32[]{:S(2)}) copy-start(bf16[256,512]{1,0:T(8,128)(2,1)} %constant.50.clone.refs_4_) | copy-start | bytes 786436
  7.3 34.3 %copy-start = (bf16[512,512]{1,0:T(8,128)(2,1)S(1)}, bf16[512,512]{1,0:T(8,128)(2,1)}, u32[]{:S(2)}) copy-start(bf16[512,512]{1,0:T(8,128)(2,1)} %constant.53.clone.refs_7_) | copy-start | bytes 1572868
  7.3 34.3 %copy-start.1 = (bf16[512,512]{1,0:T(8,128)(2,1)S(1)}, bf16[512,512]{1,0:T(8,128)(2,1)}, u32[]{:S(2)}) copy-start(bf16[512,512]{1,0:T(8,128)(2,1)} %constant.52.clone.refs_6_) | copy-start | bytes 1572868

commit v12 on v9

--- a/solution.py
+++ b/solution.py
@@ -57,19 +57,19 @@
     return lax.dot_general(a, b, (dims, ((), ())), preferred_element_type=jnp.float32)
 
 
-def from_right(block, table_high, table_low):
+def from_right(block, table_high, table_low, stacked=False):
     dims = ((1,), (0,))
     count = block.shape[0]
-    if count <= TILE:
+    if stacked or count <= TILE:
         high = block.astype(jnp.bfloat16).astype(jnp.float32)
         both = jnp.concatenate([high, block - high], axis=0).astype(jnp.bfloat16)
-        main, rest = product(both, table_high, dims), product(both, table_low, dims)
+        main, rest = product(both, table_high, dims), product(both[: max(count, 2 * TILE)], table_low, dims)
         return main[:count] + main[count:] + rest[:count]
     high, low = pieces(block)
     return product(high, table_high, dims) + product(low, table_high, dims) + product(high, table_low, dims)
 
 
-def transform(block, tables):
+def transform(block, tables, stacked=False):
     quarter_high, quarter_low, half_high, half_low = tables
     half = half_high.shape[0]
     quarter = half // 2
@@ -77,9 +77,9 @@
     even, odd = left + right, left - right
     left, right = even[:, :quarter], even[:, quarter:]
     return jnp.concatenate([
-        from_right(left + right, quarter_high[:, :quarter], quarter_low[:, :quarter]),
-        from_right(left - right, quarter_high[:, quarter:], quarter_low[:, quarter:]),
-        from_right(odd, half_high, half_low),
+        from_right(left + right, quarter_high[:, :quarter], quarter_low[:, :quarter], stacked),
+        from_right(left - right, quarter_high[:, quarter:], quarter_low[:, quarter:], stacked),
+        from_right(odd, half_high, half_low, stacked),
     ], axis=1)
 
 
@@ -256,7 +256,7 @@
     keep = jnp.where(step_ref[0] == steps - 1, 0.0, 1.0)
     first = restore(y_ref[...].T, tables) - keep * x_ref[...]
     first_ref[...] = first
-    out_ref[...] = transform(excess_ref[...] * first, tables).T
+    out_ref[...] = transform(excess_ref[...] * first, tables, True).T
 
 
 def finish_kernel(y_ref, first_ref, *refs):

time: 123 us -> 123 us (level)
  no operation moved by 1% of the time
where the time goes in v12:
time: 123 us
  blocking collectives  111 us (90%)
  Pallas kernels  8.51 us (7%)
  starting transfers between devices  2.2 us (2%)
    all_to_all x4, blocking collectives, exchange(): lax.all_to_all(block.reshape(devices, comps, rows), GROUP, split_axis=0,...  111 us
    pallas_call x1, Pallas kernels, local(): call(functools.partial(load_kernel, steps, SHIFT), [plane, strip, turned,...  2.7 us
  transfers between devices with their start and end apart: 1, of which 1 were waited for; matrix products, arithmetic and copies ran while one was open for 0% of the time, Pallas kernels for 2%

profile of v12, /device:TPU:1, one launch (start us, length us, event | category | flops | bytes accessed | tf_op | source)
XLA Modules:
  0.0 123.1 jit_solution(7212807798735599542)
XLA Ops:
  0.0 0.9 shard_map.119
  0.9 2.2 %collective-permute-start = (f32[8,1024]{1,0:T(8,128)S(1)}, f32[8,1024]{1,0:T(8,128)S(1)}, u32[]{:S(2)}, u32[]{:S(2)}) collective-permute-start(f32[8,1024]{1,0:T(8,128)S(1)} %shard_map.119), channel_id=1, source_target_pairs={{0,1},{1,2},{2,3},{3,4},{4,5},{5,6},{6,7},{7,0},{8,9},{9,10},{10,1... | collective-permute-start | bytes 98312 | tf_op jit(solution)/shard_map/ppermute | solution.py:311
  3.1 2.7 %shard_map.118 = (f32[128,1024]{1,0:T(8,128)S(1)}, f32[8,1024]{1,0:T(8,128)S(1)}, f32[1024,128]{1,0:T(8,128)S(1)}, f32[128,1024]{1,0:T(8,128)S(1)}, f32[8,1024]{...) custom-call(s32[1]{0:T(128)} %bitcast.step_ref, ...), custom_call_target="tpu_custom_call" | custom-call | flops 301989888 | bytes 4194304 | tf_op jit(solution)/shard_map/pallas_call | solution.py:312
  5.9 1.0 collective-permute-done.edge_ref
  6.8 0.0 copy-start.2
  6.8 0.0 copy-start.3
  6.8 0.4 shard_map.120
  7.3 0.0 copy-start
  7.3 0.0 copy-start.1
  7.3 34.3 %all_to_all.20 = f32[256,4,128]{2,1,0:T(4,128)S(1)} all-to-all(f32[256,4,128]{2,1,0:T(4,128)S(1)} %bitcast.15), channel_id=1, replica_groups=mesh['xh'=2,'z'=8,'c'=2,'xl'=2,'y'=4] {'xl','y','z','c','xh'}, dimensions={0} | all-to-all | bytes 1048576 | tf_op jit(solution)/shard_map/all_to_all | solution.py:296
  41.6 0.0 copy-done.2
  41.6 0.0 copy-done.3
  41.6 0.0 copy-done
  41.6 0.0 copy-done.1
  41.6 1.0 shard_map.121
  42.6 25.7 %all_to_all.21 = f32[256,4,128]{2,1,0:T(4,128)S(1)} all-to-all(f32[256,4,128]{2,1,0:T(4,128)S(1)} %bitcast.17), channel_id=1, replica_groups=mesh['xh'=2,'z'=8,'c'=2,'xl'=2,'y'=4] {'xl','y','z','c','xh'}, dimensions={0} | all-to-all | bytes 1048576 | tf_op jit(solution)/shard_map/all_to_all | solution.py:296
  68.3 1.2 shard_map.122
  69.4 25.7 %all_to_all.22 = f32[256,4,128]{2,1,0:T(4,128)S(1)} all-to-all(f32[256,4,128]{2,1,0:T(4,128)S(1)} %bitcast.20), channel_id=1, replica_groups=mesh['xh'=2,'z'=8,'c'=2,'xl'=2,'y'=4] {'xl','y','z','c','xh'}, dimensions={0} | all-to-all | bytes 1048576 | tf_op jit(solution)/shard_map/all_to_all | solution.py:296
  95.1 0.9 shard_map.123
  96.1 25.7 %all_to_all.23 = f32[256,4,128]{2,1,0:T(4,128)S(1)} all-to-all(f32[256,4,128]{2,1,0:T(4,128)S(1)} %bitcast.19), channel_id=1, replica_groups=mesh['xh'=2,'z'=8,'c'=2,'xl'=2,'y'=4] {'xl','y','z','c','xh'}, dimensions={0} | all-to-all | bytes 1048576 | tf_op jit(solution)/shard_map/all_to_all | solution.py:296
  121.8 1.4 %shard_map.124 = f32[128,1024]{1,0:T(8,128)} custom-call(f32[1024,128]{1,0:T(8,128)S(1)} %bitcast.14, f32[128,1024]{1,0:T(8,128)S(1)} %get-tuple-element.26.first_ref, bf16[256,512]{1,0:T(8,128)(2,1)S(1)} %get-tuple-element.19.refs_0_.refs_4_, bf16[256,512]{1,0:T(8,128)(2,1)S(1)} %get-tuple-element.20.refs_1_.refs_5_, ...), custom_call_target="tpu_custom_call" | custom-call | flops 301989888 | bytes 4194304 | tf_op jit(solution)/shard_map/pallas_call | solution.py:335
Async XLA Ops:
  0.9 5.9 %collective-permute-start = (f32[8,1024]{1,0:T(8,128)S(1)}, f32[8,1024]{1,0:T(8,128)S(1)}, u32[]{:S(2)}, u32[]{:S(2)}) collective-permute-start(f32[8,1024]{1,0:T(8,128)S(1)} %shard_map.119), channel_id=1, source_target_pairs={{0,1},{1,2},{2,3},{3,4},{4,5},{5,6},{6,7},{7,0},{8,9},{9,10},{10,1... | collective-permute-start | bytes 98312 | tf_op jit(solution)/shard_map/ppermute | solution.py:311
  6.8 34.8 %copy-start.2 = (bf16[256,512]{1,0:T(8,128)(2,1)S(1)}, bf16[256,512]{1,0:T(8,128)(2,1)}, u32[]{:S(2)}) copy-start(bf16[256,512]{1,0:T(8,128)(2,1)} %constant.51.clone.refs_5_) | copy-start | bytes 786436
  6.8 34.8 %copy-start.3 = (bf16[256,512]{1,0:T(8,128)(2,1)S(1)}, bf16[256,512]{1,0:T(8,128)(2,1)}, u32[]{:S(2)}) copy-start(bf16[256,512]{1,0:T(8,128)(2,1)} %constant.50.clone.refs_4_) | copy-start | bytes 786436
  7.3 34.3 %copy-start = (bf16[512,512]{1,0:T(8,128)(2,1)S(1)}, bf16[512,512]{1,0:T(8,128)(2,1)}, u32[]{:S(2)}) copy-start(bf16[512,512]{1,0:T(8,128)(2,1)} %constant.53.clone.refs_7_) | copy-start | bytes 1572868
  7.3 34.3 %copy-start.1 = (bf16[512,512]{1,0:T(8,128)(2,1)S(1)}, bf16[512,512]{1,0:T(8,128)(2,1)}, u32[]{:S(2)}) copy-start(bf16[512,512]{1,0:T(8,128)(2,1)} %constant.52.clone.refs_6_) | copy-start | bytes 1572868
